TPU v7x, 32 devices: a whole 2x2x4 slice. The times are simulated.
32 devices in a mesh: leaf: 8 (over z, x), rhs: 4 (over y, core).
Axes of the slice: x: 2, y: 2, z: 4, core: 2. Of those that a mesh axis runs over, the one named last changes fastest.
Arguments:
- fields: bfloat16 [16384, 1024], P('leaf', 'rhs'), may hold values from -6 to 6
- owner: int32 [16384, 1], P('leaf'), may hold values from 0 to 7; in each aligned block of 2048 rows (0 to 2047, 2048 to 4095, ...) at most 512 rows name the same one
- source_basis: bfloat16 [16384, 256], P('leaf'), may hold values from -0.125 to 0.125
- field_basis: bfloat16 [16384, 256], P('leaf'), may hold values from -0.375 to 0.375
- transfer: bfloat16 [8, 3, 256, 512], P('leaf', None, 'rhs'), may hold values from -0.25 to 0.25
- near_blocks: bfloat16 [64, 7, 256, 256], P('leaf'), may hold values from -0.25 to 0.25
- near_index: int32 [64, 7], P('leaf'), may hold values from 0 to 7
- near_count: int32 [64], P('leaf'), may hold values from 1 to 7
Outputs:
- scattered: bfloat16 [16384, 1024], P('leaf', 'rhs')
Inputs may be any that keep to these rules, and one draw needn't show every extreme that they name: In the rows of one group of 2048 rows at most 512 name one owner; in some group one owner is named by exactly 512. `near_index`: Row-block numbers counted within the same group of 8 row blocks.
All inputs are finite; a program needn't handle non-finite values.
Results may differ from a plain program's by a relative error of at most 0.006.
Values may be sent and summed in bfloat16 or wider, within the bound.
No kernel may reach another device: no remote copies, remote signals or barrier semaphores. Data moves between devices by JAX's collectives and lax.ppermute only.
A program may use at most 128 MiB of HBM per device.

v0:
```python
import jax
import jax.numpy as jnp
from jax import lax
from jax.sharding import PartitionSpec as P


def swapped(value, axis, stride):
    return lax.ppermute(value, axis, [(i, i ^ 1 << stride) for i in range(lax.axis_size(axis))])


def slot_numbers(owners_of, n_leaf, capacity):
    onehot = (owners_of[:, None] == jnp.arange(n_leaf, dtype=jnp.int32)[None, :]).astype(jnp.int32)
    before = jnp.cumsum(onehot, axis=0) - onehot
    rank_in = jnp.sum(before * onehot, axis=1)
    return owners_of * capacity + rank_in


def on_device(
    fields, owner, source_basis, field_basis, transfer, near_blocks, near_index, near_count
):
    n_leaf = lax.axis_size("leaf")
    row_count, col_count = fields.shape
    basis_width = source_basis.shape[1]
    capacity = 2 * row_count // n_leaf
    slot_index = slot_numbers(owner[:, 0], n_leaf, capacity)
    block_rows = near_blocks.shape[2]
    block_count, near_slots = near_index.shape
    chosen = fields.reshape(block_count, block_rows, col_count)[near_index]
    keep_mask = jnp.arange(near_slots, dtype=jnp.int32)[None, :] < near_count[:, None]
    chosen = jnp.where(keep_mask[:, :, None, None], chosen, jnp.zeros((), jnp.bfloat16))
    near_term = jnp.einsum(
        "gjab,gjbn->gan", near_blocks, chosen, preferred_element_type=jnp.float32
    ).reshape(row_count, col_count)
    x_slots = jnp.zeros((n_leaf * capacity, col_count), jnp.bfloat16).at[slot_index].set(fields)
    v_slots = (
        jnp.zeros((n_leaf * capacity, basis_width), jnp.bfloat16).at[slot_index].set(source_basis)
    )
    u_slots = (
        jnp.zeros((n_leaf * capacity, basis_width), jnp.bfloat16).at[slot_index].set(field_basis)
    )
    x_three = x_slots.reshape(n_leaf, capacity, col_count)
    v_three = v_slots.reshape(n_leaf, capacity, basis_width)
    coefficients = lax.psum_scatter(
        jnp.einsum("bck,bcn->bkn", v_three, x_three, preferred_element_type=jnp.float32),
        "leaf",
        scatter_dimension=0,
        tiled=True,
    )[0].astype(jnp.bfloat16)
    for level_num in range(transfer.shape[1]):
        partner = swapped(coefficients, "leaf", level_num)
        stacked = jnp.concatenate([coefficients, partner], axis=0)

        def apply_rows(shard_piece, offset, stacked=stacked):
            return jnp.dot(shard_piece, stacked, preferred_element_type=jnp.float32)

        coefficients = apply_rows(
            lax.all_gather(transfer[0, level_num], "rhs", axis=0, tiled=True), jnp.int32(0)
        ).astype(jnp.bfloat16)
    u_three = u_slots.reshape(n_leaf, capacity, basis_width)
    far_slots = (
        jnp.einsum(
            "bck,bkn->bcn",
            u_three,
            lax.all_gather(coefficients[None], "leaf", axis=0, tiled=True),
            preferred_element_type=jnp.float32,
        )
        .astype(jnp.bfloat16)
        .reshape(n_leaf * capacity, col_count)
    )
    far_term = far_slots[slot_index]
    return (far_term.astype(jnp.float32) + near_term).astype(jnp.bfloat16)


def solution(mesh):
    in_specs = (
        P("leaf", "rhs"),
        P("leaf", None),
        P("leaf", None),
        P("leaf", None),
        P("leaf", None, "rhs", None),
        P("leaf", None, None, None),
        P("leaf", None),
        P("leaf"),
    )
    out_specs = P("leaf", "rhs")
    return jax.shard_map(
        on_device, mesh=mesh, in_specs=in_specs, out_specs=out_specs, check_vma=False
    )
```

profile of v0, /device:TPU:0, one launch (start us, length us, event | category | flops | bytes accessed | tf_op | source)
XLA Modules:
  0.0 193.1 jit_solution(11566974402506715368)
XLA Ops:
  6.5 0.7 fusion.29
  7.2 2.3 %reduce-window.6 = s32[8,16,128]{2,1,0:T(8,128)S(1)} reduce-window(s32[8,16,128]{2,1,0:T(8,128)S(1)} %fusion.29, s32[]{:T(128)} %constant.7.clone.1), window={size=1x1x128 pad=0_0x0_0x127_0}, to_apply=%region_0.0 | reduce-window | flops 2080768 | bytes 131076 | tf_op jit(solution)/shard_map/reduce-window
  9.5 0.3 slice_reduce_fusion
  9.8 0.2 reduce-window.9
  10.0 0.1 add_bitcast_fusion
  10.1 0.7 fusion.28
  10.8 0.7 compare_select_fusion
  11.5 10.4 %scatter_custom_fusion.2 = bf16[4096,256]{1,0:T(8,128)(2,1)S(1)} fusion(s32[2048]{0:T(1024)S(1)} %bitcast.74, bf16[2048,256]{1,0:T(8,128)(2,1)} %param.8, bf16[]{:T(256)} %constant.5.clone.1), kind=kCustom, calls=%fused_computation.18 | custom fusion | bytes 2097664 | tf_op jit(solution)/shard_map/scatter | solution.py:34
  21.9 11.2 %scatter_custom_fusion.1 = bf16[4096,256]{1,0:T(8,128)(2,1)} fusion(s32[2048]{0:T(1024)S(1)} %bitcast.75, bf16[2048,256]{1,0:T(8,128)(2,1)} %param.10, bf16[]{:T(256)} %constant.5.clone.1), kind=kCustom, calls=%fused_computation.20 | custom fusion | bytes 2097664 | tf_op jit(solution)/shard_map/scatter | solution.py:36
  33.1 3.7 %fusion.35 = f32[8,256,256]{2,1,0:T(8,128)} fusion(bf16[8,512,256]{2,1,0:T(8,128)(2,1)} %bitcast.67, bf16[8,512,256]{2,1,0:T(8,128)(2,1)S(1)} %bitcast.66), kind=kOutput, calls=%fused_computation.56 | convolution fusion | flops 536870912 | bytes 6291456 | tf_op jit(solution)/shard_map/bck,bcn->bkn/dot_general | solution.py:44
  36.9 70.9 %reduce-scatter.2.cloned.1.call-done = f32[1,256,256]{2,1,0:T(8,128)} async-done(((f32[8,256,256]{2,1,0:T(8,128)}), f32[1,256,256]{2,1,0:T(8,128)}) %reduce-scatter.2.cloned.1.call-update) | async-done | bytes 262160 | tf_op jit(solution)/shard_map/reduce_scatter | solution.py:43
  107.9 1.0 convert_bitcast_fusion
  108.8 0.8 collective-permute-start
  109.6 5.8 %all-gather = bf16[1,1,256,512]{3,2,1,0:T(8,128)(2,1)S(1)} all-gather(bf16[1,1,64,512]{3,2,1,0:T(8,128)(2,1)S(1)} %get-tuple-element.6), channel_id=2, replica_groups=mesh['leaf'=8,'rhs'=4] {'rhs'}, dimensions={2}, use_global_device_ids=true | all-gather | bytes 327680 | tf_op jit(solution)/shard_map/all_gather | solution.py:57
  115.4 0.2 fusion.6
  115.6 1.7 collective-permute-start.1
  117.4 5.8 %all-gather.1 = bf16[1,1,256,512]{3,2,1,0:T(8,128)(2,1)S(1)} all-gather(bf16[1,1,64,512]{3,2,1,0:T(8,128)(2,1)S(1)} %get-tuple-element.7), channel_id=3, replica_groups=mesh['leaf'=8,'rhs'=4] {'rhs'}, dimensions={2}, use_global_device_ids=true | all-gather | bytes 327680 | tf_op jit(solution)/shard_map/all_gather | solution.py:57
  123.2 0.2 fusion.7
  123.4 0.8 collective-permute-start.2
  124.2 0.1 iota_compare_fusion.2
  124.3 0.1 reshape.74
  124.4 5.8 %all-gather.2 = bf16[1,1,256,512]{3,2,1,0:T(8,128)(2,1)S(1)} all-gather(bf16[1,1,64,512]{3,2,1,0:T(8,128)(2,1)S(1)} %get-tuple-element.5), channel_id=4, replica_groups=mesh['leaf'=8,'rhs'=4] {'rhs'}, dimensions={2}, use_global_device_ids=true | all-gather | bytes 327680 | tf_op jit(solution)/shard_map/all_gather | solution.py:57
  130.1 2.6 %collective-permute-done.2 = bf16[256,256]{1,0:T(8,128)(2,1)S(1)} collective-permute-done((bf16[256,256]{1,0:T(8,128)(2,1)S(1)}, bf16[256,256]{1,0:T(8,128)(2,1)S(1)}, u32[]{:S(2)}, u32[]{:S(2)}) %collective-permute-start.2) | collective-permute-done | bytes 131104 | tf_op jit(solution)/shard_map/ppermute | solution.py:8
  132.7 0.9 fusion.5
  133.7 11.3 %scatter_custom_fusion = bf16[4096,256]{1,0:T(8,128)(2,1)} fusion(s32[2048]{0:T(1024)S(1)} %bitcast.76, bf16[2048,256]{1,0:T(8,128)(2,1)} %param.11, bf16[]{:T(256)} %constant.5.clone.1), kind=kCustom, calls=%fused_computation.22 | custom fusion | bytes 2097664 | tf_op jit(solution)/shard_map/scatter | solution.py:39
  145.0 5.3 %gather_fusion.1 = bf16[56,256,256]{2,1,0:T(8,128)(2,1)} fusion(bf16[8,256,256]{2,1,0:T(8,128)(2,1)S(1)} %bitcast.65, s32[1024]{0:T(1024)S(1)} %pad_clamp_fusion), kind=kCustom, calls=%fused_computation.1 | custom fusion | bytes 14680288 | tf_op jit(solution)/shard_map/gather | solution.py:28
  150.2 8.6 %fusion = f32[8,256,256,1]{1,2,3,0:T(8,128)} fusion(bf16[8,7,256,256]{3,2,1,0:T(8,128)(2,1)} %param.13, bf16[8,7,256,256]{3,2,1,0:T(8,128)(2,1)} %bitcast.69, pred[8,7]{1,0:T(8,128)(4,1)S(1)} %iota_compare_fusion.2), kind=kOutput, calls=%fused_computation.5 | convolution fusion | flops 1882718208 | bytes 16777272 | tf_op jit(solution)/shard_map/gjab,gjbn->gan/dot_general | solution.py:31
  158.9 13.3 %all-gather.6.cloned.1.call-done = bf16[2048,256]{0,1:T(8,128)(2,1)} async-done(((bf16[256,256]{0,1:T(8,128)(2,1)}), bf16[2048,256]{0,1:T(8,128)(2,1)}) %all-gather.6.cloned.1.call-update) | async-done | bytes 1048592 | tf_op jit(solution)/shard_map/all_gather | solution.py:64
  172.2 1.5 copy.14
  173.6 2.3 %convolution_convert_fusion = bf16[8,512,256]{2,1,0:T(8,128)(2,1)S(1)} fusion(bf16[8,512,256]{2,1,0:T(8,128)(2,1)} %bitcast.68, bf16[8,256,256]{2,1,0:T(8,128)(2,1)S(1)} %bitcast.70), kind=kOutput, calls=%fused_computation.11 | convolution fusion | flops 537919488 | bytes 5242880 | tf_op jit(solution)/shard_map/bck,bkn->bcn/dot_general | solution.py:61
  175.9 7.5 %gather_fusion = bf16[2048,256]{1,0:T(8,128)(2,1)S(1)} fusion(bf16[4096,256]{1,0:T(8,128)(2,1)S(1)} %bitcast.64, s32[2048]{0:T(1024)S(1)} %broadcast_clamp_fusion), kind=kCustom, calls=%fused_computation | custom fusion | bytes 2105344 | tf_op jit(solution)/shard_map/gather | solution.py:70
  183.4 2.8 %fusion.4 = bf16[2048,256]{1,0:T(8,128)(2,1)} fusion(f32[8,256,256,1]{1,2,3,0:T(8,128)} %fusion, bf16[2048,256]{1,0:T(8,128)(2,1)S(1)} %gather_fusion), kind=kLoop, calls=%fused_computation.10 | loop fusion | flops 1572864 | bytes 4194304 | tf_op jit(solution)/shard_map/convert_element_type | solution.py:71
  (18 shorter events, 0.1 us)
Async XLA Ops:
  6.5 101.3 %reduce-scatter.2.cloned.1.call-start = ((), (), s32[]{:S(2)}) async-start(), calls=%async_computation.1 | async-start | bytes 2359296 | tf_op jit(solution)/shard_map/reduce_scatter | solution.py:43
  36.9 72.7 %copy-start.1 = (bf16[1,3,64,512]{3,2,1,0:T(8,128)(2,1)S(1)}, bf16[1,3,64,512]{3,2,1,0:T(8,128)(2,1)}, u32[]{:S(2)}) copy-start(bf16[1,3,64,512]{3,2,1,0:T(8,128)(2,1)} %param.12) | copy-start | bytes 589828
  36.9 80.5 %copy-start.2 = (s32[8,7]{1,0:T(8,128)S(1)}, s32[8,7]{1,0:T(8,128)}, u32[]{:S(2)}) copy-start(s32[8,7]{1,0:T(8,128)} %param.14) | copy-start | bytes 676
  36.9 87.4 %copy-start.3 = (s32[8]{0:T(128)S(1)}, s32[8]{0:T(128)}, u32[]{:S(2)}) copy-start(s32[8]{0:T(128)} %param.15) | copy-start | bytes 100
  36.9 135.3 %all-gather.6.cloned.1.call-start = ((), (), s32[]{:S(2)}) async-start(), calls=%async_computation.2 | async-start | bytes 1179648 | tf_op jit(solution)/shard_map/all_gather | solution.py:64
  108.8 6.6 %collective-permute-start = (bf16[256,256]{1,0:T(8,128)(2,1)S(1)}, bf16[256,256]{1,0:T(8,128)(2,1)S(1)}, u32[]{:S(2)}, u32[]{:S(2)}) collective-permute-start(bf16[256,256]{1,0:T(8,128)(2,1)S(1)} %convert_bitcast_fusion), channel_id=1, source_target_pairs={{0,4},{4,0},{8,12},{12,8},{16,20},{20,16},{24,28},{28,24},{1,5},{5... | collective-permute-start | bytes 393224 | tf_op jit(solution)/shard_map/ppermute | solution.py:8
  115.6 7.5 %collective-permute-start.1 = (bf16[256,256]{1,0:T(8,128)(2,1)S(1)}, bf16[256,256]{1,0:T(8,128)(2,1)S(1)}, u32[]{:S(2)}, u32[]{:S(2)}) collective-permute-start(bf16[256,256]{1,0:T(8,128)(2,1)S(1)} %fusion.6), channel_id=1, source_target_pairs={{0,8},{4,12},{8,0},{12,4},{16,24},{20,28},{24,16},{28,20},{1,9},{5... | collective-permute-start | bytes 393224 | tf_op jit(solution)/shard_map/ppermute | solution.py:8
  123.2 21.8 %copy-start = (bf16[2048,256]{1,0:T(8,128)(2,1)S(1)}, bf16[2048,256]{1,0:T(8,128)(2,1)}, u32[]{:S(2)}) copy-start(bf16[2048,256]{1,0:T(8,128)(2,1)} %param.8) | copy-start | bytes 3145732
  123.4 9.3 %collective-permute-start.2 = (bf16[256,256]{1,0:T(8,128)(2,1)S(1)}, bf16[256,256]{1,0:T(8,128)(2,1)S(1)}, u32[]{:S(2)}, u32[]{:S(2)}) collective-permute-start(bf16[256,256]{1,0:T(8,128)(2,1)S(1)} %fusion.7), channel_id=1, source_target_pairs={{0,16},{4,20},{8,24},{12,28},{16,0},{20,4},{24,8},{28,12},{1,17},{... | collective-permute-start | bytes 393224 | tf_op jit(solution)/shard_map/ppermute | solution.py:8
Sparse Core Ops, SparseCore 0:
  37.0 70.8 reduce-scatter.1
  133.8 38.3 all-gather.5
where the time goes:
time: 194 us; the launch traced here: 193 us
  waiting for transfers between devices  86.8 us (45%)
  local copies, waits for them, and re-layouts  47.5 us (24%)
  blocking collectives  17.3 us (9%)
  matrix products  16 us (8%)
  between operations  13.5 us (7%)
  other arithmetic  8.52 us (4%)
  starting transfers between devices  3.36 us (2%)
    reduce_scatter x1, waiting for transfers between devices, on_device(): lax.psum_scatter(jnp.einsum('bck,bcn->bkn', v_three, x_three, preferred_e...  70.9 us
    scatter x2, local copies, waits for them, and re-layouts, on_device(): jnp.zeros((n_leaf * capacity, basis_width), jnp.bfloat16).at[slot_index]  22.5 us
    all_gather x3, blocking collectives, on_device(): lax.all_gather(transfer[0, level_num], 'rhs', axis=0, tiled=True)  17.3 us
    all_gather x1, waiting for transfers between devices, on_device(): lax.all_gather(coefficients[None], 'leaf', axis=0, tiled=True)  13.3 us
    scatter x1, local copies, waits for them, and re-layouts, on_device(): jnp.zeros((n_leaf * capacity, col_count), jnp.bfloat16).at[slot_index]  10.4 us
    dot_general x1, matrix products, on_device(): jnp.einsum('gjab,gjbn->gan', near_blocks, chosen, preferred_element_type=...  8.62 us
    gather x1, local copies, waits for them, and re-layouts, on_device(): far_term = far_slots[slot_index]  7.5 us
    gather x1, local copies, waits for them, and re-layouts, on_device(): chosen = fields.reshape(block_count, block_rows, col_count)[near_index]  5.25 us
  transfers between devices with their start and end apart: 5, of which 3 were waited for; matrix products, arithmetic and copies ran while one was open for 13% of the time, Pallas kernels for 0%

commit v1 on v0

v1 whole, which is shorter than its diff:
```python
import functools

import jax
import jax.numpy as jnp
from jax import lax
from jax.experimental import pallas as pl
from jax.experimental.pallas import tpu as pltpu
from jax.sharding import PartitionSpec as P

F32 = jnp.float32
BF16 = jnp.bfloat16
CHUNKS = 2
COPIES = 4
VMEM_LIMIT = 48 * 1024 * 1024
VMEM = pl.BlockSpec(memory_space=pltpu.VMEM)
SMEM = pl.BlockSpec(memory_space=pltpu.SMEM)
ANY = pl.BlockSpec(memory_space=pl.ANY)


def cost(flops, nbytes):
    return pl.CostEstimate(flops=flops, bytes_accessed=nbytes, transcendentals=0)


def params():
    return pltpu.CompilerParams(vmem_limit_bytes=VMEM_LIMIT)


def swapped(value, axis, mask):
    return lax.ppermute(value, axis, [(i, i ^ mask) for i in range(lax.axis_size(axis))])


def compress_kernel(first, chunks, me_ref, owner_ref, basis_hbm, fields_hbm, *rest):
    outs, (basis_ref, fields_ref, sems) = rest[:chunks], rest[chunks:]
    rows = basis_ref.shape[0] // COPIES
    copies = []
    for k, (source, target) in enumerate(((basis_hbm, basis_ref), (fields_hbm, fields_ref))):
        for p in range(COPIES):
            part = pl.ds(p * rows, rows)
            copies.append(
                pltpu.make_async_copy(source.at[part], target.at[part], sems.at[k * COPIES + p])
            )
    for copy in copies:
        copy.start()
    relative = owner_ref[...] ^ me_ref[0]
    for copy in copies:
        copy.wait()
    basis_t = basis_ref[...].T
    fields = fields_ref[...]
    width = fields.shape[1] // chunks
    for i in range(outs[0].shape[0]):
        masked = jnp.where(relative == first + 2 * i, basis_t, jnp.zeros((), BF16))
        block = jnp.dot(masked, fields, preferred_element_type=F32)
        for c in range(chunks):
            outs[c][i] = block[:, c * width : (c + 1) * width].astype(outs[c].dtype)


def compress(me, owner_row, basis, fields, first, count, dtype, chunks):
    rows, cols = fields.shape
    width = basis.shape[1]
    return pl.pallas_call(
        functools.partial(compress_kernel, first, chunks),
        out_shape=[jax.ShapeDtypeStruct((count, width, cols // chunks), dtype)] * chunks,
        in_specs=[SMEM, VMEM, ANY, ANY],
        out_specs=[VMEM] * chunks,
        scratch_shapes=[
            pltpu.VMEM((rows, width), BF16),
            pltpu.VMEM((rows, cols), BF16),
            pltpu.SemaphoreType.DMA((2 * COPIES,)),
        ],
        compiler_params=params(),
        cost_estimate=cost(2 * count * rows * cols * width, 4 * rows * cols),
    )(me, owner_row, basis, fields)


def near_kernel(index_ref, count_ref, blocks_ref, fields_ref, near_ref):
    g = pl.program_id(0)
    slots, size = blocks_ref.shape[1:3]
    chosen = []
    for j in range(slots):
        start = pl.multiple_of(index_ref[g, j] * size, size)
        piece = fields_ref[pl.ds(start, size), :]
        chosen.append(jnp.where(j < count_ref[g], piece, jnp.zeros_like(piece)))
    weights = jnp.concatenate([blocks_ref[0, j] for j in range(slots)], axis=1)
    near_ref[...] = jnp.dot(
        weights, jnp.concatenate(chosen, axis=0), preferred_element_type=F32
    )


def near_field(near_index, near_count, near_blocks, fields):
    rows, cols = fields.shape
    blocks, slots, size, _ = near_blocks.shape
    return pl.pallas_call(
        near_kernel,
        out_shape=jax.ShapeDtypeStruct((rows, cols), F32),
        grid_spec=pltpu.PrefetchScalarGridSpec(
            num_scalar_prefetch=2,
            grid=(blocks,),
            in_specs=[
                pl.BlockSpec((1, slots, size, size), lambda g, *_: (g, 0, 0, 0)),
                pl.BlockSpec((rows, cols), lambda g, *_: (0, 0)),
            ],
            out_specs=pl.BlockSpec((size, cols), lambda g, *_: (g, 0)),
        ),
        compiler_params=params(),
        cost_estimate=cost(2 * blocks * slots * size * size * cols, near_blocks.size * 2),
    )(near_index, near_count, near_blocks, fields)


def first_level_kernel(me_ref, rows_ref, own_ref, other_ref, out_ref):
    n = rows_ref.shape[0]
    weights = jnp.concatenate([rows_ref[a ^ me_ref[0]] for a in range(n)], axis=0)
    stacked = jnp.concatenate([own_ref[...], other_ref[...]], axis=0)
    out_ref[...] = jnp.dot(weights, stacked, preferred_element_type=F32).astype(BF16)


def first_level(rhs_me, rows, own, other):
    return pl.pallas_call(
        first_level_kernel,
        out_shape=jax.ShapeDtypeStruct(own.shape, BF16),
        in_specs=[SMEM, VMEM, VMEM, VMEM],
        out_specs=VMEM,
        compiler_params=params(),
        cost_estimate=cost(2 * rows.size * own.shape[1], 2 * rows.size),
    )(rhs_me, rows, own, other)


def later_levels_kernel(me_ref, rows_ref, *rest):
    blocks, out_ref = [ref[...] for ref in rest[:-1]], rest[-1]
    n, count, levels = rows_ref.shape[:3]
    for level in range(levels):
        fresh = []
        for s in range(count):
            weights = jnp.concatenate([rows_ref[a ^ me_ref[0], s, level] for a in range(n)], axis=0)
            stacked = jnp.concatenate([blocks[s], blocks[s ^ (1 << level)]], axis=0)
            fresh.append(jnp.dot(weights, stacked, preferred_element_type=F32).astype(BF16))
        blocks = fresh
    for s in range(count):
        out_ref[s] = blocks[s]


def later_levels(rhs_me, rows, blocks):
    return pl.pallas_call(
        later_levels_kernel,
        out_shape=jax.ShapeDtypeStruct((len(blocks),) + blocks[0].shape, BF16),
        in_specs=[SMEM] + [VMEM] * (1 + len(blocks)),
        out_specs=VMEM,
        compiler_params=params(),
        cost_estimate=cost(2 * rows.size * blocks[0].shape[1], 2 * rows.size),
    )(rhs_me, rows, *blocks)


def far_kernel(first, last, me_ref, owner_ref, basis_ref, blocks_ref, base_ref, *rest):
    out_ref = rest[-1]
    relative = owner_ref[...] ^ me_ref[0]
    basis = basis_ref[...]
    count, width, part_cols = blocks_ref.shape
    masked = [
        jnp.where(relative == first + 2 * i, basis, jnp.zeros((), BF16)) for i in range(count)
    ]
    total = jnp.dot(
        jnp.concatenate(masked, axis=1),
        blocks_ref[...].reshape(count * width, part_cols),
        preferred_element_type=F32,
    )
    total = total.astype(BF16).astype(F32) + base_ref[...]
    if last:
        earlier = [ref[...] for ref in rest[:-1]]
        out_ref[...] = jnp.concatenate(earlier + [total.astype(out_ref.dtype)], axis=1)
    else:
        out_ref[...] = total.astype(out_ref.dtype)


def far_field(me, owner, basis, blocks, base, base_column, first, dtype, earlier=()):
    rows, width = basis.shape
    count, _, part_cols = blocks.shape
    tile = min(rows, 512)
    out_cols = part_cols * (1 + len(earlier))
    part = pl.BlockSpec((tile, part_cols), lambda r: (r, 0))
    return pl.pallas_call(
        functools.partial(far_kernel, first, bool(earlier)),
        out_shape=jax.ShapeDtypeStruct((rows, out_cols), dtype),
        grid=(rows // tile,),
        in_specs=[
            SMEM,
            pl.BlockSpec((tile, 1), lambda r: (r, 0)),
            pl.BlockSpec((tile, width), lambda r: (r, 0)),
            pl.BlockSpec((count, width, part_cols), lambda r: (0, 0, 0)),
            pl.BlockSpec((tile, part_cols), lambda r: (r, base_column)),
        ]
        + [part] * len(earlier),
        out_specs=pl.BlockSpec((tile, out_cols), lambda r: (r, 0)),
        compiler_params=params(),
        cost_estimate=cost(
            2 * count * rows * width * part_cols, rows * (width * 2 + part_cols * 6)
        ),
    )(me, owner, basis, blocks, base, *earlier)


def gathered_rows(value, axis):
    pieces = value[None]
    mask = 1
    order = [0]
    masks = []
    while mask < lax.axis_size(axis):
        masks.append(mask)
        mask *= 2
    for mask in reversed(masks):
        pieces = jnp.concatenate([pieces, swapped(pieces, axis, mask)], axis=0)
        order = order + [o ^ mask for o in order]
    return pieces, order


def in_order(pieces, order):
    return jnp.stack([pieces[order.index(o)] for o in range(len(order))])


def on_device(
    fields, owner, source_basis, field_basis, transfer, near_blocks, near_index, near_count
):
    n_leaf = lax.axis_size("leaf")
    rows, cols = fields.shape
    levels = transfer.shape[1]
    group = 2**levels
    outer = n_leaf // group
    upper = group // 2
    chunks = CHUNKS
    me = lax.axis_index("leaf").astype(jnp.int32)[None]
    rhs_me = lax.axis_index("rhs").astype(jnp.int32)[None]
    owner_row = owner.reshape(1, rows)

    send = list(compress(me, owner_row, source_basis, fields, 1, n_leaf // 2, BF16, chunks))
    got = [swapped(s, "leaf", 1) for s in send]

    transfer, send[0] = lax.optimization_barrier((transfer, send[0]))
    first, order = gathered_rows(transfer[0, 0], "rhs")
    first = in_order(first, order)
    later = transfer[:, 1:]
    spots = [0]
    mask = upper // 2
    while mask:
        later = jnp.concatenate([later, swapped(later, "leaf", 2 * mask)], axis=0)
        spots = spots + [s ^ mask for s in spots]
        mask //= 2
    later, order = gathered_rows(later, "rhs")
    later = jnp.stack(
        [jnp.stack([later[order.index(o), spots.index(s)] for s in range(upper)]) for o in range(len(order))]
    )

    keep = compress(me, owner_row, source_basis, fields, 0, n_leaf // 2, F32, chunks)
    near = near_field(near_index, near_count, near_blocks, fields)
    got[0], near = lax.optimization_barrier((got[0], near))

    bases, others = [], []
    for c in range(chunks):
        total = keep[c] + got[c].astype(F32)
        mine = total[:upper]
        for o in range(1, outer):
            part = total[o * upper : (o + 1) * upper].astype(BF16)
            mine = mine + swapped(part, "leaf", o * group).astype(F32)
        coefficients = mine[0]
        for s in range(1, upper):
            coefficients = coefficients + swapped(mine[s].astype(BF16), "leaf", 2 * s).astype(F32)
        coefficients = coefficients.astype(BF16)
        coefficients = first_level(rhs_me, first, coefficients, swapped(coefficients, "leaf", 1))
        blocks = [coefficients] + [swapped(coefficients, "leaf", 2 * s) for s in range(1, upper)]
        own = later_levels(rhs_me, later, blocks)
        if outer > 1:
            own = jnp.concatenate([own] + [swapped(own, "leaf", o * group) for o in range(1, outer)])
        others.append(swapped(own, "leaf", 1))
        bases.append(far_field(me, owner, field_basis, own, near, c, 0, F32))
    done = []
    for c in range(chunks):
        earlier = done if c == chunks - 1 else ()
        done.append(far_field(me, owner, field_basis, others[c], bases[c], 0, 1, BF16, earlier))
    return done[-1]


def solution(mesh):
    in_specs = (
        P("leaf", "rhs"),
        P("leaf", None),
        P("leaf", None),
        P("leaf", None),
        P("leaf", None, "rhs", None),
        P("leaf", None, None, None),
        P("leaf", None),
        P("leaf"),
    )
    out_specs = P("leaf", "rhs")
    return jax.shard_map(
        on_device, mesh=mesh, in_specs=in_specs, out_specs=out_specs, check_vma=False
    )
```

time: 194 us -> 88.3 us (0.46)
  waiting for transfers between devices: 86.8 us -> 16.2 us
  local copies, waits for them, and re-layouts: 47.5 us -> 5.86 us
  starting transfers between devices: 3.36 us -> 33.4 us
  Pallas kernels: 0 us -> 26.5 us
  blocking collectives: 17.3 us -> 0 us
  matrix products: 16 us -> 0 us
  between operations: 13.5 us -> 0.33 us
  other arithmetic: 8.52 us -> 5.36 us
    reduce_scatter x1 -> x0, waiting for transfers between devices: 70.9 us -> none  [on_device(): lax.psum_scatter(jnp.einsum('bck,bcn->bkn', v_three, x_three, preferred_e...]
    scatter x3 -> x0, local copies, waits for them, and re-layouts: 32.9 us -> none  [the longest x2 22.5 us: on_device(): jnp.zeros((n_leaf * capacity, basis_width), jnp.bfloat16).at[slot_index]]
    ppermute x3 -> x24, starting transfers between devices: 3.32 us -> 33.4 us  [swapped(): lax.ppermute(value, axis, [(i, i ^ mask) for i in range(lax.axis_size(axi...]
    pallas_call x0 -> x11, Pallas kernels: none -> 26.5 us  [the longest x4 12.6 us: far_field(): pl.pallas_call(functools.partial(far_kernel, first, bool(earlier)), out_s...]
    all_gather x3 -> x0, blocking collectives: 17.3 us -> none  [on_device(): lax.all_gather(transfer[0, level_num], 'rhs', axis=0, tiled=True)]
    dot_general x6 -> x0, matrix products: 16 us -> none  [the longest x1 8.62 us: on_device(): jnp.einsum('gjab,gjbn->gan', near_blocks, chosen, preferred_element_type=...]
    ppermute x3 -> x24, waiting for transfers between devices: 2.56 us -> 16.2 us  [swapped(): lax.ppermute(value, axis, [(i, i ^ mask) for i in range(lax.axis_size(axi...]
    all_gather x1 -> x0, waiting for transfers between devices: 13.3 us -> none  [on_device(): lax.all_gather(coefficients[None], 'leaf', axis=0, tiled=True)]
  transfers between devices with their start and end apart: 5 -> 24, of which waited for: 3 -> 6; matrix products, arithmetic and copies ran while one was open for 13% -> 8% of each run, Pallas kernels for 0% -> 23%
where the time goes in v1:
time: 88.3 us; the launch traced here: 87.7 us
  starting transfers between devices  33.4 us (38%)
  Pallas kernels  26.5 us (30%)
  waiting for transfers between devices  16.2 us (18%)
  local copies, waits for them, and re-layouts  5.86 us (7%)
  other arithmetic  5.36 us (6%)
    ppermute x24, starting transfers between devices, swapped(): lax.ppermute(value, axis, [(i, i ^ mask) for i in range(lax.axis_size(axi...  33.4 us
    ppermute x24, waiting for transfers between devices, swapped(): lax.ppermute(value, axis, [(i, i ^ mask) for i in range(lax.axis_size(axi...  16.2 us
    pallas_call x4, Pallas kernels, far_field(): pl.pallas_call(functools.partial(far_kernel, first, bool(earlier)), out_s...  12.6 us
    pallas_call x1, Pallas kernels, near_field(): pl.pallas_call(near_kernel, out_shape=jax.ShapeDtypeStruct((rows, cols),...  7.62 us
    unnamed x23, local copies, waits for them, and re-layouts  4.76 us
    pallas_call x2, Pallas kernels, compress(): pl.pallas_call(functools.partial(compress_kernel, first, chunks), out_sha...  3.71 us
    pallas_call x2, Pallas kernels, later_levels(): pl.pallas_call(later_levels_kernel, out_shape=jax.ShapeDtypeStruct((len(b...  2.19 us
  transfers between devices with their start and end apart: 24, of which 6 were waited for; matrix products, arithmetic and copies ran while one was open for 8% of the time, Pallas kernels for 23%

profile of v1, /device:TPU:0, one launch (start us, length us, event | category | flops | bytes accessed | tf_op | source)
XLA Modules:
  0.0 87.7 jit_solution(5768442403135632761)
XLA Ops:
  0.0 1.2 %copy-done.2 = bf16[2048,256]{1,0:T(8,128)(2,1)S(1)} copy-done((bf16[2048,256]{1,0:T(8,128)(2,1)S(1)}, bf16[2048,256]{1,0:T(8,128)(2,1)}, u32[]{:S(2)}) %copy-start.2) | copy-done | bytes 1048600
  1.9 1.2 %copy-done.7 = bf16[2048,256]{1,0:T(8,128)(2,1)S(1)} copy-done((bf16[2048,256]{1,0:T(8,128)(2,1)S(1)}, bf16[2048,256]{1,0:T(8,128)(2,1)}, u32[]{:S(2)}) %copy-start.7) | copy-done | bytes 1048600
  3.2 2.2 %shard_map.82 = (bf16[4,256,128]{2,1,0:T(8,128)(2,1)}, bf16[4,256,128]{2,1,0:T(8,128)(2,1)S(1)}) custom-call(s32[1]{0:T(128)} %bitcast.me_ref, s32[1,2048]{1,0:T(1,128)S(1)} %bitcast.79, bf16[2048,256]{1,0:T(8,128)(2,1)S(1)} %copy-done.7, bf16[2048,256]{1,0:T(8,128)(2,1)S(1)} %copy-done.2), custom_call_target="tpu_custom_call" | custom-call | flops 1073741824 | bytes 2097152 | tf_op jit(solution)/shard_map/pallas_call | solution.py:60
  5.4 3.0 %collective-permute-start.15 = (bf16[4,256,128]{2,1,0:T(8,128)(2,1)}, bf16[4,256,128]{2,1,0:T(8,128)(2,1)}, u32[]{:S(2)}, u32[]{:S(2)}) collective-permute-start(bf16[4,256,128]{2,1,0:T(8,128)(2,1)} %get-tuple-element.12), channel_id=1, source_target_pairs={{0,4},{4,0},{8,12},{12,8},{16,20},{20,16},{24,28},{28,24},{1,5},{5... | collective-permute-start | bytes 786440 | tf_op jit(solution)/shard_map/ppermute | solution.py:29
  8.5 2.0 %collective-permute-start.4 = (bf16[1,64,512]{2,1,0:T(8,128)(2,1)S(1)}, bf16[1,64,512]{2,1,0:T(8,128)(2,1)S(1)}, u32[]{:S(2)}, u32[]{:S(2)}) collective-permute-start(bf16[1,64,512]{2,1,0:T(8,128)(2,1)S(1)} %slice_bitcast_fusion.24), channel_id=1, source_target_pairs={{0,2},{1,3},{2,0},{3,1},{4,6},{5,7},{6,4},{7,5},{8,10},{9,11},{10,... | collective-permute-start | bytes 196616 | tf_op jit(solution)/shard_map/ppermute | solution.py:29
  10.5 2.7 %collective-permute-start = (bf16[1,2,64,512]{3,2,1,0:T(8,128)(2,1)S(1)}, bf16[1,2,64,512]{3,2,1,0:T(8,128)(2,1)}, u32[]{:S(2)}, u32[]{:S(2)}) collective-permute-start(bf16[1,2,64,512]{3,2,1,0:T(8,128)(2,1)S(1)} %slice.90), channel_id=1, source_target_pairs={{0,16},{4,20},{8,24},{12,28},{16,0},{20,4},{24,8},{28,12},{1,17},{... | collective-permute-start | bytes 393224 | tf_op jit(solution)/shard_map/ppermute | solution.py:29
  13.2 7.6 %shard_map.86.base_ref = f32[2048,256]{1,0:T(8,128)S(1)} custom-call(s32[8,7]{1,0:T(8,128)S(1)} %copy-done.5, s32[8]{0:T(128)S(1)} %copy-done.6, bf16[8,7,256,256]{3,2,1,0:T(8,128)(2,1)} %blocks_ref.1, bf16[2048,256]{1,0:T(8,128)(2,1)S(1)} %copy-done.2), custom_call_target="tpu_custom_call" | custom-call | flops 1879048192 | bytes 7340032 | tf_op jit(solution)/shard_map/pallas_call | solution.py:92
  21.5 1.5 %shard_map.83 = (f32[4,256,128]{2,1,0:T(8,128)S(1)}, f32[4,256,128]{2,1,0:T(8,128)S(1)}) custom-call(s32[1]{0:T(128)} %bitcast.me_ref, s32[1,2048]{1,0:T(1,128)S(1)} %bitcast.80, bf16[2048,256]{1,0:T(8,128)(2,1)S(1)} %copy-done.7, bf16[2048,256]{1,0:T(8,128)(2,1)S(1)} %copy-done.2), custom_call_target="tpu_custom_call" | custom-call | flops 1073741824 | bytes 2097152 | tf_op jit(solution)/shard_map/pallas_call | solution.py:60
  23.1 0.9 %pad_maximum_fusion.2 = bf16[2,2,64,512]{3,2,1,0:T(8,128)(2,1)S(1)} fusion(bf16[1,2,64,512]{3,2,1,0:T(8,128)(2,1)} %collective-permute-done, bf16[1,2,64,512]{3,2,1,0:T(8,128)(2,1)S(1)} %slice.90), kind=kLoop, calls=%fused_computation.9 | loop fusion | flops 131072 | bytes 524288 | tf_op jit(solution)/shard_map/concatenate | solution.py:241
  24.0 1.6 %collective-permute-start.1 = (bf16[2,2,64,512]{3,2,1,0:T(8,128)(2,1)S(1)}, bf16[2,2,64,512]{3,2,1,0:T(8,128)(2,1)S(1)}, u32[]{:S(2)}, u32[]{:S(2)}) collective-permute-start(bf16[2,2,64,512]{3,2,1,0:T(8,128)(2,1)S(1)} %pad_maximum_fusion.2), channel_id=1, source_target_pairs={{0,8},{4,12},{8,0},{12,4},{16,24},{20,28},{24,16},{28,20},{1,9},{5... | collective-permute-start | bytes 786440 | tf_op jit(solution)/shard_map/ppermute | solution.py:29
  27.4 5.3 %collective-permute-done.1 = bf16[2,2,64,512]{3,2,1,0:T(8,128)(2,1)S(1)} collective-permute-done((bf16[2,2,64,512]{3,2,1,0:T(8,128)(2,1)S(1)}, bf16[2,2,64,512]{3,2,1,0:T(8,128)(2,1)S(1)}, u32[]{:S(2)}, u32[]{:S(2)}) %collective-permute-start.1) | collective-permute-done | bytes 262176 | tf_op jit(solution)/shard_map/ppermute | solution.py:29
  32.8 1.0 %maximum_bitcast_fusion = bf16[1,4,2,64,512]{4,3,2,1,0:T(8,128)(2,1)S(1)} fusion(bf16[2,2,64,512]{3,2,1,0:T(8,128)(2,1)S(1)} %collective-permute-done.1, bf16[1,2,64,512]{3,2,1,0:T(8,128)(2,1)} %collective-permute-done, bf16[1,2,64,512]{3,2,1,0:T(8,128)(2,1)S(1)} %slice.90), kind=kLoop, calls=%fused_computation.2 | loop fusion | flops 524288 | bytes 1048576 | tf_op jit(solution)/shard_map/broadcast_in_dim | solution.py:200
  34.3 1.2 %fusion.8 = (bf16[4,256,128]{2,1,0:T(8,128)(2,1)S(1)}, f32[4,256,128]{2,1,0:T(8,128)S(1)}, bf16[4,256,128]{2,1,0:T(8,128)(2,1)S(1)}, f32[4,256,128]{2,1,0:T(8,128)S(1)}) fusion(f32[4,256,128]{2,1,0:T(8,128)S(1)} %get-tuple-element.17, bf16[4,256,128]{2,1,0:T(8,128)(2,1)} %collective-permute-done.15, f32[4,256,128]{2,1,0:T(8,128)S(1)} %get-tuple-element.14, ...), kind=kLoop, calls=%fused_computation.45 | loop fusion | flops 786432 | bytes 3145728 | tf_op jit(solution)/shard_map/convert.2
  35.5 1.7 %collective-permute-start.16 = (bf16[256,128]{1,0:T(8,128)(2,1)S(1)}, bf16[256,128]{1,0:T(8,128)(2,1)S(1)}, u32[]{:S(2)}, u32[]{:S(2)}) collective-permute-start(bf16[256,128]{1,0:T(8,128)(2,1)S(1)} %get-tuple-element.39), channel_id=1, source_target_pairs={{0,8},{4,12},{8,0},{12,4},{16,24},{20,28},{24,16},{28,20},{1,9},{5... | collective-permute-start | bytes 196616 | tf_op jit(solution)/shard_map/ppermute | solution.py:29
  37.5 2.5 %collective-permute-start.18 = (bf16[256,128]{1,0:T(8,128)(2,1)S(1)}, bf16[256,128]{1,0:T(8,128)(2,1)S(1)}, u32[]{:S(2)}, u32[]{:S(2)}) collective-permute-start(bf16[256,128]{1,0:T(8,128)(2,1)S(1)} %get-tuple-element.40), channel_id=1, source_target_pairs={{0,24},{4,28},{8,16},{12,20},{16,8},{20,12},{24,0},{28,4},{1,25},{... | collective-permute-start | bytes 196616 | tf_op jit(solution)/shard_map/ppermute | solution.py:29
  40.8 6.6 %collective-permute-done.2 = bf16[1,4,2,64,512]{4,3,2,1,0:T(8,128)(2,1)S(1)} collective-permute-done((bf16[1,4,2,64,512]{4,3,2,1,0:T(8,128)(2,1)S(1)}, bf16[1,4,2,64,512]{4,3,2,1,0:T(8,128)(2,1)S(1)}, u32[]{:S(2)}, u32[]{:S(2)}) %collective-permute-start.2) | collective-permute-done | bytes 524320 | tf_op jit(solution)/shard_map/ppermute | solution.py:29
  47.8 3.7 %collective-permute-start.9 = (bf16[256,128]{1,0:T(8,128)(2,1)S(1)}, bf16[256,128]{1,0:T(8,128)(2,1)S(1)}, u32[]{:S(2)}, u32[]{:S(2)}) collective-permute-start(bf16[256,128]{1,0:T(8,128)(2,1)S(1)} %get-tuple-element.43), channel_id=1, source_target_pairs={{0,24},{4,28},{8,16},{12,20},{16,8},{20,12},{24,0},{28,4},{1,25},{... | collective-permute-start | bytes 196616 | tf_op jit(solution)/shard_map/ppermute | solution.py:29
  51.5 1.6 %collective-permute-start.19 = (bf16[256,128]{1,0:T(8,128)(2,1)S(1)}, bf16[256,128]{1,0:T(8,128)(2,1)S(1)}, u32[]{:S(2)}, u32[]{:S(2)}) collective-permute-start(bf16[256,128]{1,0:T(8,128)(2,1)S(1)} %fusion.3.own_ref), channel_id=1, source_target_pairs={{0,4},{4,0},{8,12},{12,8},{16,20},{20,16},{24,28},{28,24},{1,5},{5... | collective-permute-start | bytes 196616 | tf_op jit(solution)/shard_map/ppermute | solution.py:29
  53.1 1.5 %collective-permute-done.8 = bf16[256,128]{1,0:T(8,128)(2,1)S(1)} collective-permute-done((bf16[256,128]{1,0:T(8,128)(2,1)S(1)}, bf16[256,128]{1,0:T(8,128)(2,1)S(1)}, u32[]{:S(2)}, u32[]{:S(2)}) %collective-permute-start.8) | collective-permute-done | bytes 65568 | tf_op jit(solution)/shard_map/ppermute | solution.py:29
  54.7 1.5 %collective-permute-start.10 = (bf16[256,128]{1,0:T(8,128)(2,1)S(1)}, bf16[256,128]{1,0:T(8,128)(2,1)S(1)}, u32[]{:S(2)}, u32[]{:S(2)}) collective-permute-start(bf16[256,128]{1,0:T(8,128)(2,1)S(1)} %fusion.7.own_ref), channel_id=1, source_target_pairs={{0,4},{4,0},{8,12},{12,8},{16,20},{20,16},{24,28},{28,24},{1,5},{5... | collective-permute-start | bytes 196616 | tf_op jit(solution)/shard_map/ppermute | solution.py:29
  56.5 1.3 %collective-permute-start.20 = (bf16[256,128]{1,0:T(8,128)(2,1)S(1)}, bf16[256,128]{1,0:T(8,128)(2,1)S(1)}, u32[]{:S(2)}, u32[]{:S(2)}) collective-permute-start(bf16[256,128]{1,0:T(8,128)(2,1)S(1)} %shard_map.88.rest_0_), channel_id=1, source_target_pairs={{0,8},{4,12},{8,0},{12,4},{16,24},{20,28},{24,16},{28,20},{1,9},{5... | collective-permute-start | bytes 196616 | tf_op jit(solution)/shard_map/ppermute | solution.py:29
  57.8 2.2 %collective-permute-start.21 = (bf16[256,128]{1,0:T(8,128)(2,1)S(1)}, bf16[256,128]{1,0:T(8,128)(2,1)S(1)}, u32[]{:S(2)}, u32[]{:S(2)}) collective-permute-start(bf16[256,128]{1,0:T(8,128)(2,1)S(1)} %shard_map.88.rest_0_), channel_id=1, source_target_pairs={{0,16},{4,20},{8,24},{12,28},{16,0},{20,4},{24,8},{28,12},{1,17},{... | collective-permute-start | bytes 196616 | tf_op jit(solution)/shard_map/ppermute | solution.py:29
  61.8 3.2 %collective-permute-start.12 = (bf16[256,128]{1,0:T(8,128)(2,1)S(1)}, bf16[256,128]{1,0:T(8,128)(2,1)S(1)}, u32[]{:S(2)}, u32[]{:S(2)}) collective-permute-start(bf16[256,128]{1,0:T(8,128)(2,1)S(1)} %shard_map.84.rest_0_), channel_id=1, source_target_pairs={{0,16},{4,20},{8,24},{12,28},{16,0},{20,4},{24,8},{28,12},{1,17},{... | collective-permute-start | bytes 196616 | tf_op jit(solution)/shard_map/ppermute | solution.py:29
  65.2 1.0 %collective-permute-start.13 = (bf16[256,128]{1,0:T(8,128)(2,1)S(1)}, bf16[256,128]{1,0:T(8,128)(2,1)S(1)}, u32[]{:S(2)}, u32[]{:S(2)}) collective-permute-start(bf16[256,128]{1,0:T(8,128)(2,1)S(1)} %shard_map.84.rest_0_), channel_id=1, source_target_pairs={{0,24},{4,28},{8,16},{12,20},{16,8},{20,12},{24,0},{28,4},{1,25},{... | collective-permute-start | bytes 196616 | tf_op jit(solution)/shard_map/ppermute | solution.py:29
  67.6 1.4 %collective-permute-start.23 = (bf16[4,256,128]{2,1,0:T(8,128)(2,1)S(1)}, bf16[4,256,128]{2,1,0:T(8,128)(2,1)}, u32[]{:S(2)}, u32[]{:S(2)}) collective-permute-start(bf16[4,256,128]{2,1,0:T(8,128)(2,1)S(1)} %shard_map.89.blocks_ref), channel_id=1, source_target_pairs={{0,4},{4,0},{8,12},{12,8},{16,20},{20,16},{24,28},{28,24},{1,5},{5... | collective-permute-start | bytes 786440 | tf_op jit(solution)/shard_map/ppermute | solution.py:29
  69.8 1.5 %collective-permute-done.13.rest_3_ = bf16[256,128]{1,0:T(8,128)(2,1)S(1)} collective-permute-done((bf16[256,128]{1,0:T(8,128)(2,1)S(1)}, bf16[256,128]{1,0:T(8,128)(2,1)S(1)}, u32[]{:S(2)}, u32[]{:S(2)}) %collective-permute-start.13) | collective-permute-done | bytes 65568 | tf_op jit(solution)/shard_map/ppermute | solution.py:29
  71.4 1.4 %shard_map.85.blocks_ref = bf16[4,256,128]{2,1,0:T(8,128)(2,1)} custom-call(s32[1]{0:T(128)} %bitcast.1.me_ref, bf16[4,4,2,64,512]{4,3,2,1,0:T(8,128)(2,1)S(1)} %pad_maximum_fusion.rows_ref, bf16[256,128]{1,0:T(8,128)(2,1)S(1)} %shard_map.84.rest_0_, bf16[256,128]{1,0:T(8,128)(2,1)S(1)} %collective-permute-done.11.rest_1_, ...), custom_call_target="tpu_custom_call" | custom-call | flops 268435456 | bytes 2097152 | tf_op jit(solution)/shard_map/pallas_call | solution.py:142
  73.8 1.2 %copy-done = bf16[2048,256]{1,0:T(8,128)(2,1)S(1)} copy-done((bf16[2048,256]{1,0:T(8,128)(2,1)S(1)}, bf16[2048,256]{1,0:T(8,128)(2,1)}, u32[]{:S(2)}) %copy-start) | copy-done | bytes 1048600
  75.1 2.2 %shard_map.90.base_ref = f32[2048,128]{1,0:T(8,128)S(1)} custom-call(s32[1]{0:T(128)} %bitcast.me_ref, s32[2048,1]{1,0:T(8,128)S(1)} %copy.12.owner_ref, bf16[2048,256]{1,0:T(8,128)(2,1)S(1)} %copy-done, bf16[4,256,128]{2,1,0:T(8,128)(2,1)S(1)} %shard_map.89.blocks_ref, f32[2048,256]{1,0:T(8,128)S(1)} %shard_map.86.base_ref), custom_call_target="tpu_custom_call" | custom-call | flops 536870912 | bytes 2621440 | tf_op jit(solution)/shard_map/pallas_call | solution.py:179
  77.3 3.2 %shard_map.87.base_ref = f32[2048,128]{1,0:T(8,128)S(1)} custom-call(s32[1]{0:T(128)} %bitcast.me_ref, s32[2048,1]{1,0:T(8,128)S(1)} %copy.12.owner_ref, bf16[2048,256]{1,0:T(8,128)(2,1)S(1)} %copy-done.1, bf16[4,256,128]{2,1,0:T(8,128)(2,1)} %shard_map.85.blocks_ref, f32[2048,256]{1,0:T(8,128)S(1)} %shard_map.86.base_ref), custom_call_target="tpu_custom_call" | custom-call | flops 536870912 | bytes 2621440 | tf_op jit(solution)/shard_map/pallas_call | solution.py:179
  80.5 3.1 %shard_map.91.rest_0_ = bf16[2048,128]{1,0:T(8,128)(2,1)S(1)} custom-call(s32[1]{0:T(128)} %bitcast.me_ref, s32[2048,1]{1,0:T(8,128)S(1)} %copy.12.owner_ref, bf16[2048,256]{1,0:T(8,128)(2,1)S(1)} %copy-done.1, bf16[4,256,128]{2,1,0:T(8,128)(2,1)} %collective-permute-done.23.blocks_ref, f32[2048,128]{1,0:T(8,128)S(1)} %shard_map.90.base_ref), custom_call_target="tpu_custom_call" | custom-call | flops 536870912 | bytes 2621440 | tf_op jit(solution)/shard_map/pallas_call | solution.py:179
  83.7 4.0 %shard_map.92 = bf16[2048,256]{1,0:T(8,128)(2,1)} custom-call(s32[1]{0:T(128)} %bitcast.me_ref, s32[2048,1]{1,0:T(8,128)S(1)} %copy.12.owner_ref, bf16[2048,256]{1,0:T(8,128)(2,1)S(1)} %copy-done.1, bf16[4,256,128]{2,1,0:T(8,128)(2,1)} %collective-permute-done.14.blocks_ref, f32[2048,128]{1,0:T(8,128)S(1)} %shard_map.87.base_ref, ...), custom_call_target="tpu_custom_call" | custom-call | flops 536870912 | bytes 2621440 | tf_op jit(solution)/shard_map/pallas_call | solution.py:179
  (69 shorter events, 10.9 us)
Async XLA Ops:
  0.0 1.2 %copy-start.2 = (bf16[2048,256]{1,0:T(8,128)(2,1)S(1)}, bf16[2048,256]{1,0:T(8,128)(2,1)}, u32[]{:S(2)}) copy-start(bf16[2048,256]{1,0:T(8,128)(2,1)} %fields_ref.1) | copy-start | bytes 3145732
  3.1 5.3 %copy-start.10 = (bf16[1,3,64,512]{3,2,1,0:T(8,128)(2,1)S(1)}, bf16[1,3,64,512]{3,2,1,0:T(8,128)(2,1)}, u32[]{:S(2)}) copy-start(bf16[1,3,64,512]{3,2,1,0:T(8,128)(2,1)} %param.12) | copy-start | bytes 589828
  3.2 10.0 %copy-start.5 = (s32[8,7]{1,0:T(8,128)S(1)}, s32[8,7]{1,0:T(8,128)}, u32[]{:S(2)}) copy-start(s32[8,7]{1,0:T(8,128)} %index_ref.1) | copy-start | bytes 676
  3.2 10.0 %copy-start.6 = (s32[8]{0:T(128)S(1)}, s32[8]{0:T(128)}, u32[]{:S(2)}) copy-start(s32[8]{0:T(128)} %count_ref.1) | copy-start | bytes 100
  5.4 22.1 %collective-permute-start.15 = (bf16[4,256,128]{2,1,0:T(8,128)(2,1)}, bf16[4,256,128]{2,1,0:T(8,128)(2,1)}, u32[]{:S(2)}, u32[]{:S(2)}) collective-permute-start(bf16[4,256,128]{2,1,0:T(8,128)(2,1)} %get-tuple-element.12), channel_id=1, source_target_pairs={{0,4},{4,0},{8,12},{12,8},{16,20},{20,16},{24,28},{28,24},{1,5},{5... | collective-permute-start | bytes 786440 | tf_op jit(solution)/shard_map/ppermute | solution.py:29
  8.4 25.9 %collective-permute-start.6 = (bf16[4,256,128]{2,1,0:T(8,128)(2,1)S(1)}, bf16[4,256,128]{2,1,0:T(8,128)(2,1)}, u32[]{:S(2)}, u32[]{:S(2)}) collective-permute-start(bf16[4,256,128]{2,1,0:T(8,128)(2,1)S(1)} %get-tuple-element.15), channel_id=1, source_target_pairs={{0,4},{4,0},{8,12},{12,8},{16,20},{20,16},{24,28},{28,24},{1,5},{5... | collective-permute-start | bytes 786440 | tf_op jit(solution)/shard_map/ppermute | solution.py:29
  8.5 12.4 %copy-start.8 = (bf16[1,64,512]{2,1,0:T(8,128)(2,1)}, bf16[1,64,512]{2,1,0:T(8,128)(2,1)S(1)}, u32[]{:S(2)}) copy-start(bf16[1,64,512]{2,1,0:T(8,128)(2,1)S(1)} %slice_bitcast_fusion.24) | copy-start | bytes 196612
  8.5 12.3 %collective-permute-start.4 = (bf16[1,64,512]{2,1,0:T(8,128)(2,1)S(1)}, bf16[1,64,512]{2,1,0:T(8,128)(2,1)S(1)}, u32[]{:S(2)}, u32[]{:S(2)}) collective-permute-start(bf16[1,64,512]{2,1,0:T(8,128)(2,1)S(1)} %slice_bitcast_fusion.24), channel_id=1, source_target_pairs={{0,2},{1,3},{2,0},{3,1},{4,6},{5,7},{6,4},{7,5},{8,10},{9,11},{10,... | collective-permute-start | bytes 196616 | tf_op jit(solution)/shard_map/ppermute | solution.py:29
  10.5 12.5 %collective-permute-start = (bf16[1,2,64,512]{3,2,1,0:T(8,128)(2,1)S(1)}, bf16[1,2,64,512]{3,2,1,0:T(8,128)(2,1)}, u32[]{:S(2)}, u32[]{:S(2)}) collective-permute-start(bf16[1,2,64,512]{3,2,1,0:T(8,128)(2,1)S(1)} %slice.90), channel_id=1, source_target_pairs={{0,16},{4,20},{8,24},{12,28},{16,0},{20,4},{24,8},{28,12},{1,17},{... | collective-permute-start | bytes 393224 | tf_op jit(solution)/shard_map/ppermute | solution.py:29
  21.5 4.1 %collective-permute-start.5 = (bf16[2,64,512]{2,1,0:T(8,128)(2,1)}, bf16[2,64,512]{2,1,0:T(8,128)(2,1)}, u32[]{:S(2)}, u32[]{:S(2)}) collective-permute-start(bf16[2,64,512]{2,1,0:T(8,128)(2,1)} %pad_maximum_fusion.4), channel_id=1, source_target_pairs={{0,1},{1,0},{2,3},{3,2},{4,5},{5,4},{6,7},{7,6},{8,9},{9,8},{10,11... | collective-permute-start | bytes 393224 | tf_op jit(solution)/shard_map/ppermute | solution.py:29
  24.0 8.8 %collective-permute-start.1 = (bf16[2,2,64,512]{3,2,1,0:T(8,128)(2,1)S(1)}, bf16[2,2,64,512]{3,2,1,0:T(8,128)(2,1)S(1)}, u32[]{:S(2)}, u32[]{:S(2)}) collective-permute-start(bf16[2,2,64,512]{3,2,1,0:T(8,128)(2,1)S(1)} %pad_maximum_fusion.2), channel_id=1, source_target_pairs={{0,8},{4,12},{8,0},{12,4},{16,24},{20,28},{24,16},{28,20},{1,9},{5... | collective-permute-start | bytes 786440 | tf_op jit(solution)/shard_map/ppermute | solution.py:29
  33.7 13.6 %collective-permute-start.2 = (bf16[1,4,2,64,512]{4,3,2,1,0:T(8,128)(2,1)S(1)}, bf16[1,4,2,64,512]{4,3,2,1,0:T(8,128)(2,1)S(1)}, u32[]{:S(2)}, u32[]{:S(2)}) collective-permute-start(bf16[1,4,2,64,512]{4,3,2,1,0:T(8,128)(2,1)S(1)} %maximum_bitcast_fusion), channel_id=1, source_target_pairs={{0,2},{1,3},{2,0},{3,1},{4,6},{5,7},{6,4},{7,5},{8,10},{9,11},{10,... | collective-permute-start | bytes 1572872 | tf_op jit(solution)/shard_map/ppermute | solution.py:29
  35.5 12.3 %collective-permute-start.16 = (bf16[256,128]{1,0:T(8,128)(2,1)S(1)}, bf16[256,128]{1,0:T(8,128)(2,1)S(1)}, u32[]{:S(2)}, u32[]{:S(2)}) collective-permute-start(bf16[256,128]{1,0:T(8,128)(2,1)S(1)} %get-tuple-element.39), channel_id=1, source_target_pairs={{0,8},{4,12},{8,0},{12,4},{16,24},{20,28},{24,16},{28,20},{1,9},{5... | collective-permute-start | bytes 196616 | tf_op jit(solution)/shard_map/ppermute | solution.py:29
  37.2 14.3 %collective-permute-start.17 = (bf16[256,128]{1,0:T(8,128)(2,1)S(1)}, bf16[256,128]{1,0:T(8,128)(2,1)S(1)}, u32[]{:S(2)}, u32[]{:S(2)}) collective-permute-start(bf16[256,128]{1,0:T(8,128)(2,1)S(1)} %get-tuple-element.41), channel_id=1, source_target_pairs={{0,16},{4,20},{8,24},{12,28},{16,0},{20,4},{24,8},{28,12},{1,17},{... | collective-permute-start | bytes 196616 | tf_op jit(solution)/shard_map/ppermute | solution.py:29
  37.5 14.0 %collective-permute-start.18 = (bf16[256,128]{1,0:T(8,128)(2,1)S(1)}, bf16[256,128]{1,0:T(8,128)(2,1)S(1)}, u32[]{:S(2)}, u32[]{:S(2)}) collective-permute-start(bf16[256,128]{1,0:T(8,128)(2,1)S(1)} %get-tuple-element.40), channel_id=1, source_target_pairs={{0,24},{4,28},{8,16},{12,20},{16,8},{20,12},{24,0},{28,4},{1,25},{... | collective-permute-start | bytes 196616 | tf_op jit(solution)/shard_map/ppermute | solution.py:29
  40.0 13.1 %collective-permute-start.7 = (bf16[256,128]{1,0:T(8,128)(2,1)S(1)}, bf16[256,128]{1,0:T(8,128)(2,1)S(1)}, u32[]{:S(2)}, u32[]{:S(2)}) collective-permute-start(bf16[256,128]{1,0:T(8,128)(2,1)S(1)} %get-tuple-element.42), channel_id=1, source_target_pairs={{0,8},{4,12},{8,0},{12,4},{16,24},{20,28},{24,16},{28,20},{1,9},{5... | collective-permute-start | bytes 196616 | tf_op jit(solution)/shard_map/ppermute | solution.py:29
  47.4 7.3 %collective-permute-start.8 = (bf16[256,128]{1,0:T(8,128)(2,1)S(1)}, bf16[256,128]{1,0:T(8,128)(2,1)S(1)}, u32[]{:S(2)}, u32[]{:S(2)}) collective-permute-start(bf16[256,128]{1,0:T(8,128)(2,1)S(1)} %get-tuple-element.44), channel_id=1, source_target_pairs={{0,16},{4,20},{8,24},{12,28},{16,0},{20,4},{24,8},{28,12},{1,17},{... | collective-permute-start | bytes 196616 | tf_op jit(solution)/shard_map/ppermute | solution.py:29
  47.8 6.8 %collective-permute-start.9 = (bf16[256,128]{1,0:T(8,128)(2,1)S(1)}, bf16[256,128]{1,0:T(8,128)(2,1)S(1)}, u32[]{:S(2)}, u32[]{:S(2)}) collective-permute-start(bf16[256,128]{1,0:T(8,128)(2,1)S(1)} %get-tuple-element.43), channel_id=1, source_target_pairs={{0,24},{4,28},{8,16},{12,20},{16,8},{20,12},{24,0},{28,4},{1,25},{... | collective-permute-start | bytes 196616 | tf_op jit(solution)/shard_map/ppermute | solution.py:29
  51.5 10.3 %collective-permute-start.3 = (bf16[2,4,2,64,512]{4,3,2,1,0:T(8,128)(2,1)S(1)}, bf16[2,4,2,64,512]{4,3,2,1,0:T(8,128)(2,1)S(1)}, u32[]{:S(2)}, u32[]{:S(2)}) collective-permute-start(bf16[2,4,2,64,512]{4,3,2,1,0:T(8,128)(2,1)S(1)} %pad_maximum_fusion.1), channel_id=1, source_target_pairs={{0,1},{1,0},{2,3},{3,2},{4,5},{5,4},{6,7},{7,6},{8,9},{9,8},{10,11... | collective-permute-start | bytes 3145736 | tf_op jit(solution)/shard_map/ppermute | solution.py:29
  51.5 4.7 %collective-permute-start.19 = (bf16[256,128]{1,0:T(8,128)(2,1)S(1)}, bf16[256,128]{1,0:T(8,128)(2,1)S(1)}, u32[]{:S(2)}, u32[]{:S(2)}) collective-permute-start(bf16[256,128]{1,0:T(8,128)(2,1)S(1)} %fusion.3.own_ref), channel_id=1, source_target_pairs={{0,4},{4,0},{8,12},{12,8},{16,20},{20,16},{24,28},{28,24},{1,5},{5... | collective-permute-start | bytes 196616 | tf_op jit(solution)/shard_map/ppermute | solution.py:29
  54.7 6.3 %collective-permute-start.10 = (bf16[256,128]{1,0:T(8,128)(2,1)S(1)}, bf16[256,128]{1,0:T(8,128)(2,1)S(1)}, u32[]{:S(2)}, u32[]{:S(2)}) collective-permute-start(bf16[256,128]{1,0:T(8,128)(2,1)S(1)} %fusion.7.own_ref), channel_id=1, source_target_pairs={{0,4},{4,0},{8,12},{12,8},{16,20},{20,16},{24,28},{28,24},{1,5},{5... | collective-permute-start | bytes 196616 | tf_op jit(solution)/shard_map/ppermute | solution.py:29
  56.5 8.7 %collective-permute-start.20 = (bf16[256,128]{1,0:T(8,128)(2,1)S(1)}, bf16[256,128]{1,0:T(8,128)(2,1)S(1)}, u32[]{:S(2)}, u32[]{:S(2)}) collective-permute-start(bf16[256,128]{1,0:T(8,128)(2,1)S(1)} %shard_map.88.rest_0_), channel_id=1, source_target_pairs={{0,8},{4,12},{8,0},{12,4},{16,24},{20,28},{24,16},{28,20},{1,9},{5... | collective-permute-start | bytes 196616 | tf_op jit(solution)/shard_map/ppermute | solution.py:29
  57.8 8.7 %collective-permute-start.21 = (bf16[256,128]{1,0:T(8,128)(2,1)S(1)}, bf16[256,128]{1,0:T(8,128)(2,1)S(1)}, u32[]{:S(2)}, u32[]{:S(2)}) collective-permute-start(bf16[256,128]{1,0:T(8,128)(2,1)S(1)} %shard_map.88.rest_0_), channel_id=1, source_target_pairs={{0,16},{4,20},{8,24},{12,28},{16,0},{20,4},{24,8},{28,12},{1,17},{... | collective-permute-start | bytes 196616 | tf_op jit(solution)/shard_map/ppermute | solution.py:29
  60.1 6.8 %collective-permute-start.22 = (bf16[256,128]{1,0:T(8,128)(2,1)S(1)}, bf16[256,128]{1,0:T(8,128)(2,1)S(1)}, u32[]{:S(2)}, u32[]{:S(2)}) collective-permute-start(bf16[256,128]{1,0:T(8,128)(2,1)S(1)} %shard_map.88.rest_0_), channel_id=1, source_target_pairs={{0,24},{4,28},{8,16},{12,20},{16,8},{20,12},{24,0},{28,4},{1,25},{... | collective-permute-start | bytes 196616 | tf_op jit(solution)/shard_map/ppermute | solution.py:29
  61.2 7.9 %collective-permute-start.11 = (bf16[256,128]{1,0:T(8,128)(2,1)S(1)}, bf16[256,128]{1,0:T(8,128)(2,1)S(1)}, u32[]{:S(2)}, u32[]{:S(2)}) collective-permute-start(bf16[256,128]{1,0:T(8,128)(2,1)S(1)} %shard_map.84.rest_0_), channel_id=1, source_target_pairs={{0,8},{4,12},{8,0},{12,4},{16,24},{20,28},{24,16},{28,20},{1,9},{5... | collective-permute-start | bytes 196616 | tf_op jit(solution)/shard_map/ppermute | solution.py:29
  61.8 8.0 %collective-permute-start.12 = (bf16[256,128]{1,0:T(8,128)(2,1)S(1)}, bf16[256,128]{1,0:T(8,128)(2,1)S(1)}, u32[]{:S(2)}, u32[]{:S(2)}) collective-permute-start(bf16[256,128]{1,0:T(8,128)(2,1)S(1)} %shard_map.84.rest_0_), channel_id=1, source_target_pairs={{0,16},{4,20},{8,24},{12,28},{16,0},{20,4},{24,8},{28,12},{1,17},{... | collective-permute-start | bytes 196616 | tf_op jit(solution)/shard_map/ppermute | solution.py:29
  65.2 6.1 %collective-permute-start.13 = (bf16[256,128]{1,0:T(8,128)(2,1)S(1)}, bf16[256,128]{1,0:T(8,128)(2,1)S(1)}, u32[]{:S(2)}, u32[]{:S(2)}) collective-permute-start(bf16[256,128]{1,0:T(8,128)(2,1)S(1)} %shard_map.84.rest_0_), channel_id=1, source_target_pairs={{0,24},{4,28},{8,16},{12,20},{16,8},{20,12},{24,0},{28,4},{1,25},{... | collective-permute-start | bytes 196616 | tf_op jit(solution)/shard_map/ppermute | solution.py:29
  66.5 7.0 %copy-start.4 = (s32[2048,1]{0,1:T(1,128)S(1)}, s32[2048,1]{0,1:T(1,128)}, u32[]{:S(2)}) copy-start(s32[2048,1]{0,1:T(1,128)} %param.9) | copy-start | bytes 24580
  67.6 12.9 %collective-permute-start.23 = (bf16[4,256,128]{2,1,0:T(8,128)(2,1)S(1)}, bf16[4,256,128]{2,1,0:T(8,128)(2,1)}, u32[]{:S(2)}, u32[]{:S(2)}) collective-permute-start(bf16[4,256,128]{2,1,0:T(8,128)(2,1)S(1)} %shard_map.89.blocks_ref), channel_id=1, source_target_pairs={{0,4},{4,0},{8,12},{12,8},{16,20},{20,16},{24,28},{28,24},{1,5},{5... | collective-permute-start | bytes 786440 | tf_op jit(solution)/shard_map/ppermute | solution.py:29
  72.8 10.8 %collective-permute-start.14 = (bf16[4,256,128]{2,1,0:T(8,128)(2,1)}, bf16[4,256,128]{2,1,0:T(8,128)(2,1)}, u32[]{:S(2)}, u32[]{:S(2)}) collective-permute-start(bf16[4,256,128]{2,1,0:T(8,128)(2,1)} %shard_map.85.blocks_ref), channel_id=1, source_target_pairs={{0,4},{4,0},{8,12},{12,8},{16,20},{20,16},{24,28},{28,24},{1,5},{5... | collective-permute-start | bytes 786440 | tf_op jit(solution)/shard_map/ppermute | solution.py:29
  73.8 1.2 %copy-start = (bf16[2048,256]{1,0:T(8,128)(2,1)S(1)}, bf16[2048,256]{1,0:T(8,128)(2,1)}, u32[]{:S(2)}) copy-start(bf16[2048,256]{1,0:T(8,128)(2,1)} %basis_ref.7) | copy-start | bytes 3145732
  75.1 2.3 %copy-start.1 = (bf16[2048,256]{1,0:T(8,128)(2,1)S(1)}, bf16[2048,256]{1,0:T(8,128)(2,1)}, u32[]{:S(2)}) copy-start(bf16[2048,256]{1,0:T(8,128)(2,1)} %basis_ref.7) | copy-start | bytes 3145732
  (3 other events, 2.6 us)

commit v2 on v0

v2 whole, which is shorter than its diff:
```python
import functools

import jax
import jax.numpy as jnp
from jax import lax
from jax.experimental import pallas as pl
from jax.experimental.pallas import tpu as pltpu
from jax.sharding import PartitionSpec as P

F32 = jnp.float32
BF16 = jnp.bfloat16
CHUNKS = 2
COPIES = 2
VMEM_LIMIT = 48 * 1024 * 1024
VMEM = pl.BlockSpec(memory_space=pltpu.VMEM)
SMEM = pl.BlockSpec(memory_space=pltpu.SMEM)
HBM = pl.BlockSpec(memory_space=pltpu.HBM)


def cost(microseconds=0):
    return pl.CostEstimate(
        flops=microseconds * 10**9 + 1024, bytes_accessed=1024, transcendentals=0
    )


def params():
    return pltpu.CompilerParams(vmem_limit_bytes=VMEM_LIMIT)


def tie(*values):
    return lax.optimization_barrier(values)


def swapped(value, axis, mask):
    return lax.ppermute(value, axis, [(i, i ^ mask) for i in range(lax.axis_size(axis))])


def compress_kernel(groups, me_ref, owner_hbm, basis_hbm, fields_hbm, *rest):
    outs, (owner_ref, basis_ref, fields_ref, sems) = rest[: len(groups)], rest[len(groups) :]
    rows = basis_ref.shape[0] // COPIES
    copies = [pltpu.make_async_copy(owner_hbm, owner_ref, sems.at[2 * COPIES])]
    for k, (source, target) in enumerate(((basis_hbm, basis_ref), (fields_hbm, fields_ref))):
        for p in range(COPIES):
            part = pl.ds(p * rows, rows)
            copies.append(
                pltpu.make_async_copy(source.at[part], target.at[part], sems.at[k * COPIES + p])
            )
    for copy in copies:
        copy.start()
    for copy in copies[: COPIES + 1]:
        copy.wait()
    relative = owner_ref[...] ^ me_ref[0]
    basis_t = basis_ref[...].T
    for copy in copies[COPIES + 1 :]:
        copy.wait()
    fields = fields_ref[...]
    for out, group in zip(outs, groups):
        for i, j in enumerate(group):
            masked = jnp.where(relative == j, basis_t, jnp.zeros((), BF16))
            out[i] = jnp.dot(masked, fields, preferred_element_type=F32).astype(out.dtype)


def compress(me, owner_row, basis, fields, groups, dtype):
    rows, cols = fields.shape
    width = basis.shape[1]
    count = sum(len(g) for g in groups)
    return list(
        pl.pallas_call(
            functools.partial(compress_kernel, groups),
            out_shape=[jax.ShapeDtypeStruct((len(g), width, cols), dtype) for g in groups],
            in_specs=[SMEM, HBM, HBM, HBM],
            out_specs=[VMEM] * len(groups),
            scratch_shapes=[
                pltpu.VMEM((1, rows), jnp.int32),
                pltpu.VMEM((rows, width), BF16),
                pltpu.VMEM((rows, cols), BF16),
                pltpu.SemaphoreType.DMA((2 * COPIES + 1,)),
            ],
            cost_estimate=cost(2),
        )(me, owner_row, basis, fields)
    )


def near_kernel(index_ref, count_ref, blocks_hbm, fields_ref, near_ref, blocks_ref, sems):
    groups, slots, size, _ = blocks_ref.shape
    copies = [
        pltpu.make_async_copy(blocks_hbm.at[g], blocks_ref.at[g], sems.at[g]) for g in range(groups)
    ]
    for copy in copies:
        copy.start()
    for g, copy in enumerate(copies):
        chosen = []
        for j in range(slots):
            start = pl.multiple_of(index_ref[g, j] * size, size)
            piece = fields_ref[pl.ds(start, size), :]
            chosen.append(jnp.where(j < count_ref[g], piece, jnp.zeros_like(piece)))
        copy.wait()
        weights = jnp.concatenate([blocks_ref[g, j] for j in range(slots)], axis=1)
        near_ref[g * size : (g + 1) * size, :] = jnp.dot(
            weights, jnp.concatenate(chosen, axis=0), preferred_element_type=F32
        )


def near_field(near_index, near_count, near_blocks, fields):
    rows, cols = fields.shape
    return pl.pallas_call(
        near_kernel,
        out_shape=jax.ShapeDtypeStruct((rows, cols), F32),
        in_specs=[SMEM, SMEM, HBM, VMEM],
        out_specs=VMEM,
        scratch_shapes=[
            pltpu.VMEM(near_blocks.shape, BF16),
            pltpu.SemaphoreType.DMA((near_blocks.shape[0],)),
        ],
        compiler_params=params(),
        cost_estimate=cost(6),
    )(near_index, near_count, near_blocks, fields)


def apply_rows(me, pieces, stacked, out):
    product = jnp.dot(jnp.concatenate(pieces, axis=0), stacked, preferred_element_type=F32)
    size = pieces[0].shape[0]
    for o in range(len(pieces)):
        start = pl.multiple_of((me ^ o) * size, size)
        out[pl.ds(start, size), :] = product[o * size : (o + 1) * size].astype(out.dtype)


def first_level_kernel(me_ref, *refs):
    rows, (own_ref, other_ref, out_ref) = refs[:-3], refs[-3:]
    stacked = jnp.concatenate([own_ref[...], other_ref[...]], axis=0)
    apply_rows(me_ref[0], [ref[...] for ref in rows], stacked, out_ref)


def first_level(rhs_me, rows, own, other):
    return pl.pallas_call(
        first_level_kernel,
        out_shape=jax.ShapeDtypeStruct(own.shape, BF16),
        in_specs=[SMEM] + [VMEM] * (len(rows) + 2),
        out_specs=VMEM,
        compiler_params=params(),
        cost_estimate=cost(),
    )(rhs_me, *rows, own, other)


def later_levels_kernel(n_rhs, me_ref, *refs):
    rows, blocks = refs[:n_rhs], refs[n_rhs : -1 - CHUNKS]
    outs, held_ref = refs[-1 - CHUNKS : -1], refs[-1]
    count, levels = rows[0].shape[:2]
    blocks = [ref[...] for ref in blocks]
    for level in range(levels):
        for s in range(count):
            stacked = jnp.concatenate([blocks[s], blocks[s ^ (1 << level)]], axis=0)
            apply_rows(me_ref[0], [ref[s, level] for ref in rows], stacked, held_ref.at[s])
        blocks = [held_ref[s] for s in range(count)]
    width = outs[0].shape[2]
    for s in range(count):
        for c, out in enumerate(outs):
            out[s] = blocks[s][:, c * width : (c + 1) * width]


def later_levels(rhs_me, rows, blocks):
    width, cols = blocks[0].shape
    part = jax.ShapeDtypeStruct((len(blocks), width, cols // CHUNKS), BF16)
    return pl.pallas_call(
        functools.partial(later_levels_kernel, len(rows)),
        out_shape=[part] * CHUNKS,
        in_specs=[SMEM] + [VMEM] * (len(rows) + len(blocks)),
        out_specs=[VMEM] * CHUNKS,
        scratch_shapes=[pltpu.VMEM((len(blocks), width, cols), BF16)],
        compiler_params=params(),
        cost_estimate=cost(),
    )(rhs_me, *rows, *blocks)


def far_tile(me_ref, owner_ref, basis_ref, blocks_ref, base_ref, first, part):
    relative = owner_ref[part, :] ^ me_ref[0]
    basis = basis_ref[part, :]
    count, width, part_cols = blocks_ref.shape
    masked = [
        jnp.where(relative == first + 2 * i, basis, jnp.zeros((), BF16)) for i in range(count)
    ]
    total = jnp.dot(
        jnp.concatenate(masked, axis=1),
        blocks_ref[...].reshape(count * width, part_cols),
        preferred_element_type=F32,
    )
    return total.astype(BF16).astype(F32) + base_ref[part, :]


def far_kernel(first, tile, me_ref, owner_ref, basis_ref, blocks_ref, base_ref, out_ref):
    for t in range(out_ref.shape[0] // tile):
        part = pl.ds(t * tile, tile)
        value = far_tile(me_ref, owner_ref, basis_ref, blocks_ref, base_ref, first, part)
        out_ref[part, :] = value.astype(out_ref.dtype)


def far_field(me, owner, basis, blocks, base, first, dtype):
    rows, width = basis.shape
    count, _, part_cols = blocks.shape
    return pl.pallas_call(
        functools.partial(far_kernel, first, min(rows, 512)),
        out_shape=jax.ShapeDtypeStruct((rows, part_cols), dtype),
        in_specs=[SMEM, VMEM, VMEM, VMEM, VMEM],
        out_specs=VMEM,
        compiler_params=params(),
        cost_estimate=cost(),
    )(me, owner, basis, blocks, base)


def last_kernel(
    first, tile, me_ref, owner_ref, basis_ref, blocks_ref, base_ref, *rest
):
    earlier, (out_hbm, held, sems) = rest[:-3], rest[-3:]
    rows, part_cols = held.shape
    copies = []
    for c, ref in enumerate(earlier):
        target = out_hbm.at[:, pl.ds(c * part_cols, part_cols)]
        copies.append(pltpu.make_async_copy(ref, target, sems.at[c]))
        copies[-1].start()
    for t in range(rows // tile):
        part = pl.ds(t * tile, tile)
        value = far_tile(me_ref, owner_ref, basis_ref, blocks_ref, base_ref, first, part)
        held[part, :] = value.astype(BF16)
        target = out_hbm.at[part, pl.ds(len(earlier) * part_cols, part_cols)]
        copies.append(pltpu.make_async_copy(held.at[part], target, sems.at[len(earlier) + t]))
        copies[-1].start()
    for copy in copies:
        copy.wait()


def last_far_field(me, owner, basis, blocks, base, first, earlier):
    rows, width = basis.shape
    count, _, part_cols = blocks.shape
    tile = min(rows, 512)
    return pl.pallas_call(
        functools.partial(last_kernel, first, tile),
        out_shape=jax.ShapeDtypeStruct((rows, part_cols * (1 + len(earlier))), BF16),
        in_specs=[SMEM] + [VMEM] * (4 + len(earlier)),
        out_specs=HBM,
        scratch_shapes=[
            pltpu.VMEM((rows, part_cols), BF16),
            pltpu.SemaphoreType.DMA((len(earlier) + rows // tile,)),
        ],
        compiler_params=params(),
        cost_estimate=cost(),
    )(me, owner, basis, blocks, base, *earlier)


def on_device(
    fields, owner, source_basis, field_basis, transfer, near_blocks, near_index, near_count
):
    n_leaf = lax.axis_size("leaf")
    rows, cols = fields.shape
    levels = transfer.shape[1]
    group = 2**levels
    outer = n_leaf // group
    upper = group // 2
    chunks = CHUNKS
    n_rhs = lax.axis_size("rhs")
    me = lax.axis_index("leaf").astype(jnp.int32)[None]
    rhs_me = lax.axis_index("rhs").astype(jnp.int32)[None]
    owner_row = owner.reshape(1, rows)

    parts = [list(range(upper - 1, upper // 2 - 1, -1)), list(range(upper // 2 - 1, -1, -1))]

    def groups(low):
        return [[o * group + 2 * s + low for s in part for o in range(outer)] for part in parts]

    send = compress(me, owner_row, source_basis, fields, groups(1), BF16)

    fields, send[0], send[1] = tie(fields, *send)
    got = [swapped(s, "leaf", 1) for s in send]
    keep = compress(me, owner_row, source_basis, fields, groups(0)[:1], F32)

    def reduced(keep, got, part):
        total = keep + got.astype(F32)
        sums = []
        for i in range(len(part)):
            mine = total[i * outer]
            for o in range(1, outer):
                piece = total[i * outer + o].astype(BF16)
                mine = mine + swapped(piece, "leaf", o * group).astype(F32)
            sums.append(mine)
        return sums

    transfer, keep[0] = tie(transfer, keep[0])
    later = {0: transfer[0, 1:]}
    first = {0: transfer[0, 0]}
    later_next = swapped(later[0], "leaf", upper)
    first_next = swapped(first[0], "rhs", n_rhs // 2)

    far_sums = reduced(keep[0], got[0], parts[0])
    arrived = [swapped(v.astype(BF16), "leaf", 2 * s) for s, v in zip(parts[0], far_sums)]
    fields, far_sums[0] = tie(fields, far_sums[0])
    keep += compress(me, owner_row, source_basis, fields, groups(0)[1:], F32)
    near_sums = reduced(keep[1], got[1], parts[1])
    arrived += [swapped(v.astype(BF16), "leaf", 2 * s) for s, v in zip(parts[1][:-1], near_sums)]
    mine = near_sums[-1]

    mine, later_next, first_next = tie(mine, later_next, first_next)
    mask = upper // 2
    while mask:
        later.update({s ^ mask: later_next[i] if later_next.ndim == 4 else later_next for i, s in enumerate(sorted(later))})
        mask //= 2
        if mask:
            later_next = swapped(jnp.stack([later[s] for s in sorted(later)]), "leaf", 2 * mask)
    mask = n_rhs // 2
    while mask:
        first.update({o ^ mask: first_next[i] if first_next.ndim == 3 else first_next for i, o in enumerate(sorted(first))})
        mask //= 2
        if mask:
            first_next = swapped(jnp.stack([first[o] for o in sorted(first)]), "rhs", mask)
    later = {0: jnp.stack([later[s] for s in range(upper)])}
    later_next = swapped(later[0], "rhs", n_rhs // 2)

    coefficients = mine
    for value in arrived:
        coefficients = coefficients + value.astype(F32)
    coefficients = coefficients.astype(BF16)
    coefficients = first_level(
        rhs_me, [first[o] for o in range(n_rhs)], coefficients, swapped(coefficients, "leaf", 1)
    )
    blocks = {s: swapped(coefficients, "leaf", 2 * s) for s in range(upper - 1, 0, -1)}
    blocks[0], later_next, fields = tie(coefficients, later_next, fields)
    mask = n_rhs // 2
    later[mask] = later_next
    mask //= 2
    while mask:
        later.update({o ^ mask: swapped(v, "rhs", mask) for o, v in later.items()})
        mask //= 2
    near = near_field(near_index, near_count, near_blocks, fields)
    near, blocks[0] = tie(near, blocks[0])
    owns = later_levels(rhs_me, [later[o] for o in range(n_rhs)], [blocks[s] for s in range(upper)])
    if outer > 1:
        owns = [
            jnp.concatenate([own] + [swapped(own, "leaf", o * group) for o in range(1, outer)])
            for own in owns
        ]
    others = [swapped(own, "leaf", 1) for own in owns]
    bases = []
    width = cols // chunks
    for c in range(chunks):
        base = near[:, c * width : (c + 1) * width]
        bases.append(far_field(me, owner, field_basis, owns[c], base, 0, F32))
    done = []
    for c in range(chunks - 1):
        done.append(far_field(me, owner, field_basis, others[c], bases[c], 1, BF16))
    return last_far_field(me, owner, field_basis, others[-1], bases[-1], 1, done)


def solution(mesh):
    in_specs = (
        P("leaf", "rhs"),
        P("leaf", None),
        P("leaf", None),
        P("leaf", None),
        P("leaf", None, "rhs", None),
        P("leaf", None, None, None),
        P("leaf", None),
        P("leaf"),
    )
    out_specs = P("leaf", "rhs")
    return jax.shard_map(
        on_device, mesh=mesh, in_specs=in_specs, out_specs=out_specs, check_vma=False
    )
```

time: 194 us -> 70.7 us (0.36)
  waiting for transfers between devices: 86.8 us -> 20.8 us
  local copies, waits for them, and re-layouts: 47.5 us -> 0.65 us
  Pallas kernels: 0 us -> 25 us
  starting transfers between devices: 3.36 us -> 22.4 us
  blocking collectives: 17.3 us -> 0 us
  matrix products: 16 us -> 0 us
  between operations: 13.5 us -> 0.28 us
  other arithmetic: 8.52 us -> 1.39 us
    reduce_scatter x1 -> x0, waiting for transfers between devices: 70.9 us -> none  [on_device(): lax.psum_scatter(jnp.einsum('bck,bcn->bkn', v_three, x_three, preferred_e...]
    scatter x3 -> x0, local copies, waits for them, and re-layouts: 32.9 us -> none  [the longest x2 22.5 us: on_device(): jnp.zeros((n_leaf * capacity, basis_width), jnp.bfloat16).at[slot_index]]
    pallas_call x0 -> x10, Pallas kernels: none -> 25 us  [the longest x3 9.72 us: compress(): pl.pallas_call(functools.partial(compress_kernel, groups), out_shape=[jax...]
    ppermute x3 -> x18, starting transfers between devices: 3.32 us -> 22.4 us  [swapped(): lax.ppermute(value, axis, [(i, i ^ mask) for i in range(lax.axis_size(axi...]
    ppermute x3 -> x18, waiting for transfers between devices: 2.56 us -> 20.8 us  [swapped(): lax.ppermute(value, axis, [(i, i ^ mask) for i in range(lax.axis_size(axi...]
    all_gather x3 -> x0, blocking collectives: 17.3 us -> none  [on_device(): lax.all_gather(transfer[0, level_num], 'rhs', axis=0, tiled=True)]
    dot_general x6 -> x0, matrix products: 16 us -> none  [the longest x1 8.62 us: on_device(): jnp.einsum('gjab,gjbn->gan', near_blocks, chosen, preferred_element_type=...]
    all_gather x1 -> x0, waiting for transfers between devices: 13.3 us -> none  [on_device(): lax.all_gather(coefficients[None], 'leaf', axis=0, tiled=True)]
  transfers between devices with their start and end apart: 5 -> 18, of which waited for: 3 -> 8; matrix products, arithmetic and copies ran while one was open for 13% -> 3% of each run, Pallas kernels for 0% -> 26%
where the time goes in v2:
time: 70.7 us; the launch traced here: 70.5 us
  Pallas kernels  25 us (35%)
  starting transfers between devices  22.4 us (32%)
  waiting for transfers between devices  20.8 us (29%)
  other arithmetic  1.39 us (2%)
    ppermute x18, starting transfers between devices, swapped(): lax.ppermute(value, axis, [(i, i ^ mask) for i in range(lax.axis_size(axi...  22.4 us
    ppermute x18, waiting for transfers between devices, swapped(): lax.ppermute(value, axis, [(i, i ^ mask) for i in range(lax.axis_size(axi...  20.8 us
    pallas_call x3, Pallas kernels, compress(): pl.pallas_call(functools.partial(compress_kernel, groups), out_shape=[jax...  9.72 us
    pallas_call x1, Pallas kernels, near_field(): pl.pallas_call(near_kernel, out_shape=jax.ShapeDtypeStruct((rows, cols),...  6.84 us
    pallas_call x3, Pallas kernels, far_field(): pl.pallas_call(functools.partial(far_kernel, first, min(rows, 512)), out_...  4.88 us
    pallas_call x1, Pallas kernels, last_far_field(): pl.pallas_call(functools.partial(last_kernel, first, tile), out_shape=jax...  2.32 us
  transfers between devices with their start and end apart: 18, of which 8 were waited for; matrix products, arithmetic and copies ran while one was open for 3% of the time, Pallas kernels for 26%

profile of v2, /device:TPU:0, one launch (start us, length us, event | category | flops | bytes accessed | tf_op | source)
XLA Modules:
  0.0 70.5 jit_solution(15441944634146506543)
XLA Ops:
  0.0 3.6 %shard_map.82 = (bf16[2,256,256]{2,1,0:T(8,128)(2,1)}, bf16[2,256,256]{2,1,0:T(8,128)(2,1)}) custom-call(s32[1]{0:T(128)} %bitcast.me_ref, s32[1,2048]{1,0:T(1,128)} %bitcast.28, bf16[2048,256]{1,0:T(8,128)(2,1)} %basis_hbm.5, bf16[2048,256]{1,0:T(8,128)(2,1)} %fields_ref), custom_call_target="tpu_custom_call" | custom-call | flops 2000001024 | bytes 1024 | tf_op jit(solution)/shard_map/pallas_call | solution.py:68
  3.6 3.0 %collective-permute-start.1 = (bf16[2,256,256]{2,1,0:T(8,128)(2,1)}, bf16[2,256,256]{2,1,0:T(8,128)(2,1)S(1)}, u32[]{:S(2)}, u32[]{:S(2)}) collective-permute-start(bf16[2,256,256]{2,1,0:T(8,128)(2,1)} %get-tuple-element.30), channel_id=1, source_target_pairs={{0,4},{4,0},{8,12},{12,8},{16,20},{20,16},{24,28},{28,24},{1,5},{5... | collective-permute-start | bytes 786440 | tf_op jit(solution)/shard_map/ppermute | solution.py:35
  6.6 3.1 %shard_map.83 = f32[2,256,256]{2,1,0:T(8,128)} custom-call(s32[1]{0:T(128)} %bitcast.me_ref, s32[1,2048]{1,0:T(1,128)} %bitcast.29, bf16[2048,256]{1,0:T(8,128)(2,1)} %basis_hbm.5, bf16[2048,256]{1,0:T(8,128)(2,1)} %fields_ref), custom_call_target="tpu_custom_call" | custom-call | flops 2000001024 | bytes 1024 | tf_op jit(solution)/shard_map/pallas_call | solution.py:68
  9.7 1.6 %collective-permute-start.3 = (bf16[64,512]{1,0:T(8,128)(2,1)S(1)}, bf16[64,512]{1,0:T(8,128)(2,1)S(1)}, u32[]{:S(2)}, u32[]{:S(2)}) collective-permute-start(bf16[64,512]{1,0:T(8,128)(2,1)S(1)} %get-tuple-element.48.refs_0_), channel_id=1, source_target_pairs={{0,2},{1,3},{2,0},{3,1},{4,6},{5,7},{6,4},{7,5},{8,10},{9,11},{10,... | collective-permute-start | bytes 196616 | tf_op jit(solution)/shard_map/ppermute | solution.py:35
  11.3 2.7 %collective-permute-start.2 = (bf16[2,64,512]{2,1,0:T(8,128)(2,1)S(1)}, bf16[2,64,512]{2,1,0:T(8,128)(2,1)S(1)}, u32[]{:S(2)}, u32[]{:S(2)}) collective-permute-start(bf16[2,64,512]{2,1,0:T(8,128)(2,1)S(1)} %get-tuple-element.50), channel_id=1, source_target_pairs={{0,16},{4,20},{8,24},{12,28},{16,0},{20,4},{24,8},{28,12},{1,17},{... | collective-permute-start | bytes 393224 | tf_op jit(solution)/shard_map/ppermute | solution.py:35
  14.0 0.5 collective-permute-start
  14.9 3.1 %shard_map.84 = f32[2,256,256]{2,1,0:T(8,128)} custom-call(s32[1]{0:T(128)} %bitcast.me_ref, s32[1,2048]{1,0:T(1,128)} %bitcast.30, bf16[2048,256]{1,0:T(8,128)(2,1)} %basis_hbm.5, bf16[2048,256]{1,0:T(8,128)(2,1)} %fields_ref), custom_call_target="tpu_custom_call" | custom-call | flops 2000001024 | bytes 1024 | tf_op jit(solution)/shard_map/pallas_call | solution.py:68
  18.0 1.2 %convert_add_fusion = f32[2,256,256]{2,1,0:T(8,128)S(1)} fusion(f32[2,256,256]{2,1,0:T(8,128)} %shard_map.84, bf16[2,256,256]{2,1,0:T(8,128)(2,1)S(1)} %collective-permute-done.1), kind=kLoop, calls=%fused_computation.1 | loop fusion | flops 262144 | bytes 1310720 | tf_op jit(solution)/shard_map/add | solution.py:276
  19.2 0.6 collective-permute-done.2
  19.8 1.1 %collective-permute-start.4 = (bf16[2,2,64,512]{3,2,1,0:T(8,128)(2,1)S(1)}, bf16[2,2,64,512]{3,2,1,0:T(8,128)(2,1)S(1)}, u32[]{:S(2)}, u32[]{:S(2)}) collective-permute-start(bf16[2,2,64,512]{3,2,1,0:T(8,128)(2,1)S(1)} %pad_maximum_fusion.1), channel_id=1, source_target_pairs={{0,8},{4,12},{8,0},{12,4},{16,24},{20,28},{24,16},{28,20},{1,9},{5... | collective-permute-start | bytes 786440 | tf_op jit(solution)/shard_map/ppermute | solution.py:35
  21.3 2.3 %collective-permute-start.7 = (bf16[256,256]{1,0:T(8,128)(2,1)S(1)}, bf16[256,256]{1,0:T(8,128)(2,1)S(1)}, u32[]{:S(2)}, u32[]{:S(2)}) collective-permute-start(bf16[256,256]{1,0:T(8,128)(2,1)S(1)} %get-tuple-element.43), channel_id=1, source_target_pairs={{0,24},{4,28},{8,16},{12,20},{16,8},{20,12},{24,0},{28,4},{1,25},{... | collective-permute-start | bytes 393224 | tf_op jit(solution)/shard_map/ppermute | solution.py:35
  23.6 0.8 %collective-permute-start.8 = (bf16[256,256]{1,0:T(8,128)(2,1)S(1)}, bf16[256,256]{1,0:T(8,128)(2,1)S(1)}, u32[]{:S(2)}, u32[]{:S(2)}) collective-permute-start(bf16[256,256]{1,0:T(8,128)(2,1)S(1)} %get-tuple-element.44), channel_id=1, source_target_pairs={{0,16},{4,20},{8,24},{12,28},{16,0},{20,4},{24,8},{28,12},{1,17},{... | collective-permute-start | bytes 393224 | tf_op jit(solution)/shard_map/ppermute | solution.py:35
  24.4 1.4 %collective-permute-start.9 = (bf16[256,256]{1,0:T(8,128)(2,1)S(1)}, bf16[256,256]{1,0:T(8,128)(2,1)S(1)}, u32[]{:S(2)}, u32[]{:S(2)}) collective-permute-start(bf16[256,256]{1,0:T(8,128)(2,1)S(1)} %fusion.1), channel_id=1, source_target_pairs={{0,8},{4,12},{8,0},{12,4},{16,24},{20,28},{24,16},{28,20},{1,9},{5... | collective-permute-start | bytes 393224 | tf_op jit(solution)/shard_map/ppermute | solution.py:35
  25.9 6.8 %collective-permute-done.4 = bf16[2,2,64,512]{3,2,1,0:T(8,128)(2,1)S(1)} collective-permute-done((bf16[2,2,64,512]{3,2,1,0:T(8,128)(2,1)S(1)}, bf16[2,2,64,512]{3,2,1,0:T(8,128)(2,1)S(1)}, u32[]{:S(2)}, u32[]{:S(2)}) %collective-permute-start.4) | collective-permute-done | bytes 262176 | tf_op jit(solution)/shard_map/ppermute | solution.py:35
  32.8 0.6 collective-permute-start.11
  33.4 2.0 %collective-permute-done.8 = bf16[256,256]{1,0:T(8,128)(2,1)S(1)} collective-permute-done((bf16[256,256]{1,0:T(8,128)(2,1)S(1)}, bf16[256,256]{1,0:T(8,128)(2,1)S(1)}, u32[]{:S(2)}, u32[]{:S(2)}) %collective-permute-start.8) | collective-permute-done | bytes 131104 | tf_op jit(solution)/shard_map/ppermute | solution.py:35
  35.5 0.8 %collective-permute-start.10 = (bf16[256,256]{1,0:T(8,128)(2,1)S(1)}, bf16[256,256]{1,0:T(8,128)(2,1)S(1)}, u32[]{:S(2)}, u32[]{:S(2)}) collective-permute-start(bf16[256,256]{1,0:T(8,128)(2,1)S(1)} %add_convert_fusion.refs_4_), channel_id=1, source_target_pairs={{0,4},{4,0},{8,12},{12,8},{16,20},{20,16},{24,28},{28,24},{1,5},{5... | collective-permute-start | bytes 393224 | tf_op jit(solution)/shard_map/ppermute | solution.py:35
  36.3 4.2 %collective-permute-done.10.refs_5_ = bf16[256,256]{1,0:T(8,128)(2,1)S(1)} collective-permute-done((bf16[256,256]{1,0:T(8,128)(2,1)S(1)}, bf16[256,256]{1,0:T(8,128)(2,1)S(1)}, u32[]{:S(2)}, u32[]{:S(2)}) %collective-permute-start.10) | collective-permute-done | bytes 131104 | tf_op jit(solution)/shard_map/ppermute | solution.py:35
  40.8 1.7 %collective-permute-start.13 = (bf16[256,256]{1,0:T(8,128)(2,1)S(1)}, bf16[256,256]{1,0:T(8,128)(2,1)S(1)}, u32[]{:S(2)}, u32[]{:S(2)}) collective-permute-start(bf16[256,256]{1,0:T(8,128)(2,1)S(1)} %shard_map.85.refs_4_), channel_id=1, source_target_pairs={{0,8},{4,12},{8,0},{12,4},{16,24},{20,28},{24,16},{28,20},{1,9},{5... | collective-permute-start | bytes 393224 | tf_op jit(solution)/shard_map/ppermute | solution.py:35
  42.5 3.3 %collective-permute-start.14 = (bf16[256,256]{1,0:T(8,128)(2,1)S(1)}, bf16[256,256]{1,0:T(8,128)(2,1)S(1)}, u32[]{:S(2)}, u32[]{:S(2)}) collective-permute-start(bf16[256,256]{1,0:T(8,128)(2,1)S(1)} %shard_map.85.refs_4_), channel_id=1, source_target_pairs={{0,16},{4,20},{8,24},{12,28},{16,0},{20,4},{24,8},{28,12},{1,17},{... | collective-permute-start | bytes 393224 | tf_op jit(solution)/shard_map/ppermute | solution.py:35
  45.8 0.5 collective-permute-start.12
  46.3 6.8 %shard_map.86 = f32[2048,256]{1,0:T(8,128)S(1)} custom-call(s32[8,7]{1,0:T(8,128)S(1)} %copy-done.2, s32[8]{0:T(128)S(1)} %copy-done.3, bf16[8,7,256,256]{3,2,1,0:T(8,128)(2,1)} %blocks_hbm.1, bf16[2048,256]{1,0:T(8,128)(2,1)S(1)} %copy-done.1), custom_call_target="tpu_custom_call" | custom-call | flops 6000001024 | bytes 1024 | tf_op jit(solution)/shard_map/pallas_call | solution.py:106
  53.2 1.2 %collective-permute-done.14.refs_6_ = bf16[256,256]{1,0:T(8,128)(2,1)S(1)} collective-permute-done((bf16[256,256]{1,0:T(8,128)(2,1)S(1)}, bf16[256,256]{1,0:T(8,128)(2,1)S(1)}, u32[]{:S(2)}, u32[]{:S(2)}) %collective-permute-start.14) | collective-permute-done | bytes 131104 | tf_op jit(solution)/shard_map/ppermute | solution.py:35
  54.4 1.0 %shard_map.87 = (bf16[4,256,128]{2,1,0:T(8,128)(2,1)S(1)}, bf16[4,256,128]{2,1,0:T(8,128)(2,1)S(1)}) custom-call(s32[1]{0:T(128)} %bitcast.1.me_ref, bf16[4,2,64,512]{3,2,1,0:T(8,128)(2,1)S(1)} %pad_maximum_fusion.refs_0_, bf16[4,2,64,512]{3,2,1,0:T(8,128)(2,1)S(1)} %collective-permute-done.5.refs_1_, ...), custom_call_target="tpu_custom_call" | custom-call | flops 1024 | bytes 1024 | tf_op jit(solution)/shard_map/pallas_call | solution.py:164
  55.4 0.6 collective-permute-start.17
  56.0 1.5 %collective-permute-start.16 = (bf16[4,256,128]{2,1,0:T(8,128)(2,1)S(1)}, bf16[4,256,128]{2,1,0:T(8,128)(2,1)S(1)}, u32[]{:S(2)}, u32[]{:S(2)}) collective-permute-start(bf16[4,256,128]{2,1,0:T(8,128)(2,1)S(1)} %get-tuple-element.38.blocks_ref), channel_id=1, source_target_pairs={{0,4},{4,0},{8,12},{12,8},{16,20},{20,16},{24,28},{28,24},{1,5},{5... | collective-permute-start | bytes 786440 | tf_op jit(solution)/shard_map/ppermute | solution.py:35
  57.6 1.6 %shard_map.89.base_ref = f32[2048,128]{1,0:T(8,128)S(1)} custom-call(s32[1]{0:T(128)} %bitcast.me_ref, s32[2048,1]{1,0:T(8,128)S(1)} %copy.12.owner_ref, bf16[2048,256]{1,0:T(8,128)(2,1)S(1)} %copy-done, bf16[4,256,128]{2,1,0:T(8,128)(2,1)S(1)} %get-tuple-element.40.blocks_ref, f32[2048,128]{1,0:T(8,128)S(1)} %get-tuple-element.41.base_ref), custom_call_target="tpu_custom_call" | custom-call | flops 1024 | bytes 1024 | tf_op jit(solution)/shard_map/pallas_call | solution.py:200
  59.2 1.6 %shard_map.88.base_ref = f32[2048,128]{1,0:T(8,128)S(1)} custom-call(s32[1]{0:T(128)} %bitcast.me_ref, s32[2048,1]{1,0:T(8,128)S(1)} %copy.12.owner_ref, bf16[2048,256]{1,0:T(8,128)(2,1)S(1)} %copy-done, bf16[4,256,128]{2,1,0:T(8,128)(2,1)S(1)} %get-tuple-element.38.blocks_ref, f32[2048,128]{1,0:T(8,128)S(1)} %get-tuple-element.42.base_ref), custom_call_target="tpu_custom_call" | custom-call | flops 1024 | bytes 1024 | tf_op jit(solution)/shard_map/pallas_call | solution.py:200
  60.9 3.8 %collective-permute-done.17.blocks_ref = bf16[4,256,128]{2,1,0:T(8,128)(2,1)S(1)} collective-permute-done((bf16[4,256,128]{2,1,0:T(8,128)(2,1)S(1)}, bf16[4,256,128]{2,1,0:T(8,128)(2,1)S(1)}, u32[]{:S(2)}, u32[]{:S(2)}) %collective-permute-start.17) | collective-permute-done | bytes 262176 | tf_op jit(solution)/shard_map/ppermute | solution.py:35
  64.7 1.6 %shard_map.90.rest_0_ = bf16[2048,128]{1,0:T(8,128)(2,1)S(1)} custom-call(s32[1]{0:T(128)} %bitcast.me_ref, s32[2048,1]{1,0:T(8,128)S(1)} %copy.12.owner_ref, bf16[2048,256]{1,0:T(8,128)(2,1)S(1)} %copy-done, bf16[4,256,128]{2,1,0:T(8,128)(2,1)S(1)} %collective-permute-done.17.blocks_ref, f32[2048,128]{1,0:T(8,128)S(1)} %shard_map.89.base_ref), custom_call_target="tpu_custom_call" | custom-call | flops 1024 | bytes 1024 | tf_op jit(solution)/shard_map/pallas_call | solution.py:200
  66.3 1.9 %collective-permute-done.16.blocks_ref = bf16[4,256,128]{2,1,0:T(8,128)(2,1)S(1)} collective-permute-done((bf16[4,256,128]{2,1,0:T(8,128)(2,1)S(1)}, bf16[4,256,128]{2,1,0:T(8,128)(2,1)S(1)}, u32[]{:S(2)}, u32[]{:S(2)}) %collective-permute-start.16) | collective-permute-done | bytes 262176 | tf_op jit(solution)/shard_map/ppermute | solution.py:35
  68.2 2.3 %shard_map.91 = bf16[2048,256]{1,0:T(8,128)(2,1)} custom-call(s32[1]{0:T(128)} %bitcast.me_ref, s32[2048,1]{1,0:T(8,128)S(1)} %copy.12.owner_ref, bf16[2048,256]{1,0:T(8,128)(2,1)S(1)} %copy-done, bf16[4,256,128]{2,1,0:T(8,128)(2,1)S(1)} %collective-permute-done.16.blocks_ref, f32[2048,128]{1,0:T(8,128)S(1)} %shard_map.88.base_ref, ...), custom_call_target="tpu_custom_call" | custom-call | flops 1024 | bytes 1024 | tf_op jit(solution)/shard_map/pallas_call | solution.py:235
  (45 shorter events, 1.5 us)
Async XLA Ops:
  3.6 6.1 %copy-start.5 = (bf16[1,3,64,512]{3,2,1,0:T(8,128)(2,1)S(1)}, bf16[1,3,64,512]{3,2,1,0:T(8,128)(2,1)}, u32[]{:S(2)}) copy-start(bf16[1,3,64,512]{3,2,1,0:T(8,128)(2,1)} %param.12) | copy-start | bytes 589828
  3.6 10.4 %copy-start.7 = (bf16[2,256,256]{2,1,0:T(8,128)(2,1)S(1)}, bf16[2,256,256]{2,1,0:T(8,128)(2,1)}, u32[]{:S(2)}) copy-start(bf16[2,256,256]{2,1,0:T(8,128)(2,1)} %get-tuple-element.28) | copy-start | bytes 786436
  3.6 10.9 %copy-start.6 = (s32[2048,1]{0,1:T(1,128)S(1)}, s32[2048,1]{0,1:T(1,128)}, u32[]{:S(2)}) copy-start(s32[2048,1]{0,1:T(1,128)} %param.9) | copy-start | bytes 24580
  3.6 14.4 %collective-permute-start.1 = (bf16[2,256,256]{2,1,0:T(8,128)(2,1)}, bf16[2,256,256]{2,1,0:T(8,128)(2,1)S(1)}, u32[]{:S(2)}, u32[]{:S(2)}) collective-permute-start(bf16[2,256,256]{2,1,0:T(8,128)(2,1)} %get-tuple-element.30), channel_id=1, source_target_pairs={{0,4},{4,0},{8,12},{12,8},{16,20},{20,16},{24,28},{28,24},{1,5},{5... | collective-permute-start | bytes 786440 | tf_op jit(solution)/shard_map/ppermute | solution.py:35
  9.7 9.5 %collective-permute-start.3 = (bf16[64,512]{1,0:T(8,128)(2,1)S(1)}, bf16[64,512]{1,0:T(8,128)(2,1)S(1)}, u32[]{:S(2)}, u32[]{:S(2)}) collective-permute-start(bf16[64,512]{1,0:T(8,128)(2,1)S(1)} %get-tuple-element.48.refs_0_), channel_id=1, source_target_pairs={{0,2},{1,3},{2,0},{3,1},{4,6},{5,7},{6,4},{7,5},{8,10},{9,11},{10,... | collective-permute-start | bytes 196616 | tf_op jit(solution)/shard_map/ppermute | solution.py:35
  11.3 8.5 %collective-permute-start.2 = (bf16[2,64,512]{2,1,0:T(8,128)(2,1)S(1)}, bf16[2,64,512]{2,1,0:T(8,128)(2,1)S(1)}, u32[]{:S(2)}, u32[]{:S(2)}) collective-permute-start(bf16[2,64,512]{2,1,0:T(8,128)(2,1)S(1)} %get-tuple-element.50), channel_id=1, source_target_pairs={{0,16},{4,20},{8,24},{12,28},{16,0},{20,4},{24,8},{28,12},{1,17},{... | collective-permute-start | bytes 393224 | tf_op jit(solution)/shard_map/ppermute | solution.py:35
  14.0 7.2 %collective-permute-start = (bf16[2,256,256]{2,1,0:T(8,128)(2,1)S(1)}, bf16[2,256,256]{2,1,0:T(8,128)(2,1)S(1)}, u32[]{:S(2)}, u32[]{:S(2)}) collective-permute-start(bf16[2,256,256]{2,1,0:T(8,128)(2,1)S(1)} %copy-done.7), channel_id=1, source_target_pairs={{0,4},{4,0},{8,12},{12,8},{16,20},{20,16},{24,28},{28,24},{1,5},{5... | collective-permute-start | bytes 786440 | tf_op jit(solution)/shard_map/ppermute | solution.py:35
  18.0 3.2 %copy-start.4 = (f32[2,256,256]{2,1,0:T(8,128)S(1)}, f32[2,256,256]{2,1,0:T(8,128)}, u32[]{:S(2)}) copy-start(f32[2,256,256]{2,1,0:T(8,128)} %shard_map.83) | copy-start | bytes 1572868
  19.8 12.8 %collective-permute-start.4 = (bf16[2,2,64,512]{3,2,1,0:T(8,128)(2,1)S(1)}, bf16[2,2,64,512]{3,2,1,0:T(8,128)(2,1)S(1)}, u32[]{:S(2)}, u32[]{:S(2)}) collective-permute-start(bf16[2,2,64,512]{3,2,1,0:T(8,128)(2,1)S(1)} %pad_maximum_fusion.1), channel_id=1, source_target_pairs={{0,8},{4,12},{8,0},{12,4},{16,24},{20,28},{24,16},{28,20},{1,9},{5... | collective-permute-start | bytes 786440 | tf_op jit(solution)/shard_map/ppermute | solution.py:35
  21.3 25.1 %copy-start.1 = (bf16[2048,256]{1,0:T(8,128)(2,1)S(1)}, bf16[2048,256]{1,0:T(8,128)(2,1)}, u32[]{:S(2)}) copy-start(bf16[2048,256]{1,0:T(8,128)(2,1)} %fields_ref) | copy-start | bytes 3145732
  21.3 25.0 %copy-start.2 = (s32[8,7]{1,0:T(8,128)S(1)}, s32[8,7]{1,0:T(8,128)}, u32[]{:S(2)}) copy-start(s32[8,7]{1,0:T(8,128)} %index_ref.1) | copy-start | bytes 676
  21.3 25.0 %copy-start.3 = (s32[8]{0:T(128)S(1)}, s32[8]{0:T(128)}, u32[]{:S(2)}) copy-start(s32[8]{0:T(128)} %count_ref.1) | copy-start | bytes 100
  21.3 12.1 %collective-permute-start.7 = (bf16[256,256]{1,0:T(8,128)(2,1)S(1)}, bf16[256,256]{1,0:T(8,128)(2,1)S(1)}, u32[]{:S(2)}, u32[]{:S(2)}) collective-permute-start(bf16[256,256]{1,0:T(8,128)(2,1)S(1)} %get-tuple-element.43), channel_id=1, source_target_pairs={{0,24},{4,28},{8,16},{12,20},{16,8},{20,12},{24,0},{28,4},{1,25},{... | collective-permute-start | bytes 393224 | tf_op jit(solution)/shard_map/ppermute | solution.py:35
  23.6 11.8 %collective-permute-start.8 = (bf16[256,256]{1,0:T(8,128)(2,1)S(1)}, bf16[256,256]{1,0:T(8,128)(2,1)S(1)}, u32[]{:S(2)}, u32[]{:S(2)}) collective-permute-start(bf16[256,256]{1,0:T(8,128)(2,1)S(1)} %get-tuple-element.44), channel_id=1, source_target_pairs={{0,16},{4,20},{8,24},{12,28},{16,0},{20,4},{24,8},{28,12},{1,17},{... | collective-permute-start | bytes 393224 | tf_op jit(solution)/shard_map/ppermute | solution.py:35
  24.4 11.0 %collective-permute-start.9 = (bf16[256,256]{1,0:T(8,128)(2,1)S(1)}, bf16[256,256]{1,0:T(8,128)(2,1)S(1)}, u32[]{:S(2)}, u32[]{:S(2)}) collective-permute-start(bf16[256,256]{1,0:T(8,128)(2,1)S(1)} %fusion.1), channel_id=1, source_target_pairs={{0,8},{4,12},{8,0},{12,4},{16,24},{20,28},{24,16},{28,20},{1,9},{5... | collective-permute-start | bytes 393224 | tf_op jit(solution)/shard_map/ppermute | solution.py:35
  32.8 13.0 %collective-permute-start.11 = (bf16[4,2,64,512]{3,2,1,0:T(8,128)(2,1)S(1)}, bf16[4,2,64,512]{3,2,1,0:T(8,128)(2,1)S(1)}, u32[]{:S(2)}, u32[]{:S(2)}) collective-permute-start(bf16[4,2,64,512]{3,2,1,0:T(8,128)(2,1)S(1)} %pad_maximum_fusion.refs_0_), channel_id=1, source_target_pairs={{0,2},{1,3},{2,0},{3,1},{4,6},{5,7},{6,4},{7,5},{8,10},{9,11},{10,... | collective-permute-start | bytes 1572872 | tf_op jit(solution)/shard_map/ppermute | solution.py:35
  33.3 3.0 %collective-permute-start.6 = (bf16[2,64,512]{2,1,0:T(8,128)(2,1)S(1)}, bf16[2,64,512]{2,1,0:T(8,128)(2,1)S(1)}, u32[]{:S(2)}, u32[]{:S(2)}) collective-permute-start(bf16[2,64,512]{2,1,0:T(8,128)(2,1)S(1)} %pad_maximum_fusion.2), channel_id=1, source_target_pairs={{0,1},{1,0},{2,3},{3,2},{4,5},{5,4},{6,7},{7,6},{8,9},{9,8},{10,11... | collective-permute-start | bytes 393224 | tf_op jit(solution)/shard_map/ppermute | solution.py:35
  35.5 5.0 %collective-permute-start.10 = (bf16[256,256]{1,0:T(8,128)(2,1)S(1)}, bf16[256,256]{1,0:T(8,128)(2,1)S(1)}, u32[]{:S(2)}, u32[]{:S(2)}) collective-permute-start(bf16[256,256]{1,0:T(8,128)(2,1)S(1)} %add_convert_fusion.refs_4_), channel_id=1, source_target_pairs={{0,4},{4,0},{8,12},{12,8},{16,20},{20,16},{24,28},{28,24},{1,5},{5... | collective-permute-start | bytes 393224 | tf_op jit(solution)/shard_map/ppermute | solution.py:35
  40.8 12.4 %collective-permute-start.13 = (bf16[256,256]{1,0:T(8,128)(2,1)S(1)}, bf16[256,256]{1,0:T(8,128)(2,1)S(1)}, u32[]{:S(2)}, u32[]{:S(2)}) collective-permute-start(bf16[256,256]{1,0:T(8,128)(2,1)S(1)} %shard_map.85.refs_4_), channel_id=1, source_target_pairs={{0,8},{4,12},{8,0},{12,4},{16,24},{20,28},{24,16},{28,20},{1,9},{5... | collective-permute-start | bytes 393224 | tf_op jit(solution)/shard_map/ppermute | solution.py:35
  42.5 11.9 %collective-permute-start.14 = (bf16[256,256]{1,0:T(8,128)(2,1)S(1)}, bf16[256,256]{1,0:T(8,128)(2,1)S(1)}, u32[]{:S(2)}, u32[]{:S(2)}) collective-permute-start(bf16[256,256]{1,0:T(8,128)(2,1)S(1)} %shard_map.85.refs_4_), channel_id=1, source_target_pairs={{0,16},{4,20},{8,24},{12,28},{16,0},{20,4},{24,8},{28,12},{1,17},{... | collective-permute-start | bytes 393224 | tf_op jit(solution)/shard_map/ppermute | solution.py:35
  45.8 8.6 %collective-permute-start.15 = (bf16[256,256]{1,0:T(8,128)(2,1)S(1)}, bf16[256,256]{1,0:T(8,128)(2,1)S(1)}, u32[]{:S(2)}, u32[]{:S(2)}) collective-permute-start(bf16[256,256]{1,0:T(8,128)(2,1)S(1)} %shard_map.85.refs_4_), channel_id=1, source_target_pairs={{0,24},{4,28},{8,16},{12,20},{16,8},{20,12},{24,0},{28,4},{1,25},{... | collective-permute-start | bytes 393224 | tf_op jit(solution)/shard_map/ppermute | solution.py:35
  45.8 8.6 %collective-permute-start.5 = (bf16[4,2,64,512]{3,2,1,0:T(8,128)(2,1)S(1)}, bf16[4,2,64,512]{3,2,1,0:T(8,128)(2,1)S(1)}, u32[]{:S(2)}, u32[]{:S(2)}) collective-permute-start(bf16[4,2,64,512]{3,2,1,0:T(8,128)(2,1)S(1)} %pad_maximum_fusion.refs_0_), channel_id=1, source_target_pairs={{0,1},{1,0},{2,3},{3,2},{4,5},{5,4},{6,7},{7,6},{8,9},{9,8},{10,11... | collective-permute-start | bytes 1572872 | tf_op jit(solution)/shard_map/ppermute | solution.py:35
  45.8 8.6 %collective-permute-start.12 = (bf16[4,2,64,512]{3,2,1,0:T(8,128)(2,1)S(1)}, bf16[4,2,64,512]{3,2,1,0:T(8,128)(2,1)S(1)}, u32[]{:S(2)}, u32[]{:S(2)}) collective-permute-start(bf16[4,2,64,512]{3,2,1,0:T(8,128)(2,1)S(1)} %collective-permute-done.11.refs_2_), channel_id=1, source_target_pairs={{0,1},{1,0},{2,3},{3,2},{4,5},{5,4},{6,7},{7,6},{8,9},{9,8},{10,11... | collective-permute-start | bytes 1572872 | tf_op jit(solution)/shard_map/ppermute | solution.py:35
  55.4 9.3 %collective-permute-start.17 = (bf16[4,256,128]{2,1,0:T(8,128)(2,1)S(1)}, bf16[4,256,128]{2,1,0:T(8,128)(2,1)S(1)}, u32[]{:S(2)}, u32[]{:S(2)}) collective-permute-start(bf16[4,256,128]{2,1,0:T(8,128)(2,1)S(1)} %get-tuple-element.40.blocks_ref), channel_id=1, source_target_pairs={{0,4},{4,0},{8,12},{12,8},{16,20},{20,16},{24,28},{28,24},{1,5},{5... | collective-permute-start | bytes 786440 | tf_op jit(solution)/shard_map/ppermute | solution.py:35
  56.0 1.6 %copy-start = (bf16[2048,256]{1,0:T(8,128)(2,1)S(1)}, bf16[2048,256]{1,0:T(8,128)(2,1)}, u32[]{:S(2)}) copy-start(bf16[2048,256]{1,0:T(8,128)(2,1)} %basis_ref.7) | copy-start | bytes 3145732
  56.0 12.2 %collective-permute-start.16 = (bf16[4,256,128]{2,1,0:T(8,128)(2,1)S(1)}, bf16[4,256,128]{2,1,0:T(8,128)(2,1)S(1)}, u32[]{:S(2)}, u32[]{:S(2)}) collective-permute-start(bf16[4,256,128]{2,1,0:T(8,128)(2,1)S(1)} %get-tuple-element.38.blocks_ref), channel_id=1, source_target_pairs={{0,4},{4,0},{8,12},{12,8},{16,20},{20,16},{24,28},{28,24},{1,5},{5... | collective-permute-start | bytes 786440 | tf_op jit(solution)/shard_map/ppermute | solution.py:35

commit v3 on v0

v3 whole, which is shorter than its diff:
```python
import functools

import jax
import jax.numpy as jnp
from jax import lax
from jax.experimental import pallas as pl
from jax.experimental.pallas import tpu as pltpu
from jax.sharding import PartitionSpec as P

F32 = jnp.float32
BF16 = jnp.bfloat16
VMEM_LIMIT = 16 * 1024 * 1024
VMEM = pl.BlockSpec(memory_space=pltpu.VMEM)
SMEM = pl.BlockSpec(memory_space=pltpu.SMEM)
HBM = pl.BlockSpec(memory_space=pltpu.HBM)
ANY = pl.BlockSpec(memory_space=pl.ANY)


def call(kernel, out_shape, values, in_specs, out_spaces, scratch=(), after=()):
    def placed(value, spec):
        space = spec.memory_space
        pinned = space in (pltpu.VMEM, pltpu.HBM)
        return pltpu.with_memory_space_constraint(value, space) if pinned else value

    return pl.pallas_call(
        kernel,
        out_shape=[space(s.shape, s.dtype) for s, space in zip(out_shape, out_spaces)],
        in_specs=list(in_specs) + [ANY if v.ndim > 1 else SMEM for v in after],
        out_specs=[pl.BlockSpec(memory_space=space) for space in out_spaces],
        scratch_shapes=list(scratch),
        compiler_params=pltpu.CompilerParams(vmem_limit_bytes=VMEM_LIMIT),
        cost_estimate=pl.CostEstimate(flops=1024, bytes_accessed=1024, transcendentals=0),
    )(*[placed(v, s) for v, s in zip(values, in_specs)], *after)


def tie(*values):
    return lax.optimization_barrier(values)


def swapped(value, axis, mask):
    return lax.ppermute(value, axis, [(i, i ^ mask) for i in range(lax.axis_size(axis))])


def products(relative, basis_t, fields, groups, outs):
    for out, group in zip(outs, groups):
        for i, j in enumerate(group):
            masked = jnp.where(relative == j, basis_t, jnp.zeros((), BF16))
            out[i] = jnp.dot(masked, fields, preferred_element_type=F32).astype(out.dtype)


def staged_compress_kernel(groups, me_ref, owner_hbm, basis_hbm, fields_hbm, *rest):
    rest = rest[-len(groups) - 4 :]
    outs, (owner_ref, basis_ref, fields_ref, sems) = rest[: len(groups)], rest[len(groups) :]
    pairs = ((owner_hbm, owner_ref), (basis_hbm, basis_ref), (fields_hbm, fields_ref))
    copies = [
        pltpu.make_async_copy(source, target, sems.at[k]) for k, (source, target) in enumerate(pairs)
    ]
    for copy in copies:
        copy.start()
    copies[0].wait()
    relative = owner_ref[...] ^ me_ref[0]
    copies[1].wait()
    basis_t = basis_ref[...].T
    copies[2].wait()
    products(relative, basis_t, fields_ref[...], groups, outs)


def compress_kernel(groups, me_ref, owner_ref, basis_ref, fields_ref, *rest):
    outs = rest[-len(groups) :]
    products(owner_ref[...] ^ me_ref[0], basis_ref[...].T, fields_ref[...], groups, outs)


def compress(me, owner_row, basis, fields, groups, dtype, staged, after=()):
    rows, cols = fields.shape
    width = basis.shape[1]
    held = [
        pltpu.VMEM((1, rows), jnp.int32),
        pltpu.VMEM((rows, width), BF16),
        pltpu.VMEM((rows, cols), BF16),
        pltpu.SemaphoreType.DMA((3,)),
    ]
    return list(
        call(
            functools.partial(staged_compress_kernel if staged else compress_kernel, groups),
            [jax.ShapeDtypeStruct((len(g), width, cols), dtype) for g in groups],
            (me, owner_row, basis, fields),
            [SMEM] + [HBM if staged else VMEM] * 3,
            [pltpu.VMEM] * len(groups),
            held if staged else (),
            after,
        )
    )


def near_kernel(first, index_ref, count_ref, blocks_hbm, fields_ref, *rest):
    near_ref, blocks_ref, sems = rest[-3:]
    groups, slots, size, _ = blocks_ref.shape
    copies = [
        pltpu.make_async_copy(blocks_hbm.at[first + g], blocks_ref.at[g], sems.at[g])
        for g in range(groups)
    ]
    for copy in copies:
        copy.start()
    for g, copy in enumerate(copies):
        chosen = []
        for j in range(slots):
            start = pl.multiple_of(index_ref[first + g, j] * size, size)
            piece = fields_ref[pl.ds(start, size), :]
            live = j < count_ref[first + g]
            chosen.append(jnp.where(live, piece, jnp.zeros_like(piece)))
        copy.wait()
        weights = jnp.concatenate([blocks_ref[g, j] for j in range(slots)], axis=1)
        near_ref[g * size : (g + 1) * size, :] = jnp.dot(
            weights, jnp.concatenate(chosen, axis=0), preferred_element_type=F32
        )


def near_field(near_index, near_count, near_blocks, fields, first, groups, after):
    _, slots, size, _ = near_blocks.shape
    (near,) = call(
        functools.partial(near_kernel, first),
        [jax.ShapeDtypeStruct((groups * size, fields.shape[1]), F32)],
        (near_index, near_count, near_blocks, fields),
        [SMEM, SMEM, HBM, VMEM],
        [pltpu.VMEM],
        [pltpu.VMEM((groups, slots, size, size), BF16), pltpu.SemaphoreType.DMA((groups,))],
        after,
    )
    return near


def apply_rows(me, pieces, stacked, out):
    product = jnp.dot(jnp.concatenate(pieces, axis=0), stacked, preferred_element_type=F32)
    size = pieces[0].shape[0]
    for o in range(len(pieces)):
        start = pl.multiple_of((me ^ o) * size, size)
        out[pl.ds(start, size), :] = product[o * size : (o + 1) * size].astype(out.dtype)


def level_kernel(n_rhs, n_out, level, me_ref, *refs):
    rows, (own_ref, other_ref), outs = refs[: n_rhs * n_out], refs[-2 - n_out : -n_out], refs[-n_out:]
    own, other = own_ref[...], other_ref[...]
    for k, out in enumerate(outs):
        pieces = [ref[level] if k == 0 else ref[...] for ref in rows[k * n_rhs :][:n_rhs]]
        stacked = jnp.concatenate([other, own] if k else [own, other], axis=0)
        apply_rows(me_ref[0], pieces, stacked, out)


def next_level(rhs_me, level, rows, own, other, other_rows=()):
    n_out = 2 if other_rows else 1
    return call(
        functools.partial(level_kernel, len(rows), n_out, level),
        [jax.ShapeDtypeStruct(own.shape, BF16)] * n_out,
        (rhs_me, *rows, *other_rows, own, other),
        [SMEM] + [VMEM] * (len(rows) * n_out + 2),
        [pltpu.VMEM] * n_out,
    )


def far_tile(ids, me_ref, owner_ref, basis_ref, bases, blocks, start, tile):
    part = pl.ds(start, tile)
    rows = bases[0].shape[0]
    base = bases[start // rows][pl.ds(start % rows, tile), :]
    relative = owner_ref[part, :] ^ me_ref[0]
    basis = basis_ref[part, :]
    masked = [jnp.where(relative == j, basis, jnp.zeros((), BF16)) for j in ids]
    stacked = [ref[...] for ref in blocks]
    total = jnp.dot(
        jnp.concatenate(masked, axis=1),
        jnp.concatenate(stacked, axis=0),
        preferred_element_type=F32,
    )
    return total.astype(BF16).astype(F32) + base


def far_kernel(ids, tile, n_base, me_ref, owner_ref, basis_ref, *refs):
    bases, blocks, out_ref = refs[:n_base], refs[n_base:-1], refs[-1]
    for start in range(0, out_ref.shape[0], tile):
        value = far_tile(ids, me_ref, owner_ref, basis_ref, bases, blocks, start, tile)
        out_ref[pl.ds(start, tile), :] = value


def last_far_kernel(ids, tile, n_base, me_ref, owner_ref, basis_ref, *refs):
    bases, blocks, (out_hbm, held_ref, sems) = refs[:n_base], refs[n_base:-3], refs[-3:]
    copies = []
    for t in range(out_hbm.shape[0] // tile):
        value = far_tile(ids, me_ref, owner_ref, basis_ref, bases, blocks, t * tile, tile)
        part = pl.ds(t * tile, tile)
        held_ref[part, :] = value.astype(BF16)
        copies.append(pltpu.make_async_copy(held_ref.at[part], out_hbm.at[part], sems.at[t]))
        copies[-1].start()
    for copy in copies:
        copy.wait()


def far_field(ids, me, owner, basis, bases, blocks, last=False):
    rows, cols = basis.shape[0], bases[0].shape[1]
    tile = min(bases[0].shape[0], 512)
    held = [pltpu.VMEM((rows, cols), BF16), pltpu.SemaphoreType.DMA((rows // tile,))]
    (out,) = call(
        functools.partial(last_far_kernel if last else far_kernel, ids, tile, len(bases)),
        [jax.ShapeDtypeStruct((rows, cols), BF16 if last else F32)],
        (me, owner, basis, *bases, *blocks),
        [SMEM] + [VMEM] * (2 + len(bases) + len(blocks)),
        [pltpu.HBM if last else pltpu.VMEM],
        held if last else (),
    )
    return out


def across(pieces, mask):
    while mask:
        pieces = pieces | {o ^ mask: swapped(v, "rhs", mask) for o, v in pieces.items()}
        mask //= 2
    return pieces


def on_device(
    fields, owner, source_basis, field_basis, transfer, near_blocks, near_index, near_count
):
    n_leaf = lax.axis_size("leaf")
    rows, cols = fields.shape
    levels = transfer.shape[1]
    group = 2**levels
    outer = n_leaf // group
    upper = group // 2
    n_rhs = lax.axis_size("rhs")
    me = lax.axis_index("leaf").astype(jnp.int32)[None]
    rhs_me = lax.axis_index("rhs").astype(jnp.int32)[None]
    owner_row = owner.reshape(1, rows)

    parts = [list(range(upper - 1, 0, -1)), [0]]

    def groups(low):
        return [[o * group + 2 * s + low for s in part for o in range(outer)] for part in parts]

    send = compress(me, owner_row, source_basis, fields, groups(1), BF16, True, [rhs_me])

    fields, send[0], send[1] = tie(fields, *send)
    got = [swapped(s, "leaf", 1) for s in send]
    keep = compress(me, owner_row, source_basis, fields, groups(0)[:1], F32, False)

    def reduced(keep, got, part):
        total = keep + got.astype(F32)
        sums = []
        for i in range(len(part)):
            mine = total[i * outer]
            for o in range(1, outer):
                piece = total[i * outer + o].astype(BF16)
                mine = mine + swapped(piece, "leaf", o * group).astype(F32)
            sums.append(mine)
        return sums

    transfer, keep[0] = tie(transfer, keep[0])
    top = group // 2
    far_rhs = n_rhs // 2
    mine_rows = {0: transfer[0]}
    mine_rows[far_rhs] = swapped(mine_rows[0], "rhs", far_rhs)
    their_rows = {0: swapped(transfer[0, -1], "leaf", top)}
    got[0], mine_rows[far_rhs], their_rows[0] = tie(got[0], mine_rows[far_rhs], their_rows[0])

    sums = [v.astype(BF16) for v in reduced(keep[0], got[0], parts[0])]
    arrived = [swapped(v, "leaf", 2 * s) for s, v in zip(parts[0], sums)]
    keep += compress(me, owner_row, source_basis, fields, groups(0)[1:], F32, False, sums[:1])
    (total,) = reduced(keep[1], got[1], parts[1])
    half = near_blocks.shape[0] // 2
    near = [near_field(near_index, near_count, near_blocks, fields, 0, half, sums[:1])]
    mine_rows = across(mine_rows, far_rhs // 2)
    order = sorted(mine_rows)
    total, near[0] = tie(total, near[0])

    for value in arrived:
        total = total + value.astype(F32)
    coefficients = total.astype(BF16)
    for level in range(levels - 1):
        other = swapped(coefficients, "leaf", 2**level)
        if level == 0:
            their_rows[far_rhs] = swapped(their_rows[0], "rhs", far_rhs)
            coefficients, their_rows[far_rhs] = tie(coefficients, their_rows[far_rhs])
        if level == 1:
            their_rows = across(their_rows, far_rhs // 2)
            coefficients, *values = tie(coefficients, *[their_rows[o] for o in order])
            their_rows = dict(zip(order, values))
        rows = [mine_rows[o] for o in order]
        (coefficients,) = next_level(rhs_me, level, rows, coefficients, other)
    other = swapped(coefficients, "leaf", top)
    near.append(near_field(near_index, near_count, near_blocks, fields, half, half, [coefficients]))
    near[1], coefficients = tie(near[1], coefficients)
    rows = [mine_rows[o] for o in order]
    own = next_level(
        rhs_me, levels - 1, rows, coefficients, other, [their_rows[o] for o in order]
    )

    def add_far(base, known, last=False):
        ids = [o * group + j for j in sorted(known) for o in range(outer)]
        blocks = []
        for j in sorted(known):
            blocks += [known[j]] + [swapped(known[j], "leaf", o * group) for o in range(1, outer)]
        return far_field(ids, me, owner, field_basis, base, blocks, last)

    known = {0: own[0], top: own[1]}
    steps = [1 << k for k in range(levels - 1)]
    total = near
    low, high = steps
    from_low = {j ^ low: swapped(v, "leaf", low) for j, v in known.items()}
    from_high = {j ^ high: swapped(v, "leaf", high) for j, v in known.items()}
    total = [add_far(total, known)]
    total[0], from_high[high], from_low[top ^ low] = tie(
        total[0], from_high[high], from_low[top ^ low]
    )
    rest = {
        low ^ high: swapped(from_high[high], "leaf", low),
        top ^ low ^ high: swapped(from_low[top ^ low], "leaf", high),
    }
    total = [add_far(total, from_low | from_high)]
    return add_far(total, rest, True)


def solution(mesh):
    in_specs = (
        P("leaf", "rhs"),
        P("leaf", None),
        P("leaf", None),
        P("leaf", None),
        P("leaf", None, "rhs", None),
        P("leaf", None, None, None),
        P("leaf", None),
        P("leaf"),
    )
    out_specs = P("leaf", "rhs")
    return jax.shard_map(
        on_device, mesh=mesh, in_specs=in_specs, out_specs=out_specs, check_vma=False
    )
```

time: 194 us -> 64 us (0.33)
  waiting for transfers between devices: 86.8 us -> 16.9 us
  local copies, waits for them, and re-layouts: 47.5 us -> 2.61 us
  starting transfers between devices: 3.36 us -> 24.3 us
  Pallas kernels: 0 us -> 19.6 us
  blocking collectives: 17.3 us -> 0 us
  matrix products: 16 us -> 0 us
  between operations: 13.5 us -> 0.2 us
  other arithmetic: 8.52 us -> 0.24 us
    reduce_scatter x1 -> x0, waiting for transfers between devices: 70.9 us -> none  [on_device(): lax.psum_scatter(jnp.einsum('bck,bcn->bkn', v_three, x_three, preferred_e...]
    scatter x3 -> x0, local copies, waits for them, and re-layouts: 32.9 us -> none  [the longest x2 22.5 us: on_device(): jnp.zeros((n_leaf * capacity, basis_width), jnp.bfloat16).at[slot_index]]
    ppermute x3 -> x21, starting transfers between devices: 3.32 us -> 24.3 us  [swapped(): lax.ppermute(value, axis, [(i, i ^ mask) for i in range(lax.axis_size(axi...]
    pallas_call x0 -> x11, Pallas kernels: none -> 19.6 us  [call(): pl.pallas_call(kernel, out_shape=[space(s.shape, s.dtype) for s, space in...]
    all_gather x3 -> x0, blocking collectives: 17.3 us -> none  [on_device(): lax.all_gather(transfer[0, level_num], 'rhs', axis=0, tiled=True)]
    dot_general x6 -> x0, matrix products: 16 us -> none  [the longest x1 8.62 us: on_device(): jnp.einsum('gjab,gjbn->gan', near_blocks, chosen, preferred_element_type=...]
    ppermute x3 -> x21, waiting for transfers between devices: 2.56 us -> 16.9 us  [swapped(): lax.ppermute(value, axis, [(i, i ^ mask) for i in range(lax.axis_size(axi...]
    all_gather x1 -> x0, waiting for transfers between devices: 13.3 us -> none  [on_device(): lax.all_gather(coefficients[None], 'leaf', axis=0, tiled=True)]
  transfers between devices with their start and end apart: 5 -> 21, of which waited for: 3 -> 11; matrix products, arithmetic and copies ran while one was open for 13% -> 1% of each run, Pallas kernels for 0% -> 21%
where the time goes in v3:
time: 64 us; the launch traced here: 63.8 us
  starting transfers between devices  24.3 us (38%)
  Pallas kernels  19.6 us (31%)
  waiting for transfers between devices  16.9 us (26%)
  local copies, waits for them, and re-layouts  2.61 us (4%)
    ppermute x21, starting transfers between devices, swapped(): lax.ppermute(value, axis, [(i, i ^ mask) for i in range(lax.axis_size(axi...  24.3 us
    pallas_call x11, Pallas kernels, call(): pl.pallas_call(kernel, out_shape=[space(s.shape, s.dtype) for s, space in...  19.6 us
    ppermute x21, waiting for transfers between devices, swapped(): lax.ppermute(value, axis, [(i, i ^ mask) for i in range(lax.axis_size(axi...  16.9 us
    unnamed x19, local copies, waits for them, and re-layouts  2.58 us
  transfers between devices with their start and end apart: 21, of which 11 were waited for; matrix products, arithmetic and copies ran while one was open for 1% of the time, Pallas kernels for 21%

profile of v3, /device:TPU:0, one launch (start us, length us, event | category | flops | bytes accessed | tf_op | source)
XLA Modules:
  0.0 63.8 jit_solution(5799486810077099045)
XLA Ops:
  0.0 3.0 %shard_map.82 = (bf16[3,256,256]{2,1,0:T(8,128)(2,1)S(1)}, bf16[1,256,256]{2,1,0:T(8,128)(2,1)S(1)}) custom-call(s32[1]{0:T(128)} %bitcast.me_ref, s32[1,2048]{1,0:T(1,128)} %bitcast.19, bf16[2048,256]{1,0:T(8,128)(2,1)} %basis_ref.6, bf16[2048,256]{1,0:T(8,128)(2,1)} %fields_ref.3, s32[1]{0:T(128)} %bitcast.2.rest_0_.me_ref), custom_call_target="tpu_custom_call" | custom-call | flops 1024 | bytes 1024 | tf_op jit(solution)/shard_map/pallas_call | solution.py:25
  3.0 3.0 %collective-permute-start = (bf16[3,256,256]{2,1,0:T(8,128)(2,1)S(1)}, bf16[3,256,256]{2,1,0:T(8,128)(2,1)S(1)}, u32[]{:S(2)}, u32[]{:S(2)}) collective-permute-start(bf16[3,256,256]{2,1,0:T(8,128)(2,1)S(1)} %get-tuple-element.35), channel_id=1, source_target_pairs={{0,4},{4,0},{8,12},{12,8},{16,20},{20,16},{24,28},{28,24},{1,5},{5... | collective-permute-start | bytes 1179656 | tf_op jit(solution)/shard_map/ppermute | solution.py:41
  6.0 1.0 %shard_map.83 = f32[3,256,256]{2,1,0:T(8,128)S(1)} custom-call(s32[1]{0:T(128)} %bitcast.me_ref, s32[1,2048]{1,0:T(1,128)S(1)} %bitcast.20, bf16[2048,256]{1,0:T(8,128)(2,1)S(1)} %copy-done.1, bf16[2048,256]{1,0:T(8,128)(2,1)S(1)} %copy-done), custom_call_target="tpu_custom_call" | custom-call | flops 1024 | bytes 1024 | tf_op jit(solution)/shard_map/pallas_call | solution.py:25
  7.1 1.6 %collective-permute-start.1 = (bf16[3,64,512]{2,1,0:T(8,128)(2,1)S(1)}, bf16[3,64,512]{2,1,0:T(8,128)(2,1)S(1)}, u32[]{:S(2)}, u32[]{:S(2)}) collective-permute-start(bf16[3,64,512]{2,1,0:T(8,128)(2,1)S(1)} %bitcast.14), channel_id=1, source_target_pairs={{0,2},{1,3},{2,0},{3,1},{4,6},{5,7},{6,4},{7,5},{8,10},{9,11},{10,... | collective-permute-start | bytes 589832 | tf_op jit(solution)/shard_map/ppermute | solution.py:41
  8.7 2.7 %collective-permute-start.2 = (bf16[64,512]{1,0:T(8,128)(2,1)S(1)}, bf16[64,512]{1,0:T(8,128)(2,1)S(1)}, u32[]{:S(2)}, u32[]{:S(2)}) collective-permute-start(bf16[64,512]{1,0:T(8,128)(2,1)S(1)} %slice_bitcast_fusion.3), channel_id=1, source_target_pairs={{0,16},{4,20},{8,24},{12,28},{16,0},{20,4},{24,8},{28,12},{1,17},{... | collective-permute-start | bytes 196616 | tf_op jit(solution)/shard_map/ppermute | solution.py:41
  11.3 0.5 collective-permute-start.3
  11.9 2.1 %collective-permute-done.2.refs_4_ = bf16[64,512]{1,0:T(8,128)(2,1)S(1)} collective-permute-done((bf16[64,512]{1,0:T(8,128)(2,1)S(1)}, bf16[64,512]{1,0:T(8,128)(2,1)S(1)}, u32[]{:S(2)}, u32[]{:S(2)}) %collective-permute-start.2) | collective-permute-done | bytes 65568 | tf_op jit(solution)/shard_map/ppermute | solution.py:41
  13.9 1.9 %collective-permute-done = bf16[3,256,256]{2,1,0:T(8,128)(2,1)S(1)} collective-permute-done((bf16[3,256,256]{2,1,0:T(8,128)(2,1)S(1)}, bf16[3,256,256]{2,1,0:T(8,128)(2,1)S(1)}, u32[]{:S(2)}, u32[]{:S(2)}) %collective-permute-start) | collective-permute-done | bytes 393248 | tf_op jit(solution)/shard_map/ppermute | solution.py:41
  16.0 4.4 %collective-permute-start.6 = (bf16[256,256]{1,0:T(8,128)(2,1)S(1)}, bf16[256,256]{1,0:T(8,128)(2,1)S(1)}, u32[]{:S(2)}, u32[]{:S(2)}) collective-permute-start(bf16[256,256]{1,0:T(8,128)(2,1)S(1)} %get-tuple-element.59.rest_0_), channel_id=1, source_target_pairs={{0,24},{4,28},{8,16},{12,20},{16,8},{20,12},{24,0},{28,4},{1,25},{... | collective-permute-start | bytes 393224 | tf_op jit(solution)/shard_map/ppermute | solution.py:41
  20.9 0.6 collective-permute-start.8
  21.5 4.3 %shard_map.85.refs_0_ = f32[1024,256]{1,0:T(8,128)S(1)} custom-call(s32[8,7]{1,0:T(8,128)S(1)} %copy-done.7, s32[8]{0:T(128)S(1)} %copy-done.8, bf16[8,7,256,256]{3,2,1,0:T(8,128)(2,1)} %blocks_hbm.3, bf16[2048,256]{1,0:T(8,128)(2,1)S(1)} %copy-done, bf16[256,256]{1,0:T(8,128)(2,1)S(1)} %get-tuple-element.59.rest_0_), custom_call_target="tpu_custom_call" | custom-call | flops 1024 | bytes 1024 | tf_op jit(solution)/shard_map/pallas_call | solution.py:25
  25.9 3.5 %collective-permute-done.7 = bf16[256,256]{1,0:T(8,128)(2,1)S(1)} collective-permute-done((bf16[256,256]{1,0:T(8,128)(2,1)S(1)}, bf16[256,256]{1,0:T(8,128)(2,1)S(1)}, u32[]{:S(2)}, u32[]{:S(2)}) %collective-permute-start.7) | collective-permute-done | bytes 131104 | tf_op jit(solution)/shard_map/ppermute | solution.py:41
  29.5 1.6 %collective-permute-start.10 = (bf16[256,256]{1,0:T(8,128)(2,1)S(1)}, bf16[256,256]{1,0:T(8,128)(2,1)S(1)}, u32[]{:S(2)}, u32[]{:S(2)}) collective-permute-start(bf16[256,256]{1,0:T(8,128)(2,1)S(1)} %add_convert_fusion.1.refs_4_), channel_id=1, source_target_pairs={{0,4},{4,0},{8,12},{12,8},{16,20},{20,16},{24,28},{28,24},{1,5},{5... | collective-permute-start | bytes 393224 | tf_op jit(solution)/shard_map/ppermute | solution.py:41
  31.1 1.5 %collective-permute-start.9 = (bf16[64,512]{1,0:T(8,128)(2,1)S(1)}, bf16[64,512]{1,0:T(8,128)(2,1)S(1)}, u32[]{:S(2)}, u32[]{:S(2)}) collective-permute-start(bf16[64,512]{1,0:T(8,128)(2,1)S(1)} %collective-permute-done.2.refs_4_), channel_id=1, source_target_pairs={{0,2},{1,3},{2,0},{3,1},{4,6},{5,7},{6,4},{7,5},{8,10},{9,11},{10,... | collective-permute-start | bytes 196616 | tf_op jit(solution)/shard_map/ppermute | solution.py:41
  32.6 2.7 %collective-permute-done.9.refs_6_ = bf16[64,512]{1,0:T(8,128)(2,1)S(1)} collective-permute-done((bf16[64,512]{1,0:T(8,128)(2,1)S(1)}, bf16[64,512]{1,0:T(8,128)(2,1)S(1)}, u32[]{:S(2)}, u32[]{:S(2)}) %collective-permute-start.9) | collective-permute-done | bytes 65568 | tf_op jit(solution)/shard_map/ppermute | solution.py:41
  36.2 0.7 %collective-permute-done.11.refs_5_ = bf16[64,512]{1,0:T(8,128)(2,1)S(1)} collective-permute-done((bf16[64,512]{1,0:T(8,128)(2,1)S(1)}, bf16[64,512]{1,0:T(8,128)(2,1)S(1)}, u32[]{:S(2)}, u32[]{:S(2)}) %collective-permute-start.11) | collective-permute-done | bytes 65568 | tf_op jit(solution)/shard_map/ppermute | solution.py:41
  37.1 3.5 %collective-permute-done.13.refs_5_ = bf16[256,256]{1,0:T(8,128)(2,1)S(1)} collective-permute-done((bf16[256,256]{1,0:T(8,128)(2,1)S(1)}, bf16[256,256]{1,0:T(8,128)(2,1)S(1)}, u32[]{:S(2)}, u32[]{:S(2)}) %collective-permute-start.13) | collective-permute-done | bytes 131104 | tf_op jit(solution)/shard_map/ppermute | solution.py:41
  40.9 1.3 %collective-permute-start.14 = (bf16[256,256]{1,0:T(8,128)(2,1)S(1)}, bf16[256,256]{1,0:T(8,128)(2,1)S(1)}, u32[]{:S(2)}, u32[]{:S(2)}) collective-permute-start(bf16[256,256]{1,0:T(8,128)(2,1)S(1)} %shard_map.87.rest_0_.refs_8_), channel_id=1, source_target_pairs={{0,16},{4,20},{8,24},{12,28},{16,0},{20,4},{24,8},{28,12},{1,17},{... | collective-permute-start | bytes 393224 | tf_op jit(solution)/shard_map/ppermute | solution.py:41
  42.1 4.3 %shard_map.88.refs_1_ = f32[1024,256]{1,0:T(8,128)S(1)} custom-call(s32[8,7]{1,0:T(8,128)S(1)} %copy-done.7, s32[8]{0:T(128)S(1)} %copy-done.8, bf16[8,7,256,256]{3,2,1,0:T(8,128)(2,1)} %blocks_hbm.3, bf16[2048,256]{1,0:T(8,128)(2,1)S(1)} %copy-done, bf16[256,256]{1,0:T(8,128)(2,1)S(1)} %shard_map.87.rest_0_.refs_8_), custom_call_target="tpu_custom_call" | custom-call | flops 1024 | bytes 1024 | tf_op jit(solution)/shard_map/pallas_call | solution.py:25
  46.4 1.0 %copy-done.3 = f32[1024,256]{1,0:T(8,128)} copy-done((f32[1024,256]{1,0:T(8,128)}, f32[1024,256]{1,0:T(8,128)S(1)}, u32[]{:S(2)}) %copy-start.3) | copy-done | bytes 1048600
  47.9 1.0 %shard_map.89 = (bf16[256,256]{1,0:T(8,128)(2,1)}, bf16[256,256]{1,0:T(8,128)(2,1)S(1)}) custom-call(s32[1]{0:T(128)} %bitcast.2.rest_0_.me_ref, bf16[3,64,512]{2,1,0:T(8,128)(2,1)S(1)} %bitcast.18, bf16[3,64,512]{2,1,0:T(8,128)(2,1)S(1)} %collective-permute-done.4.refs_1_, bf16[3,64,512]{2,1,0:T(8,128)(2,1)S(1)} %collective-permute-done.1.refs_2_, ...), custom_call_target="tpu_custom_call" | custom-call | flops 1024 | bytes 1024 | tf_op jit(solution)/shard_map/pallas_call | solution.py:25
  48.9 1.5 %collective-permute-start.15 = (bf16[256,256]{1,0:T(8,128)(2,1)}, bf16[256,256]{1,0:T(8,128)(2,1)S(1)}, u32[]{:S(2)}, u32[]{:S(2)}) collective-permute-start(bf16[256,256]{1,0:T(8,128)(2,1)} %get-tuple-element.52.refs_2_), channel_id=1, source_target_pairs={{0,8},{4,12},{8,0},{12,4},{16,24},{20,28},{24,16},{28,20},{1,9},{5... | collective-permute-start | bytes 393224 | tf_op jit(solution)/shard_map/ppermute | solution.py:41
  50.4 0.7 %collective-permute-start.16 = (bf16[256,256]{1,0:T(8,128)(2,1)S(1)}, bf16[256,256]{1,0:T(8,128)(2,1)S(1)}, u32[]{:S(2)}, u32[]{:S(2)}) collective-permute-start(bf16[256,256]{1,0:T(8,128)(2,1)S(1)} %get-tuple-element.53.refs_3_), channel_id=1, source_target_pairs={{0,4},{4,0},{8,12},{12,8},{16,20},{20,16},{24,28},{28,24},{1,5},{5... | collective-permute-start | bytes 393224 | tf_op jit(solution)/shard_map/ppermute | solution.py:41
  51.4 1.4 %collective-permute-start.17 = (bf16[256,256]{1,0:T(8,128)(2,1)}, bf16[256,256]{1,0:T(8,128)(2,1)S(1)}, u32[]{:S(2)}, u32[]{:S(2)}) collective-permute-start(bf16[256,256]{1,0:T(8,128)(2,1)} %get-tuple-element.52.refs_2_), channel_id=1, source_target_pairs={{0,4},{4,0},{8,12},{12,8},{16,20},{20,16},{24,28},{28,24},{1,5},{5... | collective-permute-start | bytes 393224 | tf_op jit(solution)/shard_map/ppermute | solution.py:41
  53.4 1.2 %copy-done.4 = f32[1024,256]{1,0:T(8,128)S(1)} copy-done((f32[1024,256]{1,0:T(8,128)S(1)}, f32[1024,256]{1,0:T(8,128)}, u32[]{:S(2)}) %copy-start.4) | copy-done | bytes 1048600
  54.6 1.8 %shard_map.90.refs_0_ = f32[2048,256]{1,0:T(8,128)S(1)} custom-call(s32[1]{0:T(128)} %bitcast.me_ref, s32[2048,1]{1,0:T(8,128)S(1)} %copy.11.owner_ref, bf16[2048,256]{1,0:T(8,128)(2,1)S(1)} %copy-done.2, f32[1024,256]{1,0:T(8,128)S(1)} %shard_map.85.refs_0_, f32[1024,256]{1,0:T(8,128)S(1)} %copy-done.4, bf16[256,256]{1,0:T(8,128)(2,1)} %get-tuple-element.52.refs_2_, ...), custom_call_target="tpu_custom_call" | custom-call | flops 1024 | bytes 1024 | tf_op jit(solution)/shard_map/pallas_call | solution.py:25
  56.4 0.7 %collective-permute-start.19 = (bf16[256,256]{1,0:T(8,128)(2,1)S(1)}, bf16[256,256]{1,0:T(8,128)(2,1)S(1)}, u32[]{:S(2)}, u32[]{:S(2)}) collective-permute-start(bf16[256,256]{1,0:T(8,128)(2,1)S(1)} %collective-permute-done.15.refs_2_), channel_id=1, source_target_pairs={{0,4},{4,0},{8,12},{12,8},{16,20},{20,16},{24,28},{28,24},{1,5},{5... | collective-permute-start | bytes 393224 | tf_op jit(solution)/shard_map/ppermute | solution.py:41
  57.2 1.5 %collective-permute-start.20 = (bf16[256,256]{1,0:T(8,128)(2,1)S(1)}, bf16[256,256]{1,0:T(8,128)(2,1)S(1)}, u32[]{:S(2)}, u32[]{:S(2)}) collective-permute-start(bf16[256,256]{1,0:T(8,128)(2,1)S(1)} %collective-permute-done.16.refs_3_), channel_id=1, source_target_pairs={{0,8},{4,12},{8,0},{12,4},{16,24},{20,28},{24,16},{28,20},{1,9},{5... | collective-permute-start | bytes 393224 | tf_op jit(solution)/shard_map/ppermute | solution.py:41
  59.2 1.7 %shard_map.91.refs_0_ = f32[2048,256]{1,0:T(8,128)S(1)} custom-call(s32[1]{0:T(128)} %bitcast.me_ref, s32[2048,1]{1,0:T(8,128)S(1)} %copy.11.owner_ref, bf16[2048,256]{1,0:T(8,128)(2,1)S(1)} %copy-done.2, f32[2048,256]{1,0:T(8,128)S(1)} %shard_map.90.refs_0_, bf16[256,256]{1,0:T(8,128)(2,1)S(1)} %collective-permute-done.17.refs_1_, ...), custom_call_target="tpu_custom_call" | custom-call | flops 1024 | bytes 1024 | tf_op jit(solution)/shard_map/pallas_call | solution.py:25
  60.9 0.6 collective-permute-done.19.refs_1_
  61.5 0.7 %collective-permute-done.20.refs_2_ = bf16[256,256]{1,0:T(8,128)(2,1)S(1)} collective-permute-done((bf16[256,256]{1,0:T(8,128)(2,1)S(1)}, bf16[256,256]{1,0:T(8,128)(2,1)S(1)}, u32[]{:S(2)}, u32[]{:S(2)}) %collective-permute-start.20) | collective-permute-done | bytes 131104 | tf_op jit(solution)/shard_map/ppermute | solution.py:41
  62.2 1.7 %shard_map.92 = bf16[2048,256]{1,0:T(8,128)(2,1)} custom-call(s32[1]{0:T(128)} %bitcast.me_ref, s32[2048,1]{1,0:T(8,128)S(1)} %copy.11.owner_ref, bf16[2048,256]{1,0:T(8,128)(2,1)S(1)} %copy-done.2, f32[2048,256]{1,0:T(8,128)S(1)} %shard_map.91.refs_0_, bf16[256,256]{1,0:T(8,128)(2,1)S(1)} %collective-permute-done.19.refs_1_, ...), custom_call_target="tpu_custom_call" | custom-call | flops 1024 | bytes 1024 | tf_op jit(solution)/shard_map/pallas_call | solution.py:25
  (45 shorter events, 4.1 us)
Async XLA Ops:
  0.0 6.0 %copy-start.1 = (bf16[2048,256]{1,0:T(8,128)(2,1)S(1)}, bf16[2048,256]{1,0:T(8,128)(2,1)}, u32[]{:S(2)}) copy-start(bf16[2048,256]{1,0:T(8,128)(2,1)} %basis_ref.6) | copy-start | bytes 3145732
  0.0 6.0 %copy-start.6 = (s32[2048,1]{0,1:T(1,128)S(1)}, s32[2048,1]{0,1:T(1,128)}, u32[]{:S(2)}) copy-start(s32[2048,1]{0,1:T(1,128)} %param.9) | copy-start | bytes 24580
  0.0 6.0 %copy-start = (bf16[2048,256]{1,0:T(8,128)(2,1)S(1)}, bf16[2048,256]{1,0:T(8,128)(2,1)}, u32[]{:S(2)}) copy-start(bf16[2048,256]{1,0:T(8,128)(2,1)} %fields_ref.3) | copy-start | bytes 3145732
  0.0 7.1 %copy-start.5 = (bf16[1,3,64,512]{3,2,1,0:T(8,128)(2,1)S(1)}, bf16[1,3,64,512]{3,2,1,0:T(8,128)(2,1)}, u32[]{:S(2)}) copy-start(bf16[1,3,64,512]{3,2,1,0:T(8,128)(2,1)} %param.12) | copy-start | bytes 589828
  3.0 12.8 %collective-permute-start = (bf16[3,256,256]{2,1,0:T(8,128)(2,1)S(1)}, bf16[3,256,256]{2,1,0:T(8,128)(2,1)S(1)}, u32[]{:S(2)}, u32[]{:S(2)}) collective-permute-start(bf16[3,256,256]{2,1,0:T(8,128)(2,1)S(1)} %get-tuple-element.35), channel_id=1, source_target_pairs={{0,4},{4,0},{8,12},{12,8},{16,20},{20,16},{24,28},{28,24},{1,5},{5... | collective-permute-start | bytes 1179656 | tf_op jit(solution)/shard_map/ppermute | solution.py:41
  7.1 6.9 %collective-permute-start.1 = (bf16[3,64,512]{2,1,0:T(8,128)(2,1)S(1)}, bf16[3,64,512]{2,1,0:T(8,128)(2,1)S(1)}, u32[]{:S(2)}, u32[]{:S(2)}) collective-permute-start(bf16[3,64,512]{2,1,0:T(8,128)(2,1)S(1)} %bitcast.14), channel_id=1, source_target_pairs={{0,2},{1,3},{2,0},{3,1},{4,6},{5,7},{6,4},{7,5},{8,10},{9,11},{10,... | collective-permute-start | bytes 589832 | tf_op jit(solution)/shard_map/ppermute | solution.py:41
  8.7 12.8 %copy-start.7 = (s32[8,7]{1,0:T(8,128)S(1)}, s32[8,7]{1,0:T(8,128)}, u32[]{:S(2)}) copy-start(s32[8,7]{1,0:T(8,128)} %index_ref.3) | copy-start | bytes 676
  8.7 12.8 %copy-start.8 = (s32[8]{0:T(128)S(1)}, s32[8]{0:T(128)}, u32[]{:S(2)}) copy-start(s32[8]{0:T(128)} %count_ref.3) | copy-start | bytes 100
  8.7 5.2 %collective-permute-start.2 = (bf16[64,512]{1,0:T(8,128)(2,1)S(1)}, bf16[64,512]{1,0:T(8,128)(2,1)S(1)}, u32[]{:S(2)}, u32[]{:S(2)}) collective-permute-start(bf16[64,512]{1,0:T(8,128)(2,1)S(1)} %slice_bitcast_fusion.3), channel_id=1, source_target_pairs={{0,16},{4,20},{8,24},{12,28},{16,0},{20,4},{24,8},{28,12},{1,17},{... | collective-permute-start | bytes 196616 | tf_op jit(solution)/shard_map/ppermute | solution.py:41
  11.3 24.0 %collective-permute-start.4 = (bf16[3,64,512]{2,1,0:T(8,128)(2,1)S(1)}, bf16[3,64,512]{2,1,0:T(8,128)(2,1)S(1)}, u32[]{:S(2)}, u32[]{:S(2)}) collective-permute-start(bf16[3,64,512]{2,1,0:T(8,128)(2,1)S(1)} %bitcast.15), channel_id=1, source_target_pairs={{0,1},{1,0},{2,3},{3,2},{4,5},{5,4},{6,7},{7,6},{8,9},{9,8},{10,11... | collective-permute-start | bytes 589832 | tf_op jit(solution)/shard_map/ppermute | solution.py:41
  11.3 14.5 %collective-permute-start.3 = (bf16[1,256,256]{2,1,0:T(8,128)(2,1)S(1)}, bf16[1,256,256]{2,1,0:T(8,128)(2,1)S(1)}, u32[]{:S(2)}, u32[]{:S(2)}) collective-permute-start(bf16[1,256,256]{2,1,0:T(8,128)(2,1)S(1)} %get-tuple-element.38), channel_id=1, source_target_pairs={{0,4},{4,0},{8,12},{12,8},{16,20},{20,16},{24,28},{28,24},{1,5},{5... | collective-permute-start | bytes 393224 | tf_op jit(solution)/shard_map/ppermute | solution.py:41
  16.0 13.5 %collective-permute-start.6 = (bf16[256,256]{1,0:T(8,128)(2,1)S(1)}, bf16[256,256]{1,0:T(8,128)(2,1)S(1)}, u32[]{:S(2)}, u32[]{:S(2)}) collective-permute-start(bf16[256,256]{1,0:T(8,128)(2,1)S(1)} %get-tuple-element.59.rest_0_), channel_id=1, source_target_pairs={{0,24},{4,28},{8,16},{12,20},{16,8},{20,12},{24,0},{28,4},{1,25},{... | collective-permute-start | bytes 393224 | tf_op jit(solution)/shard_map/ppermute | solution.py:41
  20.9 8.6 %collective-permute-start.7 = (bf16[256,256]{1,0:T(8,128)(2,1)S(1)}, bf16[256,256]{1,0:T(8,128)(2,1)S(1)}, u32[]{:S(2)}, u32[]{:S(2)}) collective-permute-start(bf16[256,256]{1,0:T(8,128)(2,1)S(1)} %get-tuple-element.57), channel_id=1, source_target_pairs={{0,16},{4,20},{8,24},{12,28},{16,0},{20,4},{24,8},{28,12},{1,17},{... | collective-permute-start | bytes 393224 | tf_op jit(solution)/shard_map/ppermute | solution.py:41
  20.9 8.5 %collective-permute-start.8 = (bf16[256,256]{1,0:T(8,128)(2,1)S(1)}, bf16[256,256]{1,0:T(8,128)(2,1)S(1)}, u32[]{:S(2)}, u32[]{:S(2)}) collective-permute-start(bf16[256,256]{1,0:T(8,128)(2,1)S(1)} %get-tuple-element.58), channel_id=1, source_target_pairs={{0,8},{4,12},{8,0},{12,4},{16,24},{20,28},{24,16},{28,20},{1,9},{5... | collective-permute-start | bytes 393224 | tf_op jit(solution)/shard_map/ppermute | solution.py:41
  25.8 9.5 %collective-permute-start.5 = (bf16[3,64,512]{2,1,0:T(8,128)(2,1)S(1)}, bf16[3,64,512]{2,1,0:T(8,128)(2,1)S(1)}, u32[]{:S(2)}, u32[]{:S(2)}) collective-permute-start(bf16[3,64,512]{2,1,0:T(8,128)(2,1)S(1)} %collective-permute-done.1.refs_2_), channel_id=1, source_target_pairs={{0,1},{1,0},{2,3},{3,2},{4,5},{5,4},{6,7},{7,6},{8,9},{9,8},{10,11... | collective-permute-start | bytes 589832 | tf_op jit(solution)/shard_map/ppermute | solution.py:41
  29.5 5.8 %collective-permute-start.10 = (bf16[256,256]{1,0:T(8,128)(2,1)S(1)}, bf16[256,256]{1,0:T(8,128)(2,1)S(1)}, u32[]{:S(2)}, u32[]{:S(2)}) collective-permute-start(bf16[256,256]{1,0:T(8,128)(2,1)S(1)} %add_convert_fusion.1.refs_4_), channel_id=1, source_target_pairs={{0,4},{4,0},{8,12},{12,8},{16,20},{20,16},{24,28},{28,24},{1,5},{5... | collective-permute-start | bytes 393224 | tf_op jit(solution)/shard_map/ppermute | solution.py:41
  31.1 4.3 %collective-permute-start.9 = (bf16[64,512]{1,0:T(8,128)(2,1)S(1)}, bf16[64,512]{1,0:T(8,128)(2,1)S(1)}, u32[]{:S(2)}, u32[]{:S(2)}) collective-permute-start(bf16[64,512]{1,0:T(8,128)(2,1)S(1)} %collective-permute-done.2.refs_4_), channel_id=1, source_target_pairs={{0,2},{1,3},{2,0},{3,1},{4,6},{5,7},{6,4},{7,5},{8,10},{9,11},{10,... | collective-permute-start | bytes 196616 | tf_op jit(solution)/shard_map/ppermute | solution.py:41
  35.6 5.0 %collective-permute-start.13 = (bf16[256,256]{1,0:T(8,128)(2,1)S(1)}, bf16[256,256]{1,0:T(8,128)(2,1)S(1)}, u32[]{:S(2)}, u32[]{:S(2)}) collective-permute-start(bf16[256,256]{1,0:T(8,128)(2,1)S(1)} %shard_map.86.refs_4_), channel_id=1, source_target_pairs={{0,8},{4,12},{8,0},{12,4},{16,24},{20,28},{24,16},{28,20},{1,9},{5... | collective-permute-start | bytes 393224 | tf_op jit(solution)/shard_map/ppermute | solution.py:41
  35.7 1.3 %collective-permute-start.11 = (bf16[64,512]{1,0:T(8,128)(2,1)S(1)}, bf16[64,512]{1,0:T(8,128)(2,1)S(1)}, u32[]{:S(2)}, u32[]{:S(2)}) collective-permute-start(bf16[64,512]{1,0:T(8,128)(2,1)S(1)} %collective-permute-done.2.refs_4_), channel_id=1, source_target_pairs={{0,1},{1,0},{2,3},{3,2},{4,5},{5,4},{6,7},{7,6},{8,9},{9,8},{10,11... | collective-permute-start | bytes 196616 | tf_op jit(solution)/shard_map/ppermute | solution.py:41
  35.7 1.4 %collective-permute-start.12 = (bf16[64,512]{1,0:T(8,128)(2,1)S(1)}, bf16[64,512]{1,0:T(8,128)(2,1)S(1)}, u32[]{:S(2)}, u32[]{:S(2)}) collective-permute-start(bf16[64,512]{1,0:T(8,128)(2,1)S(1)} %collective-permute-done.9.refs_6_), channel_id=1, source_target_pairs={{0,1},{1,0},{2,3},{3,2},{4,5},{5,4},{6,7},{7,6},{8,9},{9,8},{10,11... | collective-permute-start | bytes 196616 | tf_op jit(solution)/shard_map/ppermute | solution.py:41
  40.9 7.1 %collective-permute-start.14 = (bf16[256,256]{1,0:T(8,128)(2,1)S(1)}, bf16[256,256]{1,0:T(8,128)(2,1)S(1)}, u32[]{:S(2)}, u32[]{:S(2)}) collective-permute-start(bf16[256,256]{1,0:T(8,128)(2,1)S(1)} %shard_map.87.rest_0_.refs_8_), channel_id=1, source_target_pairs={{0,16},{4,20},{8,24},{12,28},{16,0},{20,4},{24,8},{28,12},{1,17},{... | collective-permute-start | bytes 393224 | tf_op jit(solution)/shard_map/ppermute | solution.py:41
  46.4 1.0 %copy-start.3 = (f32[1024,256]{1,0:T(8,128)}, f32[1024,256]{1,0:T(8,128)S(1)}, u32[]{:S(2)}) copy-start(f32[1024,256]{1,0:T(8,128)S(1)} %shard_map.88.refs_1_) | copy-start | bytes 3145732
  47.4 6.0 %copy-start.2 = (bf16[2048,256]{1,0:T(8,128)(2,1)S(1)}, bf16[2048,256]{1,0:T(8,128)(2,1)}, u32[]{:S(2)}) copy-start(bf16[2048,256]{1,0:T(8,128)(2,1)} %basis_ref.9) | copy-start | bytes 3145732
  48.9 7.5 %collective-permute-start.15 = (bf16[256,256]{1,0:T(8,128)(2,1)}, bf16[256,256]{1,0:T(8,128)(2,1)S(1)}, u32[]{:S(2)}, u32[]{:S(2)}) collective-permute-start(bf16[256,256]{1,0:T(8,128)(2,1)} %get-tuple-element.52.refs_2_), channel_id=1, source_target_pairs={{0,8},{4,12},{8,0},{12,4},{16,24},{20,28},{24,16},{28,20},{1,9},{5... | collective-permute-start | bytes 393224 | tf_op jit(solution)/shard_map/ppermute | solution.py:41
  50.4 6.0 %collective-permute-start.16 = (bf16[256,256]{1,0:T(8,128)(2,1)S(1)}, bf16[256,256]{1,0:T(8,128)(2,1)S(1)}, u32[]{:S(2)}, u32[]{:S(2)}) collective-permute-start(bf16[256,256]{1,0:T(8,128)(2,1)S(1)} %get-tuple-element.53.refs_3_), channel_id=1, source_target_pairs={{0,4},{4,0},{8,12},{12,8},{16,20},{20,16},{24,28},{28,24},{1,5},{5... | collective-permute-start | bytes 393224 | tf_op jit(solution)/shard_map/ppermute | solution.py:41
  51.4 7.3 %collective-permute-start.17 = (bf16[256,256]{1,0:T(8,128)(2,1)}, bf16[256,256]{1,0:T(8,128)(2,1)S(1)}, u32[]{:S(2)}, u32[]{:S(2)}) collective-permute-start(bf16[256,256]{1,0:T(8,128)(2,1)} %get-tuple-element.52.refs_2_), channel_id=1, source_target_pairs={{0,4},{4,0},{8,12},{12,8},{16,20},{20,16},{24,28},{28,24},{1,5},{5... | collective-permute-start | bytes 393224 | tf_op jit(solution)/shard_map/ppermute | solution.py:41
  52.8 6.4 %collective-permute-start.18 = (bf16[256,256]{1,0:T(8,128)(2,1)S(1)}, bf16[256,256]{1,0:T(8,128)(2,1)S(1)}, u32[]{:S(2)}, u32[]{:S(2)}) collective-permute-start(bf16[256,256]{1,0:T(8,128)(2,1)S(1)} %get-tuple-element.53.refs_3_), channel_id=1, source_target_pairs={{0,8},{4,12},{8,0},{12,4},{16,24},{20,28},{24,16},{28,20},{1,9},{5... | collective-permute-start | bytes 393224 | tf_op jit(solution)/shard_map/ppermute | solution.py:41
  53.4 1.2 %copy-start.4 = (f32[1024,256]{1,0:T(8,128)S(1)}, f32[1024,256]{1,0:T(8,128)}, u32[]{:S(2)}) copy-start(f32[1024,256]{1,0:T(8,128)} %copy-done.3) | copy-start | bytes 3145732
  56.4 5.0 %collective-permute-start.19 = (bf16[256,256]{1,0:T(8,128)(2,1)S(1)}, bf16[256,256]{1,0:T(8,128)(2,1)S(1)}, u32[]{:S(2)}, u32[]{:S(2)}) collective-permute-start(bf16[256,256]{1,0:T(8,128)(2,1)S(1)} %collective-permute-done.15.refs_2_), channel_id=1, source_target_pairs={{0,4},{4,0},{8,12},{12,8},{16,20},{20,16},{24,28},{28,24},{1,5},{5... | collective-permute-start | bytes 393224 | tf_op jit(solution)/shard_map/ppermute | solution.py:41
  57.2 5.0 %collective-permute-start.20 = (bf16[256,256]{1,0:T(8,128)(2,1)S(1)}, bf16[256,256]{1,0:T(8,128)(2,1)S(1)}, u32[]{:S(2)}, u32[]{:S(2)}) collective-permute-start(bf16[256,256]{1,0:T(8,128)(2,1)S(1)} %collective-permute-done.16.refs_3_), channel_id=1, source_target_pairs={{0,8},{4,12},{8,0},{12,4},{16,24},{20,28},{24,16},{28,20},{1,9},{5... | collective-permute-start | bytes 393224 | tf_op jit(solution)/shard_map/ppermute | solution.py:41

commit v4 on v3

--- a/solution.py
+++ b/solution.py
@@ -10,6 +10,7 @@
 F32 = jnp.float32
 BF16 = jnp.bfloat16
 VMEM_LIMIT = 16 * 1024 * 1024
+LANES = 128
 VMEM = pl.BlockSpec(memory_space=pltpu.VMEM)
 SMEM = pl.BlockSpec(memory_space=pltpu.SMEM)
 HBM = pl.BlockSpec(memory_space=pltpu.HBM)
@@ -70,22 +71,34 @@
     products(owner_ref[...] ^ me_ref[0], basis_ref[...].T, fields_ref[...], groups, outs)
 
 
-def compress(me, owner_row, basis, fields, groups, dtype, staged, after=()):
+def tagged_compress_kernel(groups, me_ref, owner_ref, basis_ref, fields_ref, *rest):
+    outs, tag_ref = rest[-len(groups) - 1 : -1], rest[-1]
+    relative = owner_ref[...] ^ me_ref[0]
+    products(relative, basis_ref[...].T, fields_ref[...], groups, outs)
+    wide = jnp.broadcast_to(relative.astype(F32), (LANES, relative.shape[1]))
+    tag_ref[...] = wide.T.astype(BF16)
+
+
+def compress(me, owner_row, basis, fields, groups, dtypes, kind, after=()):
     rows, cols = fields.shape
     width = basis.shape[1]
+    staged = kind is staged_compress_kernel
     held = [
         pltpu.VMEM((1, rows), jnp.int32),
         pltpu.VMEM((rows, width), BF16),
         pltpu.VMEM((rows, cols), BF16),
         pltpu.SemaphoreType.DMA((3,)),
     ]
+    shapes = [jax.ShapeDtypeStruct((len(g), width, cols), d) for g, d in zip(groups, dtypes)]
+    if kind is tagged_compress_kernel:
+        shapes.append(jax.ShapeDtypeStruct((rows, LANES), BF16))
     return list(
         call(
-            functools.partial(staged_compress_kernel if staged else compress_kernel, groups),
-            [jax.ShapeDtypeStruct((len(g), width, cols), dtype) for g in groups],
+            functools.partial(kind, groups),
+            shapes,
             (me, owner_row, basis, fields),
             [SMEM] + [HBM if staged else VMEM] * 3,
-            [pltpu.VMEM] * len(groups),
+            [pltpu.VMEM] * len(shapes),
             held if staged else (),
             after,
         )
@@ -138,7 +151,8 @@
 
 
 def level_kernel(n_rhs, n_out, level, me_ref, *refs):
-    rows, (own_ref, other_ref), outs = refs[: n_rhs * n_out], refs[-2 - n_out : -n_out], refs[-n_out:]
+    rows, (own_ref, other_ref) = refs[: n_rhs * n_out], refs[n_rhs * n_out :][:2]
+    outs = refs[-n_out:]
     own, other = own_ref[...], other_ref[...]
     for k, out in enumerate(outs):
         pieces = [ref[level] if k == 0 else ref[...] for ref in rows[k * n_rhs :][:n_rhs]]
@@ -146,7 +160,7 @@
         apply_rows(me_ref[0], pieces, stacked, out)
 
 
-def next_level(rhs_me, level, rows, own, other, other_rows=()):
+def next_level(rhs_me, level, rows, own, other, other_rows=(), after=()):
     n_out = 2 if other_rows else 1
     return call(
         functools.partial(level_kernel, len(rows), n_out, level),
@@ -154,16 +168,19 @@
         (rhs_me, *rows, *other_rows, own, other),
         [SMEM] + [VMEM] * (len(rows) * n_out + 2),
         [pltpu.VMEM] * n_out,
-    )
-
-
-def far_tile(ids, me_ref, owner_ref, basis_ref, bases, blocks, start, tile):
+        (),
+        after,
+    )
+
+
+def far_tile(ids, tag_ref, basis_ref, bases, blocks, start, tile):
     part = pl.ds(start, tile)
     rows = bases[0].shape[0]
     base = bases[start // rows][pl.ds(start % rows, tile), :]
-    relative = owner_ref[part, :] ^ me_ref[0]
+    tag = tag_ref[part, :]
     basis = basis_ref[part, :]
-    masked = [jnp.where(relative == j, basis, jnp.zeros((), BF16)) for j in ids]
+    lanes = [basis[:, k : k + LANES] for k in range(0, basis.shape[1], LANES)]
+    masked = [jnp.where(tag == j, piece, jnp.zeros((), BF16)) for j in ids for piece in lanes]
     stacked = [ref[...] for ref in blocks]
     total = jnp.dot(
         jnp.concatenate(masked, axis=1),
@@ -173,18 +190,18 @@
     return total.astype(BF16).astype(F32) + base
 
 
-def far_kernel(ids, tile, n_base, me_ref, owner_ref, basis_ref, *refs):
+def far_kernel(ids, tile, n_base, tag_ref, basis_ref, *refs):
     bases, blocks, out_ref = refs[:n_base], refs[n_base:-1], refs[-1]
     for start in range(0, out_ref.shape[0], tile):
-        value = far_tile(ids, me_ref, owner_ref, basis_ref, bases, blocks, start, tile)
+        value = far_tile(ids, tag_ref, basis_ref, bases, blocks, start, tile)
         out_ref[pl.ds(start, tile), :] = value
 
 
-def last_far_kernel(ids, tile, n_base, me_ref, owner_ref, basis_ref, *refs):
+def last_far_kernel(ids, tile, n_base, tag_ref, basis_ref, *refs):
     bases, blocks, (out_hbm, held_ref, sems) = refs[:n_base], refs[n_base:-3], refs[-3:]
     copies = []
     for t in range(out_hbm.shape[0] // tile):
-        value = far_tile(ids, me_ref, owner_ref, basis_ref, bases, blocks, t * tile, tile)
+        value = far_tile(ids, tag_ref, basis_ref, bases, blocks, t * tile, tile)
         part = pl.ds(t * tile, tile)
         held_ref[part, :] = value.astype(BF16)
         copies.append(pltpu.make_async_copy(held_ref.at[part], out_hbm.at[part], sems.at[t]))
@@ -193,15 +210,15 @@
         copy.wait()
 
 
-def far_field(ids, me, owner, basis, bases, blocks, last=False):
+def far_field(ids, tag, basis, bases, blocks, last=False):
     rows, cols = basis.shape[0], bases[0].shape[1]
     tile = min(bases[0].shape[0], 512)
     held = [pltpu.VMEM((rows, cols), BF16), pltpu.SemaphoreType.DMA((rows // tile,))]
     (out,) = call(
         functools.partial(last_far_kernel if last else far_kernel, ids, tile, len(bases)),
         [jax.ShapeDtypeStruct((rows, cols), BF16 if last else F32)],
-        (me, owner, basis, *bases, *blocks),
-        [SMEM] + [VMEM] * (2 + len(bases) + len(blocks)),
+        (tag, basis, *bases, *blocks),
+        [VMEM] * (2 + len(bases) + len(blocks)),
         [pltpu.HBM if last else pltpu.VMEM],
         held if last else (),
     )
@@ -234,11 +251,13 @@
     def groups(low):
         return [[o * group + 2 * s + low for s in part for o in range(outer)] for part in parts]
 
-    send = compress(me, owner_row, source_basis, fields, groups(1), BF16, True, [rhs_me])
-
-    fields, send[0], send[1] = tie(fields, *send)
-    got = [swapped(s, "leaf", 1) for s in send]
-    keep = compress(me, owner_row, source_basis, fields, groups(0)[:1], F32, False)
+    odd, even = groups(1), groups(0)
+    operands = (me, owner_row, source_basis)
+    (send,) = compress(*operands, fields, odd[:1], [BF16], staged_compress_kernel, [rhs_me])
+    fields, send = tie(fields, send)
+    got = [swapped(send, "leaf", 1)]
+    *keep, send = compress(*operands, fields, [even[0], odd[1]], [F32, BF16], compress_kernel)
+    got.append(swapped(send, "leaf", 1))
 
     def reduced(keep, got, part):
         total = keep + got.astype(F32)
@@ -261,7 +280,8 @@
 
     sums = [v.astype(BF16) for v in reduced(keep[0], got[0], parts[0])]
     arrived = [swapped(v, "leaf", 2 * s) for s, v in zip(parts[0], sums)]
-    keep += compress(me, owner_row, source_basis, fields, groups(0)[1:], F32, False, sums[:1])
+    more, tag = compress(*operands, fields, even[1:], [F32], tagged_compress_kernel, sums[:1])
+    keep.append(more)
     (total,) = reduced(keep[1], got[1], parts[1])
     half = near_blocks.shape[0] // 2
     near = [near_field(near_index, near_count, near_blocks, fields, 0, half, sums[:1])]
@@ -285,18 +305,15 @@
         (coefficients,) = next_level(rhs_me, level, rows, coefficients, other)
     other = swapped(coefficients, "leaf", top)
     near.append(near_field(near_index, near_count, near_blocks, fields, half, half, [coefficients]))
-    near[1], coefficients = tie(near[1], coefficients)
-    rows = [mine_rows[o] for o in order]
-    own = next_level(
-        rhs_me, levels - 1, rows, coefficients, other, [their_rows[o] for o in order]
-    )
+    rows, more = [mine_rows[o] for o in order], [their_rows[o] for o in order]
+    own = next_level(rhs_me, levels - 1, rows, coefficients, other, more, near[1:])
 
     def add_far(base, known, last=False):
         ids = [o * group + j for j in sorted(known) for o in range(outer)]
         blocks = []
         for j in sorted(known):
             blocks += [known[j]] + [swapped(known[j], "leaf", o * group) for o in range(1, outer)]
-        return far_field(ids, me, owner, field_basis, base, blocks, last)
+        return far_field(ids, tag, field_basis, base, blocks, last)
 
     known = {0: own[0], top: own[1]}
     steps = [1 << k for k in range(levels - 1)]
@@ -305,9 +322,6 @@
     from_low = {j ^ low: swapped(v, "leaf", low) for j, v in known.items()}
     from_high = {j ^ high: swapped(v, "leaf", high) for j, v in known.items()}
     total = [add_far(total, known)]
-    total[0], from_high[high], from_low[top ^ low] = tie(
-        total[0], from_high[high], from_low[top ^ low]
-    )
     rest = {
         low ^ high: swapped(from_high[high], "leaf", low),
         top ^ low ^ high: swapped(from_low[top ^ low], "leaf", high),

time: 64 us -> 61.5 us (0.961)
  waiting for transfers between devices: 16.9 us -> 20.4 us
  local copies, waits for them, and re-layouts: 2.61 us -> 0.06 us
  Pallas kernels: 19.6 us -> 17.7 us
  starting transfers between devices: 24.3 us -> 22.7 us
    ppermute x21, waiting for transfers between devices: 16.9 us -> 20.4 us  [swapped(): lax.ppermute(value, axis, [(i, i ^ mask) for i in range(lax.axis_size(axi...]
    unnamed x19 -> x14, local copies, waits for them, and re-layouts: 2.58 us -> 0.03 us
    pallas_call x11, Pallas kernels: 19.6 us -> 17.7 us  [call(): pl.pallas_call(kernel, out_shape=[space(s.shape, s.dtype) for s, space in...]
    ppermute x21, starting transfers between devices: 24.3 us -> 22.7 us  [swapped(): lax.ppermute(value, axis, [(i, i ^ mask) for i in range(lax.axis_size(axi...]
  transfers between devices with their start and end apart: 21 -> 21, of which waited for: 11 -> 12; matrix products, arithmetic and copies ran while one was open for 1% -> 0% of each run, Pallas kernels for 21% -> 21%
where the time goes in v4:
time: 61.5 us; the launch traced here: 61.3 us
  starting transfers between devices  22.7 us (37%)
  waiting for transfers between devices  20.4 us (33%)
  Pallas kernels  17.7 us (29%)
    ppermute x21, starting transfers between devices, swapped(): lax.ppermute(value, axis, [(i, i ^ mask) for i in range(lax.axis_size(axi...  22.7 us
    ppermute x21, waiting for transfers between devices, swapped(): lax.ppermute(value, axis, [(i, i ^ mask) for i in range(lax.axis_size(axi...  20.4 us
    pallas_call x11, Pallas kernels, call(): pl.pallas_call(kernel, out_shape=[space(s.shape, s.dtype) for s, space in...  17.7 us
  transfers between devices with their start and end apart: 21, of which 12 were waited for; matrix products, arithmetic and copies ran while one was open for 0% of the time, Pallas kernels for 21%

profile of v4, /device:TPU:0, one launch (start us, length us, event | category | flops | bytes accessed | tf_op | source)
XLA Modules:
  0.0 61.3 jit_solution(1448049475375066866)
XLA Ops:
  0.0 2.7 %shard_map.82 = bf16[3,256,256]{2,1,0:T(8,128)(2,1)S(1)} custom-call(s32[1]{0:T(128)} %bitcast.me_ref, s32[1,2048]{1,0:T(1,128)} %bitcast.19, bf16[2048,256]{1,0:T(8,128)(2,1)} %basis_ref.6, bf16[2048,256]{1,0:T(8,128)(2,1)} %fields_ref.3, s32[1]{0:T(128)} %bitcast.2.rest_0_.me_ref), custom_call_target="tpu_custom_call" | custom-call | flops 1024 | bytes 1024 | tf_op jit(solution)/shard_map/pallas_call | solution.py:26
  2.7 3.0 %collective-permute-start = (bf16[3,256,256]{2,1,0:T(8,128)(2,1)S(1)}, bf16[3,256,256]{2,1,0:T(8,128)(2,1)S(1)}, u32[]{:S(2)}, u32[]{:S(2)}) collective-permute-start(bf16[3,256,256]{2,1,0:T(8,128)(2,1)S(1)} %shard_map.82), channel_id=1, source_target_pairs={{0,4},{4,0},{8,12},{12,8},{16,20},{20,16},{24,28},{28,24},{1,5},{5... | collective-permute-start | bytes 1179656 | tf_op jit(solution)/shard_map/ppermute | solution.py:42
  5.8 1.3 %shard_map.83 = (f32[3,256,256]{2,1,0:T(8,128)S(1)}, bf16[1,256,256]{2,1,0:T(8,128)(2,1)S(1)}) custom-call(s32[1]{0:T(128)} %bitcast.me_ref, s32[1,2048]{1,0:T(1,128)S(1)} %bitcast.20, bf16[2048,256]{1,0:T(8,128)(2,1)S(1)} %copy-done.1, bf16[2048,256]{1,0:T(8,128)(2,1)S(1)} %copy-done), custom_call_target="tpu_custom_call" | custom-call | flops 1024 | bytes 1024 | tf_op jit(solution)/shard_map/pallas_call | solution.py:26
  7.1 1.6 %collective-permute-start.1 = (bf16[3,64,512]{2,1,0:T(8,128)(2,1)S(1)}, bf16[3,64,512]{2,1,0:T(8,128)(2,1)S(1)}, u32[]{:S(2)}, u32[]{:S(2)}) collective-permute-start(bf16[3,64,512]{2,1,0:T(8,128)(2,1)S(1)} %bitcast.14), channel_id=1, source_target_pairs={{0,2},{1,3},{2,0},{3,1},{4,6},{5,7},{6,4},{7,5},{8,10},{9,11},{10,... | collective-permute-start | bytes 589832 | tf_op jit(solution)/shard_map/ppermute | solution.py:42
  8.7 2.6 %collective-permute-start.2 = (bf16[64,512]{1,0:T(8,128)(2,1)S(1)}, bf16[64,512]{1,0:T(8,128)(2,1)S(1)}, u32[]{:S(2)}, u32[]{:S(2)}) collective-permute-start(bf16[64,512]{1,0:T(8,128)(2,1)S(1)} %slice_bitcast_fusion.3), channel_id=1, source_target_pairs={{0,16},{4,20},{8,24},{12,28},{16,0},{20,4},{24,8},{28,12},{1,17},{... | collective-permute-start | bytes 196616 | tf_op jit(solution)/shard_map/ppermute | solution.py:42
  11.3 0.5 collective-permute-start.3
  11.8 2.0 %collective-permute-done.2.refs_4_ = bf16[64,512]{1,0:T(8,128)(2,1)S(1)} collective-permute-done((bf16[64,512]{1,0:T(8,128)(2,1)S(1)}, bf16[64,512]{1,0:T(8,128)(2,1)S(1)}, u32[]{:S(2)}, u32[]{:S(2)}) %collective-permute-start.2) | collective-permute-done | bytes 65568 | tf_op jit(solution)/shard_map/ppermute | solution.py:42
  13.8 1.5 %collective-permute-done = bf16[3,256,256]{2,1,0:T(8,128)(2,1)S(1)} collective-permute-done((bf16[3,256,256]{2,1,0:T(8,128)(2,1)S(1)}, bf16[3,256,256]{2,1,0:T(8,128)(2,1)S(1)}, u32[]{:S(2)}, u32[]{:S(2)}) %collective-permute-start) | collective-permute-done | bytes 393248 | tf_op jit(solution)/shard_map/ppermute | solution.py:42
  15.5 0.6 shard_map.84
  16.1 4.6 %collective-permute-start.6 = (bf16[256,256]{1,0:T(8,128)(2,1)S(1)}, bf16[256,256]{1,0:T(8,128)(2,1)S(1)}, u32[]{:S(2)}, u32[]{:S(2)}) collective-permute-start(bf16[256,256]{1,0:T(8,128)(2,1)S(1)} %get-tuple-element.51.rest_0_), channel_id=1, source_target_pairs={{0,24},{4,28},{8,16},{12,20},{16,8},{20,12},{24,0},{28,4},{1,25},{... | collective-permute-start | bytes 393224 | tf_op jit(solution)/shard_map/ppermute | solution.py:42
  20.7 0.6 %collective-permute-start.8 = (bf16[256,256]{1,0:T(8,128)(2,1)S(1)}, bf16[256,256]{1,0:T(8,128)(2,1)S(1)}, u32[]{:S(2)}, u32[]{:S(2)}) collective-permute-start(bf16[256,256]{1,0:T(8,128)(2,1)S(1)} %get-tuple-element.50), channel_id=1, source_target_pairs={{0,8},{4,12},{8,0},{12,4},{16,24},{20,28},{24,16},{28,20},{1,9},{5... | collective-permute-start | bytes 393224 | tf_op jit(solution)/shard_map/ppermute | solution.py:42
  21.3 4.3 %shard_map.85.refs_0_ = f32[1024,256]{1,0:T(8,128)S(1)} custom-call(s32[8,7]{1,0:T(8,128)S(1)} %copy-done.5, s32[8]{0:T(128)S(1)} %copy-done.6, bf16[8,7,256,256]{3,2,1,0:T(8,128)(2,1)} %blocks_hbm.3, bf16[2048,256]{1,0:T(8,128)(2,1)S(1)} %copy-done, bf16[256,256]{1,0:T(8,128)(2,1)S(1)} %get-tuple-element.51.rest_0_), custom_call_target="tpu_custom_call" | custom-call | flops 1024 | bytes 1024 | tf_op jit(solution)/shard_map/pallas_call | solution.py:26
  25.8 4.0 %collective-permute-done.7 = bf16[256,256]{1,0:T(8,128)(2,1)S(1)} collective-permute-done((bf16[256,256]{1,0:T(8,128)(2,1)S(1)}, bf16[256,256]{1,0:T(8,128)(2,1)S(1)}, u32[]{:S(2)}, u32[]{:S(2)}) %collective-permute-start.7) | collective-permute-done | bytes 131104 | tf_op jit(solution)/shard_map/ppermute | solution.py:42
  29.8 1.6 %collective-permute-start.10 = (bf16[256,256]{1,0:T(8,128)(2,1)S(1)}, bf16[256,256]{1,0:T(8,128)(2,1)S(1)}, u32[]{:S(2)}, u32[]{:S(2)}) collective-permute-start(bf16[256,256]{1,0:T(8,128)(2,1)S(1)} %add_convert_fusion.1.refs_4_), channel_id=1, source_target_pairs={{0,4},{4,0},{8,12},{12,8},{16,20},{20,16},{24,28},{28,24},{1,5},{5... | collective-permute-start | bytes 393224 | tf_op jit(solution)/shard_map/ppermute | solution.py:42
  31.4 1.5 %collective-permute-start.9 = (bf16[64,512]{1,0:T(8,128)(2,1)S(1)}, bf16[64,512]{1,0:T(8,128)(2,1)S(1)}, u32[]{:S(2)}, u32[]{:S(2)}) collective-permute-start(bf16[64,512]{1,0:T(8,128)(2,1)S(1)} %collective-permute-done.2.refs_4_), channel_id=1, source_target_pairs={{0,2},{1,3},{2,0},{3,1},{4,6},{5,7},{6,4},{7,5},{8,10},{9,11},{10,... | collective-permute-start | bytes 196616 | tf_op jit(solution)/shard_map/ppermute | solution.py:42
  32.9 2.7 %collective-permute-done.9.refs_6_ = bf16[64,512]{1,0:T(8,128)(2,1)S(1)} collective-permute-done((bf16[64,512]{1,0:T(8,128)(2,1)S(1)}, bf16[64,512]{1,0:T(8,128)(2,1)S(1)}, u32[]{:S(2)}, u32[]{:S(2)}) %collective-permute-start.9) | collective-permute-done | bytes 65568 | tf_op jit(solution)/shard_map/ppermute | solution.py:42
  36.0 0.5 collective-permute-start.12
  36.5 0.7 %collective-permute-done.11.refs_5_ = bf16[64,512]{1,0:T(8,128)(2,1)S(1)} collective-permute-done((bf16[64,512]{1,0:T(8,128)(2,1)S(1)}, bf16[64,512]{1,0:T(8,128)(2,1)S(1)}, u32[]{:S(2)}, u32[]{:S(2)}) %collective-permute-start.11) | collective-permute-done | bytes 65568 | tf_op jit(solution)/shard_map/ppermute | solution.py:42
  37.4 3.5 %collective-permute-done.13.refs_5_ = bf16[256,256]{1,0:T(8,128)(2,1)S(1)} collective-permute-done((bf16[256,256]{1,0:T(8,128)(2,1)S(1)}, bf16[256,256]{1,0:T(8,128)(2,1)S(1)}, u32[]{:S(2)}, u32[]{:S(2)}) %collective-permute-start.13) | collective-permute-done | bytes 131104 | tf_op jit(solution)/shard_map/ppermute | solution.py:42
  41.1 1.1 %collective-permute-start.14 = (bf16[256,256]{1,0:T(8,128)(2,1)S(1)}, bf16[256,256]{1,0:T(8,128)(2,1)S(1)}, u32[]{:S(2)}, u32[]{:S(2)}) collective-permute-start(bf16[256,256]{1,0:T(8,128)(2,1)S(1)} %shard_map.87.rest_0_.refs_8_), channel_id=1, source_target_pairs={{0,16},{4,20},{8,24},{12,28},{16,0},{20,4},{24,8},{28,12},{1,17},{... | collective-permute-start | bytes 393224 | tf_op jit(solution)/shard_map/ppermute | solution.py:42
  42.2 4.3 %shard_map.88.refs_10_.refs_1_ = f32[1024,256]{1,0:T(8,128)S(1)} custom-call(s32[8,7]{1,0:T(8,128)S(1)} %copy-done.5, s32[8]{0:T(128)S(1)} %copy-done.6, bf16[8,7,256,256]{3,2,1,0:T(8,128)(2,1)} %blocks_hbm.3, bf16[2048,256]{1,0:T(8,128)(2,1)S(1)} %copy-done, bf16[256,256]{1,0:T(8,128)(2,1)S(1)} %shard_map.87.rest_0_.refs_8_), custom_call_target="tpu_custom_call" | custom-call | flops 1024 | bytes 1024 | tf_op jit(solution)/shard_map/pallas_call | solution.py:26
  46.5 1.5 %collective-permute-done.14.refs_9_ = bf16[256,256]{1,0:T(8,128)(2,1)S(1)} collective-permute-done((bf16[256,256]{1,0:T(8,128)(2,1)S(1)}, bf16[256,256]{1,0:T(8,128)(2,1)S(1)}, u32[]{:S(2)}, u32[]{:S(2)}) %collective-permute-start.14) | collective-permute-done | bytes 131104 | tf_op jit(solution)/shard_map/ppermute | solution.py:42
  48.3 0.6 collective-permute-start.16
  48.9 0.7 %collective-permute-start.17 = (bf16[256,256]{1,0:T(8,128)(2,1)S(1)}, bf16[256,256]{1,0:T(8,128)(2,1)S(1)}, u32[]{:S(2)}, u32[]{:S(2)}) collective-permute-start(bf16[256,256]{1,0:T(8,128)(2,1)S(1)} %get-tuple-element.48.refs_3_), channel_id=1, source_target_pairs={{0,4},{4,0},{8,12},{12,8},{16,20},{20,16},{24,28},{28,24},{1,5},{5... | collective-permute-start | bytes 393224 | tf_op jit(solution)/shard_map/ppermute | solution.py:42
  49.6 1.3 %collective-permute-start.15 = (bf16[256,256]{1,0:T(8,128)(2,1)S(1)}, bf16[256,256]{1,0:T(8,128)(2,1)S(1)}, u32[]{:S(2)}, u32[]{:S(2)}) collective-permute-start(bf16[256,256]{1,0:T(8,128)(2,1)S(1)} %get-tuple-element.47.refs_2_), channel_id=1, source_target_pairs={{0,4},{4,0},{8,12},{12,8},{16,20},{20,16},{24,28},{28,24},{1,5},{5... | collective-permute-start | bytes 393224 | tf_op jit(solution)/shard_map/ppermute | solution.py:42
  51.0 1.5 %collective-permute-start.18 = (bf16[256,256]{1,0:T(8,128)(2,1)S(1)}, bf16[256,256]{1,0:T(8,128)(2,1)S(1)}, u32[]{:S(2)}, u32[]{:S(2)}) collective-permute-start(bf16[256,256]{1,0:T(8,128)(2,1)S(1)} %get-tuple-element.48.refs_3_), channel_id=1, source_target_pairs={{0,8},{4,12},{8,0},{12,4},{16,24},{20,28},{24,16},{28,20},{1,9},{5... | collective-permute-start | bytes 393224 | tf_op jit(solution)/shard_map/ppermute | solution.py:42
  52.5 2.0 %collective-permute-done.16.refs_2_ = bf16[256,256]{1,0:T(8,128)(2,1)S(1)} collective-permute-done((bf16[256,256]{1,0:T(8,128)(2,1)S(1)}, bf16[256,256]{1,0:T(8,128)(2,1)S(1)}, u32[]{:S(2)}, u32[]{:S(2)}) %collective-permute-start.16) | collective-permute-done | bytes 131104 | tf_op jit(solution)/shard_map/ppermute | solution.py:42
  54.7 0.7 %collective-permute-start.20 = (bf16[256,256]{1,0:T(8,128)(2,1)S(1)}, bf16[256,256]{1,0:T(8,128)(2,1)S(1)}, u32[]{:S(2)}, u32[]{:S(2)}) collective-permute-start(bf16[256,256]{1,0:T(8,128)(2,1)S(1)} %collective-permute-done.17.refs_3_), channel_id=1, source_target_pairs={{0,8},{4,12},{8,0},{12,4},{16,24},{20,28},{24,16},{28,20},{1,9},{5... | collective-permute-start | bytes 393224 | tf_op jit(solution)/shard_map/ppermute | solution.py:42
  55.4 0.8 %shard_map.90.refs_0_ = f32[2048,256]{1,0:T(8,128)S(1)} custom-call(bf16[2048,128]{1,0:T(8,128)(2,1)S(1)} %get-tuple-element.33.tag_ref, bf16[2048,256]{1,0:T(8,128)(2,1)S(1)} %copy-done.2, f32[1024,256]{1,0:T(8,128)S(1)} %shard_map.85.refs_0_, f32[1024,256]{1,0:T(8,128)S(1)} %shard_map.88.refs_10_.refs_1_, bf16[256,256]{1,0:T(8,128)(2,1)S(1)} %get-tuple-element.47.refs_2_, ...), custom_call_target="tpu_custom_call" | custom-call | flops 1024 | bytes 1024 | tf_op jit(solution)/shard_map/pallas_call | solution.py:26
  56.2 1.4 %shard_map.91.refs_0_ = f32[2048,256]{1,0:T(8,128)S(1)} custom-call(bf16[2048,128]{1,0:T(8,128)(2,1)S(1)} %get-tuple-element.33.tag_ref, bf16[2048,256]{1,0:T(8,128)(2,1)S(1)} %copy-done.2, f32[2048,256]{1,0:T(8,128)S(1)} %shard_map.90.refs_0_, bf16[256,256]{1,0:T(8,128)(2,1)S(1)} %collective-permute-done.15.refs_1_, ...), custom_call_target="tpu_custom_call" | custom-call | flops 1024 | bytes 1024 | tf_op jit(solution)/shard_map/pallas_call | solution.py:26
  57.6 1.8 %collective-permute-done.19.refs_1_ = bf16[256,256]{1,0:T(8,128)(2,1)S(1)} collective-permute-done((bf16[256,256]{1,0:T(8,128)(2,1)S(1)}, bf16[256,256]{1,0:T(8,128)(2,1)S(1)}, u32[]{:S(2)}, u32[]{:S(2)}) %collective-permute-start.19) | collective-permute-done | bytes 131104 | tf_op jit(solution)/shard_map/ppermute | solution.py:42
  59.7 1.7 %shard_map.92 = bf16[2048,256]{1,0:T(8,128)(2,1)} custom-call(bf16[2048,128]{1,0:T(8,128)(2,1)S(1)} %get-tuple-element.33.tag_ref, bf16[2048,256]{1,0:T(8,128)(2,1)S(1)} %copy-done.2, f32[2048,256]{1,0:T(8,128)S(1)} %shard_map.91.refs_0_, bf16[256,256]{1,0:T(8,128)(2,1)S(1)} %collective-permute-done.19.refs_1_, ...), custom_call_target="tpu_custom_call" | custom-call | flops 1024 | bytes 1024 | tf_op jit(solution)/shard_map/pallas_call | solution.py:26
  (40 shorter events, 1.9 us)
Async XLA Ops:
  0.0 5.8 %copy-start.4 = (s32[2048,1]{0,1:T(1,128)S(1)}, s32[2048,1]{0,1:T(1,128)}, u32[]{:S(2)}) copy-start(s32[2048,1]{0,1:T(1,128)} %param.9) | copy-start | bytes 24580
  0.0 5.8 %copy-start.1 = (bf16[2048,256]{1,0:T(8,128)(2,1)S(1)}, bf16[2048,256]{1,0:T(8,128)(2,1)}, u32[]{:S(2)}) copy-start(bf16[2048,256]{1,0:T(8,128)(2,1)} %basis_ref.6) | copy-start | bytes 3145732
  0.0 5.8 %copy-start = (bf16[2048,256]{1,0:T(8,128)(2,1)S(1)}, bf16[2048,256]{1,0:T(8,128)(2,1)}, u32[]{:S(2)}) copy-start(bf16[2048,256]{1,0:T(8,128)(2,1)} %fields_ref.3) | copy-start | bytes 3145732
  0.0 7.0 %copy-start.3 = (bf16[1,3,64,512]{3,2,1,0:T(8,128)(2,1)S(1)}, bf16[1,3,64,512]{3,2,1,0:T(8,128)(2,1)}, u32[]{:S(2)}) copy-start(bf16[1,3,64,512]{3,2,1,0:T(8,128)(2,1)} %param.12) | copy-start | bytes 589828
  2.7 12.6 %collective-permute-start = (bf16[3,256,256]{2,1,0:T(8,128)(2,1)S(1)}, bf16[3,256,256]{2,1,0:T(8,128)(2,1)S(1)}, u32[]{:S(2)}, u32[]{:S(2)}) collective-permute-start(bf16[3,256,256]{2,1,0:T(8,128)(2,1)S(1)} %shard_map.82), channel_id=1, source_target_pairs={{0,4},{4,0},{8,12},{12,8},{16,20},{20,16},{24,28},{28,24},{1,5},{5... | collective-permute-start | bytes 1179656 | tf_op jit(solution)/shard_map/ppermute | solution.py:42
  7.1 6.8 %collective-permute-start.1 = (bf16[3,64,512]{2,1,0:T(8,128)(2,1)S(1)}, bf16[3,64,512]{2,1,0:T(8,128)(2,1)S(1)}, u32[]{:S(2)}, u32[]{:S(2)}) collective-permute-start(bf16[3,64,512]{2,1,0:T(8,128)(2,1)S(1)} %bitcast.14), channel_id=1, source_target_pairs={{0,2},{1,3},{2,0},{3,1},{4,6},{5,7},{6,4},{7,5},{8,10},{9,11},{10,... | collective-permute-start | bytes 589832 | tf_op jit(solution)/shard_map/ppermute | solution.py:42
  8.7 5.2 %collective-permute-start.2 = (bf16[64,512]{1,0:T(8,128)(2,1)S(1)}, bf16[64,512]{1,0:T(8,128)(2,1)S(1)}, u32[]{:S(2)}, u32[]{:S(2)}) collective-permute-start(bf16[64,512]{1,0:T(8,128)(2,1)S(1)} %slice_bitcast_fusion.3), channel_id=1, source_target_pairs={{0,16},{4,20},{8,24},{12,28},{16,0},{20,4},{24,8},{28,12},{1,17},{... | collective-permute-start | bytes 196616 | tf_op jit(solution)/shard_map/ppermute | solution.py:42
  11.2 24.4 %collective-permute-start.4 = (bf16[3,64,512]{2,1,0:T(8,128)(2,1)S(1)}, bf16[3,64,512]{2,1,0:T(8,128)(2,1)S(1)}, u32[]{:S(2)}, u32[]{:S(2)}) collective-permute-start(bf16[3,64,512]{2,1,0:T(8,128)(2,1)S(1)} %bitcast.15), channel_id=1, source_target_pairs={{0,1},{1,0},{2,3},{3,2},{4,5},{5,4},{6,7},{7,6},{8,9},{9,8},{10,11... | collective-permute-start | bytes 589832 | tf_op jit(solution)/shard_map/ppermute | solution.py:42
  11.2 10.1 %copy-start.5 = (s32[8,7]{1,0:T(8,128)S(1)}, s32[8,7]{1,0:T(8,128)}, u32[]{:S(2)}) copy-start(s32[8,7]{1,0:T(8,128)} %index_ref.3) | copy-start | bytes 676
  11.2 10.1 %copy-start.6 = (s32[8]{0:T(128)S(1)}, s32[8]{0:T(128)}, u32[]{:S(2)}) copy-start(s32[8]{0:T(128)} %count_ref.3) | copy-start | bytes 100
  11.3 14.4 %collective-permute-start.3 = (bf16[1,256,256]{2,1,0:T(8,128)(2,1)S(1)}, bf16[1,256,256]{2,1,0:T(8,128)(2,1)S(1)}, u32[]{:S(2)}, u32[]{:S(2)}) collective-permute-start(bf16[1,256,256]{2,1,0:T(8,128)(2,1)S(1)} %get-tuple-element.35), channel_id=1, source_target_pairs={{0,4},{4,0},{8,12},{12,8},{16,20},{20,16},{24,28},{28,24},{1,5},{5... | collective-permute-start | bytes 393224 | tf_op jit(solution)/shard_map/ppermute | solution.py:42
  16.1 9.7 %collective-permute-start.6 = (bf16[256,256]{1,0:T(8,128)(2,1)S(1)}, bf16[256,256]{1,0:T(8,128)(2,1)S(1)}, u32[]{:S(2)}, u32[]{:S(2)}) collective-permute-start(bf16[256,256]{1,0:T(8,128)(2,1)S(1)} %get-tuple-element.51.rest_0_), channel_id=1, source_target_pairs={{0,24},{4,28},{8,16},{12,20},{16,8},{20,12},{24,0},{28,4},{1,25},{... | collective-permute-start | bytes 393224 | tf_op jit(solution)/shard_map/ppermute | solution.py:42
  20.7 9.0 %collective-permute-start.7 = (bf16[256,256]{1,0:T(8,128)(2,1)S(1)}, bf16[256,256]{1,0:T(8,128)(2,1)S(1)}, u32[]{:S(2)}, u32[]{:S(2)}) collective-permute-start(bf16[256,256]{1,0:T(8,128)(2,1)S(1)} %get-tuple-element.49), channel_id=1, source_target_pairs={{0,16},{4,20},{8,24},{12,28},{16,0},{20,4},{24,8},{28,12},{1,17},{... | collective-permute-start | bytes 393224 | tf_op jit(solution)/shard_map/ppermute | solution.py:42
  20.7 9.0 %collective-permute-start.8 = (bf16[256,256]{1,0:T(8,128)(2,1)S(1)}, bf16[256,256]{1,0:T(8,128)(2,1)S(1)}, u32[]{:S(2)}, u32[]{:S(2)}) collective-permute-start(bf16[256,256]{1,0:T(8,128)(2,1)S(1)} %get-tuple-element.50), channel_id=1, source_target_pairs={{0,8},{4,12},{8,0},{12,4},{16,24},{20,28},{24,16},{28,20},{1,9},{5... | collective-permute-start | bytes 393224 | tf_op jit(solution)/shard_map/ppermute | solution.py:42
  25.7 10.0 %collective-permute-start.5 = (bf16[3,64,512]{2,1,0:T(8,128)(2,1)S(1)}, bf16[3,64,512]{2,1,0:T(8,128)(2,1)S(1)}, u32[]{:S(2)}, u32[]{:S(2)}) collective-permute-start(bf16[3,64,512]{2,1,0:T(8,128)(2,1)S(1)} %collective-permute-done.1.refs_2_), channel_id=1, source_target_pairs={{0,1},{1,0},{2,3},{3,2},{4,5},{5,4},{6,7},{7,6},{8,9},{9,8},{10,11... | collective-permute-start | bytes 589832 | tf_op jit(solution)/shard_map/ppermute | solution.py:42
  29.8 5.8 %collective-permute-start.10 = (bf16[256,256]{1,0:T(8,128)(2,1)S(1)}, bf16[256,256]{1,0:T(8,128)(2,1)S(1)}, u32[]{:S(2)}, u32[]{:S(2)}) collective-permute-start(bf16[256,256]{1,0:T(8,128)(2,1)S(1)} %add_convert_fusion.1.refs_4_), channel_id=1, source_target_pairs={{0,4},{4,0},{8,12},{12,8},{16,20},{20,16},{24,28},{28,24},{1,5},{5... | collective-permute-start | bytes 393224 | tf_op jit(solution)/shard_map/ppermute | solution.py:42
  31.4 4.3 %collective-permute-start.9 = (bf16[64,512]{1,0:T(8,128)(2,1)S(1)}, bf16[64,512]{1,0:T(8,128)(2,1)S(1)}, u32[]{:S(2)}, u32[]{:S(2)}) collective-permute-start(bf16[64,512]{1,0:T(8,128)(2,1)S(1)} %collective-permute-done.2.refs_4_), channel_id=1, source_target_pairs={{0,2},{1,3},{2,0},{3,1},{4,6},{5,7},{6,4},{7,5},{8,10},{9,11},{10,... | collective-permute-start | bytes 196616 | tf_op jit(solution)/shard_map/ppermute | solution.py:42
  35.9 5.0 %collective-permute-start.13 = (bf16[256,256]{1,0:T(8,128)(2,1)S(1)}, bf16[256,256]{1,0:T(8,128)(2,1)S(1)}, u32[]{:S(2)}, u32[]{:S(2)}) collective-permute-start(bf16[256,256]{1,0:T(8,128)(2,1)S(1)} %shard_map.86.refs_4_), channel_id=1, source_target_pairs={{0,8},{4,12},{8,0},{12,4},{16,24},{20,28},{24,16},{28,20},{1,9},{5... | collective-permute-start | bytes 393224 | tf_op jit(solution)/shard_map/ppermute | solution.py:42
  36.0 1.3 %collective-permute-start.11 = (bf16[64,512]{1,0:T(8,128)(2,1)S(1)}, bf16[64,512]{1,0:T(8,128)(2,1)S(1)}, u32[]{:S(2)}, u32[]{:S(2)}) collective-permute-start(bf16[64,512]{1,0:T(8,128)(2,1)S(1)} %collective-permute-done.2.refs_4_), channel_id=1, source_target_pairs={{0,1},{1,0},{2,3},{3,2},{4,5},{5,4},{6,7},{7,6},{8,9},{9,8},{10,11... | collective-permute-start | bytes 196616 | tf_op jit(solution)/shard_map/ppermute | solution.py:42
  36.0 1.4 %collective-permute-start.12 = (bf16[64,512]{1,0:T(8,128)(2,1)S(1)}, bf16[64,512]{1,0:T(8,128)(2,1)S(1)}, u32[]{:S(2)}, u32[]{:S(2)}) collective-permute-start(bf16[64,512]{1,0:T(8,128)(2,1)S(1)} %collective-permute-done.9.refs_6_), channel_id=1, source_target_pairs={{0,1},{1,0},{2,3},{3,2},{4,5},{5,4},{6,7},{7,6},{8,9},{9,8},{10,11... | collective-permute-start | bytes 196616 | tf_op jit(solution)/shard_map/ppermute | solution.py:42
  41.1 6.9 %collective-permute-start.14 = (bf16[256,256]{1,0:T(8,128)(2,1)S(1)}, bf16[256,256]{1,0:T(8,128)(2,1)S(1)}, u32[]{:S(2)}, u32[]{:S(2)}) collective-permute-start(bf16[256,256]{1,0:T(8,128)(2,1)S(1)} %shard_map.87.rest_0_.refs_8_), channel_id=1, source_target_pairs={{0,16},{4,20},{8,24},{12,28},{16,0},{20,4},{24,8},{28,12},{1,17},{... | collective-permute-start | bytes 393224 | tf_op jit(solution)/shard_map/ppermute | solution.py:42
  46.5 8.9 %copy-start.2 = (bf16[2048,256]{1,0:T(8,128)(2,1)S(1)}, bf16[2048,256]{1,0:T(8,128)(2,1)}, u32[]{:S(2)}) copy-start(bf16[2048,256]{1,0:T(8,128)(2,1)} %basis_ref.9) | copy-start | bytes 3145732
  48.3 6.1 %collective-permute-start.16 = (bf16[256,256]{1,0:T(8,128)(2,1)S(1)}, bf16[256,256]{1,0:T(8,128)(2,1)S(1)}, u32[]{:S(2)}, u32[]{:S(2)}) collective-permute-start(bf16[256,256]{1,0:T(8,128)(2,1)S(1)} %get-tuple-element.47.refs_2_), channel_id=1, source_target_pairs={{0,8},{4,12},{8,0},{12,4},{16,24},{20,28},{24,16},{28,20},{1,9},{5... | collective-permute-start | bytes 393224 | tf_op jit(solution)/shard_map/ppermute | solution.py:42
  48.9 5.7 %collective-permute-start.17 = (bf16[256,256]{1,0:T(8,128)(2,1)S(1)}, bf16[256,256]{1,0:T(8,128)(2,1)S(1)}, u32[]{:S(2)}, u32[]{:S(2)}) collective-permute-start(bf16[256,256]{1,0:T(8,128)(2,1)S(1)} %get-tuple-element.48.refs_3_), channel_id=1, source_target_pairs={{0,4},{4,0},{8,12},{12,8},{16,20},{20,16},{24,28},{28,24},{1,5},{5... | collective-permute-start | bytes 393224 | tf_op jit(solution)/shard_map/ppermute | solution.py:42
  49.6 6.6 %collective-permute-start.15 = (bf16[256,256]{1,0:T(8,128)(2,1)S(1)}, bf16[256,256]{1,0:T(8,128)(2,1)S(1)}, u32[]{:S(2)}, u32[]{:S(2)}) collective-permute-start(bf16[256,256]{1,0:T(8,128)(2,1)S(1)} %get-tuple-element.47.refs_2_), channel_id=1, source_target_pairs={{0,4},{4,0},{8,12},{12,8},{16,20},{20,16},{24,28},{28,24},{1,5},{5... | collective-permute-start | bytes 393224 | tf_op jit(solution)/shard_map/ppermute | solution.py:42
  51.0 5.3 %collective-permute-start.18 = (bf16[256,256]{1,0:T(8,128)(2,1)S(1)}, bf16[256,256]{1,0:T(8,128)(2,1)S(1)}, u32[]{:S(2)}, u32[]{:S(2)}) collective-permute-start(bf16[256,256]{1,0:T(8,128)(2,1)S(1)} %get-tuple-element.48.refs_3_), channel_id=1, source_target_pairs={{0,8},{4,12},{8,0},{12,4},{16,24},{20,28},{24,16},{28,20},{1,9},{5... | collective-permute-start | bytes 393224 | tf_op jit(solution)/shard_map/ppermute | solution.py:42
  54.5 5.0 %collective-permute-start.19 = (bf16[256,256]{1,0:T(8,128)(2,1)S(1)}, bf16[256,256]{1,0:T(8,128)(2,1)S(1)}, u32[]{:S(2)}, u32[]{:S(2)}) collective-permute-start(bf16[256,256]{1,0:T(8,128)(2,1)S(1)} %collective-permute-done.16.refs_2_), channel_id=1, source_target_pairs={{0,4},{4,0},{8,12},{12,8},{16,20},{20,16},{24,28},{28,24},{1,5},{5... | collective-permute-start | bytes 393224 | tf_op jit(solution)/shard_map/ppermute | solution.py:42
  54.7 5.0 %collective-permute-start.20 = (bf16[256,256]{1,0:T(8,128)(2,1)S(1)}, bf16[256,256]{1,0:T(8,128)(2,1)S(1)}, u32[]{:S(2)}, u32[]{:S(2)}) collective-permute-start(bf16[256,256]{1,0:T(8,128)(2,1)S(1)} %collective-permute-done.17.refs_3_), channel_id=1, source_target_pairs={{0,8},{4,12},{8,0},{12,4},{16,24},{20,28},{24,16},{28,20},{1,9},{5... | collective-permute-start | bytes 393224 | tf_op jit(solution)/shard_map/ppermute | solution.py:42

commit v5 on v4

--- a/solution.py
+++ b/solution.py
@@ -150,24 +150,47 @@
         out[pl.ds(start, size), :] = product[o * size : (o + 1) * size].astype(out.dtype)
 
 
-def level_kernel(n_rhs, n_out, level, me_ref, *refs):
-    rows, (own_ref, other_ref) = refs[: n_rhs * n_out], refs[n_rhs * n_out :][:2]
-    outs = refs[-n_out:]
-    own, other = own_ref[...], other_ref[...]
-    for k, out in enumerate(outs):
-        pieces = [ref[level] if k == 0 else ref[...] for ref in rows[k * n_rhs :][:n_rhs]]
-        stacked = jnp.concatenate([other, own] if k else [own, other], axis=0)
-        apply_rows(me_ref[0], pieces, stacked, out)
-
-
-def next_level(rhs_me, level, rows, own, other, other_rows=(), after=()):
-    n_out = 2 if other_rows else 1
+def first_levels_kernel(n_rhs, me_ref, *refs):
+    rows, pair_rows = refs[:n_rhs], refs[n_rhs : 2 * n_rhs]
+    own_ref, low_ref, mid_ref, both_ref, out_ref, held_ref = refs[2 * n_rhs :]
+    stacked = jnp.concatenate([own_ref[...], low_ref[...]], axis=0)
+    apply_rows(me_ref[0], [ref[0] for ref in rows], stacked, held_ref.at[0])
+    stacked = jnp.concatenate([mid_ref[...], both_ref[...]], axis=0)
+    apply_rows(me_ref[0], [ref[0] for ref in pair_rows], stacked, held_ref.at[1])
+    stacked = jnp.concatenate([held_ref[0], held_ref[1]], axis=0)
+    apply_rows(me_ref[0], [ref[1] for ref in rows], stacked, out_ref)
+
+
+def first_levels(rhs_me, rows, pair_rows, values):
+    shape = values[0].shape
+    (out,) = call(
+        functools.partial(first_levels_kernel, len(rows)),
+        [jax.ShapeDtypeStruct(shape, BF16)],
+        (rhs_me, *rows, *pair_rows, *values),
+        [SMEM] + [VMEM] * (2 * len(rows) + len(values)),
+        [pltpu.VMEM],
+        [pltpu.VMEM((2,) + shape, BF16)],
+    )
+    return out
+
+
+def last_level_kernel(n_rhs, me_ref, *refs):
+    rows, pair_rows = refs[:n_rhs], refs[n_rhs : 2 * n_rhs]
+    own, other = [ref[...] for ref in refs[2 * n_rhs :][:2]]
+    level = rows[0].shape[0] - 1
+    stacked = jnp.concatenate([own, other], axis=0)
+    apply_rows(me_ref[0], [ref[level] for ref in rows], stacked, refs[-2])
+    stacked = jnp.concatenate([other, own], axis=0)
+    apply_rows(me_ref[0], [ref[1] for ref in pair_rows], stacked, refs[-1])
+
+
+def last_level(rhs_me, rows, pair_rows, own, other, after):
     return call(
-        functools.partial(level_kernel, len(rows), n_out, level),
-        [jax.ShapeDtypeStruct(own.shape, BF16)] * n_out,
-        (rhs_me, *rows, *other_rows, own, other),
-        [SMEM] + [VMEM] * (len(rows) * n_out + 2),
-        [pltpu.VMEM] * n_out,
+        functools.partial(last_level_kernel, len(rows)),
+        [jax.ShapeDtypeStruct(own.shape, BF16)] * 2,
+        (rhs_me, *rows, *pair_rows, own, other),
+        [SMEM] + [VMEM] * (2 * len(rows) + 2),
+        [pltpu.VMEM] * 2,
         (),
         after,
     )
@@ -246,7 +269,7 @@
     rhs_me = lax.axis_index("rhs").astype(jnp.int32)[None]
     owner_row = owner.reshape(1, rows)
 
-    parts = [list(range(upper - 1, 0, -1)), [0]]
+    parts = [list(range(upper - 1, upper // 2 - 1, -1)), list(range(upper // 2 - 1, -1, -1))]
 
     def groups(low):
         return [[o * group + 2 * s + low for s in part for o in range(outer)] for part in parts]
@@ -271,42 +294,38 @@
         return sums
 
     transfer, keep[0] = tie(transfer, keep[0])
-    top = group // 2
+    low, mid, top = 1, 2, group // 2
     far_rhs = n_rhs // 2
-    mine_rows = {0: transfer[0]}
-    mine_rows[far_rhs] = swapped(mine_rows[0], "rhs", far_rhs)
-    their_rows = {0: swapped(transfer[0, -1], "leaf", top)}
-    got[0], mine_rows[far_rhs], their_rows[0] = tie(got[0], mine_rows[far_rhs], their_rows[0])
+    mine_rows = {0: transfer[0], far_rhs: swapped(transfer[0], "rhs", far_rhs)}
+    pair = [swapped(transfer[0, 0], "leaf", mid), swapped(transfer[0, -1], "leaf", top)]
 
     sums = [v.astype(BF16) for v in reduced(keep[0], got[0], parts[0])]
     arrived = [swapped(v, "leaf", 2 * s) for s, v in zip(parts[0], sums)]
     more, tag = compress(*operands, fields, even[1:], [F32], tagged_compress_kernel, sums[:1])
-    keep.append(more)
-    (total,) = reduced(keep[1], got[1], parts[1])
+    got[1], mine_rows[0], mine_rows[far_rhs], *pair = tie(
+        got[1], mine_rows[0], mine_rows[far_rhs], *pair
+    )
+    pair_rows = {0: jnp.stack(pair)}
+    pair_rows[far_rhs] = swapped(pair_rows[0], "rhs", far_rhs)
+    *near_sums, total = reduced(more, got[1], parts[1])
+    for s, v in zip(parts[1], near_sums):
+        arrived.append(swapped(v.astype(BF16), "leaf", 2 * s))
     half = near_blocks.shape[0] // 2
     near = [near_field(near_index, near_count, near_blocks, fields, 0, half, sums[:1])]
     mine_rows = across(mine_rows, far_rhs // 2)
     order = sorted(mine_rows)
-    total, near[0] = tie(total, near[0])
-
-    for value in arrived:
+    total, near[0], pair_rows[far_rhs] = tie(total, near[0], pair_rows[far_rhs])
+
+    for value in arrived[len(sums) :] + arrived[: len(sums)]:
         total = total + value.astype(F32)
     coefficients = total.astype(BF16)
-    for level in range(levels - 1):
-        other = swapped(coefficients, "leaf", 2**level)
-        if level == 0:
-            their_rows[far_rhs] = swapped(their_rows[0], "rhs", far_rhs)
-            coefficients, their_rows[far_rhs] = tie(coefficients, their_rows[far_rhs])
-        if level == 1:
-            their_rows = across(their_rows, far_rhs // 2)
-            coefficients, *values = tie(coefficients, *[their_rows[o] for o in order])
-            their_rows = dict(zip(order, values))
-        rows = [mine_rows[o] for o in order]
-        (coefficients,) = next_level(rhs_me, level, rows, coefficients, other)
+    values = [swapped(coefficients, "leaf", mask) for mask in (low, mid, low ^ mid)]
+    pair_rows = across(pair_rows, far_rhs // 2)
+    rows, pair_rows = [[r[o] for o in order] for r in (mine_rows, pair_rows)]
+    coefficients = first_levels(rhs_me, rows, pair_rows, [coefficients] + values)
     other = swapped(coefficients, "leaf", top)
     near.append(near_field(near_index, near_count, near_blocks, fields, half, half, [coefficients]))
-    rows, more = [mine_rows[o] for o in order], [their_rows[o] for o in order]
-    own = next_level(rhs_me, levels - 1, rows, coefficients, other, more, near[1:])
+    own = last_level(rhs_me, rows, pair_rows, coefficients, other, near[1:])
 
     def add_far(base, known, last=False):
         ids = [o * group + j for j in sorted(known) for o in range(outer)]
@@ -316,9 +335,8 @@
         return far_field(ids, tag, field_basis, base, blocks, last)
 
     known = {0: own[0], top: own[1]}
-    steps = [1 << k for k in range(levels - 1)]
     total = near
-    low, high = steps
+    high = mid
     from_low = {j ^ low: swapped(v, "leaf", low) for j, v in known.items()}
     from_high = {j ^ high: swapped(v, "leaf", high) for j, v in known.items()}
     total = [add_far(total, known)]

time: 61.5 us -> 60.7 us (0.987)
  waiting for transfers between devices: 20.4 us -> 14.5 us
  starting transfers between devices: 22.7 us -> 27.7 us
    ppermute x21 -> x23, waiting for transfers between devices: 20.4 us -> 14.5 us  [swapped(): lax.ppermute(value, axis, [(i, i ^ mask) for i in range(lax.axis_size(axi...]
    ppermute x21 -> x23, starting transfers between devices: 22.7 us -> 27.7 us  [swapped(): lax.ppermute(value, axis, [(i, i ^ mask) for i in range(lax.axis_size(axi...]
    pallas_call x11 -> x10, Pallas kernels: 17.7 us -> 17.9 us  [call(): pl.pallas_call(kernel, out_shape=[space(s.shape, s.dtype) for s, space in...]
  transfers between devices with their start and end apart: 21 -> 23, of which waited for: 12 -> 10; matrix products, arithmetic and copies ran while one was open for 0% -> 0% of each run, Pallas kernels for 21% -> 21%
where the time goes in v5:
time: 60.7 us; the launch traced here: 60.6 us
  starting transfers between devices  27.7 us (46%)
  Pallas kernels  17.9 us (29%)
  waiting for transfers between devices  14.5 us (24%)
    ppermute x23, starting transfers between devices, swapped(): lax.ppermute(value, axis, [(i, i ^ mask) for i in range(lax.axis_size(axi...  27.7 us
    pallas_call x10, Pallas kernels, call(): pl.pallas_call(kernel, out_shape=[space(s.shape, s.dtype) for s, space in...  17.9 us
    ppermute x23, waiting for transfers between devices, swapped(): lax.ppermute(value, axis, [(i, i ^ mask) for i in range(lax.axis_size(axi...  14.5 us
  transfers between devices with their start and end apart: 23, of which 10 were waited for; matrix products, arithmetic and copies ran while one was open for 0% of the time, Pallas kernels for 21%

profile of v5, /device:TPU:0, one launch (start us, length us, event | category | flops | bytes accessed | tf_op | source)
XLA Modules:
  0.0 60.6 jit_solution(13375826448709201)
XLA Ops:
  0.0 2.4 %shard_map.82 = bf16[2,256,256]{2,1,0:T(8,128)(2,1)S(1)} custom-call(s32[1]{0:T(128)} %bitcast.me_ref, s32[1,2048]{1,0:T(1,128)} %bitcast.22, bf16[2048,256]{1,0:T(8,128)(2,1)} %basis_ref.6, bf16[2048,256]{1,0:T(8,128)(2,1)} %fields_ref.3, s32[1]{0:T(128)} %bitcast.2.rest_0_.me_ref), custom_call_target="tpu_custom_call" | custom-call | flops 1024 | bytes 1024 | tf_op jit(solution)/shard_map/pallas_call | solution.py:26
  2.5 3.0 %collective-permute-start = (bf16[2,256,256]{2,1,0:T(8,128)(2,1)S(1)}, bf16[2,256,256]{2,1,0:T(8,128)(2,1)S(1)}, u32[]{:S(2)}, u32[]{:S(2)}) collective-permute-start(bf16[2,256,256]{2,1,0:T(8,128)(2,1)S(1)} %shard_map.82), channel_id=1, source_target_pairs={{0,4},{4,0},{8,12},{12,8},{16,20},{20,16},{24,28},{28,24},{1,5},{5... | collective-permute-start | bytes 786440 | tf_op jit(solution)/shard_map/ppermute | solution.py:42
  5.5 1.3 %shard_map.83 = (f32[2,256,256]{2,1,0:T(8,128)S(1)}, bf16[2,256,256]{2,1,0:T(8,128)(2,1)S(1)}) custom-call(s32[1]{0:T(128)} %bitcast.me_ref, s32[1,2048]{1,0:T(1,128)S(1)} %bitcast.23, bf16[2048,256]{1,0:T(8,128)(2,1)S(1)} %copy-done.1, bf16[2048,256]{1,0:T(8,128)(2,1)S(1)} %copy-done), custom_call_target="tpu_custom_call" | custom-call | flops 1024 | bytes 1024 | tf_op jit(solution)/shard_map/pallas_call | solution.py:26
  6.8 1.6 %collective-permute-start.3 = (bf16[64,512]{1,0:T(8,128)(2,1)S(1)}, bf16[64,512]{1,0:T(8,128)(2,1)S(1)}, u32[]{:S(2)}, u32[]{:S(2)}) collective-permute-start(bf16[64,512]{1,0:T(8,128)(2,1)S(1)} %get-tuple-element.44), channel_id=1, source_target_pairs={{0,8},{4,12},{8,0},{12,4},{16,24},{20,28},{24,16},{28,20},{1,9},{5... | collective-permute-start | bytes 196616 | tf_op jit(solution)/shard_map/ppermute | solution.py:42
  8.4 2.6 %collective-permute-start.4 = (bf16[64,512]{1,0:T(8,128)(2,1)S(1)}, bf16[64,512]{1,0:T(8,128)(2,1)S(1)}, u32[]{:S(2)}, u32[]{:S(2)}) collective-permute-start(bf16[64,512]{1,0:T(8,128)(2,1)S(1)} %get-tuple-element.43), channel_id=1, source_target_pairs={{0,16},{4,20},{8,24},{12,28},{16,0},{20,4},{24,8},{28,12},{1,17},{... | collective-permute-start | bytes 196616 | tf_op jit(solution)/shard_map/ppermute | solution.py:42
  11.0 1.5 %collective-permute-start.2 = (bf16[3,64,512]{2,1,0:T(8,128)(2,1)S(1)}, bf16[3,64,512]{2,1,0:T(8,128)(2,1)S(1)}, u32[]{:S(2)}, u32[]{:S(2)}) collective-permute-start(bf16[3,64,512]{2,1,0:T(8,128)(2,1)S(1)} %bitcast.18), channel_id=1, source_target_pairs={{0,2},{1,3},{2,0},{3,1},{4,6},{5,7},{6,4},{7,5},{8,10},{9,11},{10,... | collective-permute-start | bytes 589832 | tf_op jit(solution)/shard_map/ppermute | solution.py:42
  13.2 0.7 %shard_map.84 = (f32[2,256,256]{2,1,0:T(8,128)S(1)}, bf16[2048,128]{1,0:T(8,128)(2,1)S(1)}) custom-call(s32[1]{0:T(128)} %bitcast.me_ref, s32[1,2048]{1,0:T(1,128)S(1)} %bitcast.24, bf16[2048,256]{1,0:T(8,128)(2,1)S(1)} %copy-done.1, bf16[2048,256]{1,0:T(8,128)(2,1)S(1)} %copy-done, bf16[256,256]{1,0:T(8,128)(2,1)S(1)} %get-tuple-element.42.rest_0_), custom_call_target="tpu_custom_call" | custom-call | flops 1024 | bytes 1024 | tf_op jit(solution)/shard_map/pallas_call | solution.py:26
  14.0 3.8 %collective-permute-start.11 = (bf16[256,256]{1,0:T(8,128)(2,1)S(1)}, bf16[256,256]{1,0:T(8,128)(2,1)S(1)}, u32[]{:S(2)}, u32[]{:S(2)}) collective-permute-start(bf16[256,256]{1,0:T(8,128)(2,1)S(1)} %get-tuple-element.42.rest_0_), channel_id=1, source_target_pairs={{0,24},{4,28},{8,16},{12,20},{16,8},{20,12},{24,0},{28,4},{1,25},{... | collective-permute-start | bytes 393224 | tf_op jit(solution)/shard_map/ppermute | solution.py:42
  17.7 1.7 %collective-permute-done.1 = bf16[2,256,256]{2,1,0:T(8,128)(2,1)S(1)} collective-permute-done((bf16[2,256,256]{2,1,0:T(8,128)(2,1)S(1)}, bf16[2,256,256]{2,1,0:T(8,128)(2,1)S(1)}, u32[]{:S(2)}, u32[]{:S(2)}) %collective-permute-start.1) | collective-permute-done | bytes 262176 | tf_op jit(solution)/shard_map/ppermute | solution.py:42
  19.5 0.6 collective-permute-start.5
  20.2 0.8 %collective-permute-start.10 = (bf16[256,256]{1,0:T(8,128)(2,1)S(1)}, bf16[256,256]{1,0:T(8,128)(2,1)S(1)}, u32[]{:S(2)}, u32[]{:S(2)}) collective-permute-start(bf16[256,256]{1,0:T(8,128)(2,1)S(1)} %fusion), channel_id=1, source_target_pairs={{0,8},{4,12},{8,0},{12,4},{16,24},{20,28},{24,16},{28,20},{1,9},{5... | collective-permute-start | bytes 393224 | tf_op jit(solution)/shard_map/ppermute | solution.py:42
  21.0 2.6 %collective-permute-start.12 = (bf16[256,256]{1,0:T(8,128)(2,1)S(1)}, bf16[256,256]{1,0:T(8,128)(2,1)S(1)}, u32[]{:S(2)}, u32[]{:S(2)}) collective-permute-start(bf16[256,256]{1,0:T(8,128)(2,1)S(1)} %get-tuple-element.41), channel_id=1, source_target_pairs={{0,16},{4,20},{8,24},{12,28},{16,0},{20,4},{24,8},{28,12},{1,17},{... | collective-permute-start | bytes 393224 | tf_op jit(solution)/shard_map/ppermute | solution.py:42
  23.6 4.3 %shard_map.85.refs_0_ = f32[1024,256]{1,0:T(8,128)S(1)} custom-call(s32[8,7]{1,0:T(8,128)S(1)} %copy-done.5, s32[8]{0:T(128)S(1)} %copy-done.6, bf16[8,7,256,256]{3,2,1,0:T(8,128)(2,1)} %blocks_hbm.3, bf16[2048,256]{1,0:T(8,128)(2,1)S(1)} %copy-done, bf16[256,256]{1,0:T(8,128)(2,1)S(1)} %get-tuple-element.42.rest_0_), custom_call_target="tpu_custom_call" | custom-call | flops 1024 | bytes 1024 | tf_op jit(solution)/shard_map/pallas_call | solution.py:26
  28.0 0.8 %collective-permute-done.10 = bf16[256,256]{1,0:T(8,128)(2,1)S(1)} collective-permute-done((bf16[256,256]{1,0:T(8,128)(2,1)S(1)}, bf16[256,256]{1,0:T(8,128)(2,1)S(1)}, u32[]{:S(2)}, u32[]{:S(2)}) %collective-permute-start.10) | collective-permute-done | bytes 131104 | tf_op jit(solution)/shard_map/ppermute | solution.py:42
  28.8 1.5 %collective-permute-done.12 = bf16[256,256]{1,0:T(8,128)(2,1)S(1)} collective-permute-done((bf16[256,256]{1,0:T(8,128)(2,1)S(1)}, bf16[256,256]{1,0:T(8,128)(2,1)S(1)}, u32[]{:S(2)}, u32[]{:S(2)}) %collective-permute-start.12) | collective-permute-done | bytes 131104 | tf_op jit(solution)/shard_map/ppermute | solution.py:42
  30.4 1.6 %collective-permute-start.13 = (bf16[256,256]{1,0:T(8,128)(2,1)S(1)}, bf16[256,256]{1,0:T(8,128)(2,1)S(1)}, u32[]{:S(2)}, u32[]{:S(2)}) collective-permute-start(bf16[256,256]{1,0:T(8,128)(2,1)S(1)} %add_convert_fusion.1.refs_8_), channel_id=1, source_target_pairs={{0,4},{4,0},{8,12},{12,8},{16,20},{20,16},{24,28},{28,24},{1,5},{5... | collective-permute-start | bytes 393224 | tf_op jit(solution)/shard_map/ppermute | solution.py:42
  32.4 1.5 %collective-permute-start.15 = (bf16[256,256]{1,0:T(8,128)(2,1)S(1)}, bf16[256,256]{1,0:T(8,128)(2,1)S(1)}, u32[]{:S(2)}, u32[]{:S(2)}) collective-permute-start(bf16[256,256]{1,0:T(8,128)(2,1)S(1)} %add_convert_fusion.1.refs_8_), channel_id=1, source_target_pairs={{0,12},{4,8},{8,4},{12,0},{16,28},{20,24},{24,20},{28,16},{1,13},{... | collective-permute-start | bytes 393224 | tf_op jit(solution)/shard_map/ppermute | solution.py:42
  34.0 2.3 %collective-permute-done.13.refs_9_ = bf16[256,256]{1,0:T(8,128)(2,1)S(1)} collective-permute-done((bf16[256,256]{1,0:T(8,128)(2,1)S(1)}, bf16[256,256]{1,0:T(8,128)(2,1)S(1)}, u32[]{:S(2)}, u32[]{:S(2)}) %collective-permute-start.13) | collective-permute-done | bytes 131104 | tf_op jit(solution)/shard_map/ppermute | solution.py:42
  36.3 0.7 %collective-permute-done.14.refs_10_ = bf16[256,256]{1,0:T(8,128)(2,1)S(1)} collective-permute-done((bf16[256,256]{1,0:T(8,128)(2,1)S(1)}, bf16[256,256]{1,0:T(8,128)(2,1)S(1)}, u32[]{:S(2)}, u32[]{:S(2)}) %collective-permute-start.14) | collective-permute-done | bytes 131104 | tf_op jit(solution)/shard_map/ppermute | solution.py:42
  37.0 2.3 %collective-permute-done.15.refs_11_ = bf16[256,256]{1,0:T(8,128)(2,1)S(1)} collective-permute-done((bf16[256,256]{1,0:T(8,128)(2,1)S(1)}, bf16[256,256]{1,0:T(8,128)(2,1)S(1)}, u32[]{:S(2)}, u32[]{:S(2)}) %collective-permute-start.15) | collective-permute-done | bytes 131104 | tf_op jit(solution)/shard_map/ppermute | solution.py:42
  39.3 0.7 %shard_map.86.rest_0_.refs_8_ = bf16[256,256]{1,0:T(8,128)(2,1)S(1)} custom-call(s32[1]{0:T(128)} %bitcast.2.rest_0_.me_ref, bf16[3,64,512]{2,1,0:T(8,128)(2,1)S(1)} %bitcast.20, bf16[3,64,512]{2,1,0:T(8,128)(2,1)S(1)} %collective-permute-done.6.refs_1_, bf16[3,64,512]{2,1,0:T(8,128)(2,1)S(1)} %collective-permute-done.2.refs_2_, ...), custom_call_target="tpu_custom_call" | custom-call | flops 1024 | bytes 1024 | tf_op jit(solution)/shard_map/pallas_call | solution.py:26
  39.9 1.7 %collective-permute-start.16 = (bf16[256,256]{1,0:T(8,128)(2,1)S(1)}, bf16[256,256]{1,0:T(8,128)(2,1)S(1)}, u32[]{:S(2)}, u32[]{:S(2)}) collective-permute-start(bf16[256,256]{1,0:T(8,128)(2,1)S(1)} %shard_map.86.rest_0_.refs_8_), channel_id=1, source_target_pairs={{0,16},{4,20},{8,24},{12,28},{16,0},{20,4},{24,8},{28,12},{1,17},{... | collective-permute-start | bytes 393224 | tf_op jit(solution)/shard_map/ppermute | solution.py:42
  41.6 4.3 %shard_map.87.refs_10_.refs_1_ = f32[1024,256]{1,0:T(8,128)S(1)} custom-call(s32[8,7]{1,0:T(8,128)S(1)} %copy-done.5, s32[8]{0:T(128)S(1)} %copy-done.6, bf16[8,7,256,256]{3,2,1,0:T(8,128)(2,1)} %blocks_hbm.3, bf16[2048,256]{1,0:T(8,128)(2,1)S(1)} %copy-done, bf16[256,256]{1,0:T(8,128)(2,1)S(1)} %shard_map.86.rest_0_.refs_8_), custom_call_target="tpu_custom_call" | custom-call | flops 1024 | bytes 1024 | tf_op jit(solution)/shard_map/pallas_call | solution.py:26
  45.9 1.3 %collective-permute-done.16.refs_9_ = bf16[256,256]{1,0:T(8,128)(2,1)S(1)} collective-permute-done((bf16[256,256]{1,0:T(8,128)(2,1)S(1)}, bf16[256,256]{1,0:T(8,128)(2,1)S(1)}, u32[]{:S(2)}, u32[]{:S(2)}) %collective-permute-start.16) | collective-permute-done | bytes 131104 | tf_op jit(solution)/shard_map/ppermute | solution.py:42
  47.8 1.5 %collective-permute-start.19 = (bf16[256,256]{1,0:T(8,128)(2,1)S(1)}, bf16[256,256]{1,0:T(8,128)(2,1)S(1)}, u32[]{:S(2)}, u32[]{:S(2)}) collective-permute-start(bf16[256,256]{1,0:T(8,128)(2,1)S(1)} %get-tuple-element.40.refs_3_), channel_id=1, source_target_pairs={{0,4},{4,0},{8,12},{12,8},{16,20},{20,16},{24,28},{28,24},{1,5},{5... | collective-permute-start | bytes 393224 | tf_op jit(solution)/shard_map/ppermute | solution.py:42
  49.8 1.9 %collective-permute-start.20 = (bf16[256,256]{1,0:T(8,128)(2,1)S(1)}, bf16[256,256]{1,0:T(8,128)(2,1)S(1)}, u32[]{:S(2)}, u32[]{:S(2)}) collective-permute-start(bf16[256,256]{1,0:T(8,128)(2,1)S(1)} %get-tuple-element.40.refs_3_), channel_id=1, source_target_pairs={{0,8},{4,12},{8,0},{12,4},{16,24},{20,28},{24,16},{28,20},{1,9},{5... | collective-permute-start | bytes 393224 | tf_op jit(solution)/shard_map/ppermute | solution.py:42
  51.7 1.9 %collective-permute-done.18.refs_2_ = bf16[256,256]{1,0:T(8,128)(2,1)S(1)} collective-permute-done((bf16[256,256]{1,0:T(8,128)(2,1)S(1)}, bf16[256,256]{1,0:T(8,128)(2,1)S(1)}, u32[]{:S(2)}, u32[]{:S(2)}) %collective-permute-start.18) | collective-permute-done | bytes 131104 | tf_op jit(solution)/shard_map/ppermute | solution.py:42
  53.9 0.8 %collective-permute-start.22 = (bf16[256,256]{1,0:T(8,128)(2,1)S(1)}, bf16[256,256]{1,0:T(8,128)(2,1)S(1)}, u32[]{:S(2)}, u32[]{:S(2)}) collective-permute-start(bf16[256,256]{1,0:T(8,128)(2,1)S(1)} %collective-permute-done.19.refs_3_), channel_id=1, source_target_pairs={{0,8},{4,12},{8,0},{12,4},{16,24},{20,28},{24,16},{28,20},{1,9},{5... | collective-permute-start | bytes 393224 | tf_op jit(solution)/shard_map/ppermute | solution.py:42
  54.8 0.8 %shard_map.89.refs_0_ = f32[2048,256]{1,0:T(8,128)S(1)} custom-call(bf16[2048,128]{1,0:T(8,128)(2,1)S(1)} %get-tuple-element.27.tag_ref, bf16[2048,256]{1,0:T(8,128)(2,1)S(1)} %copy-done.2, f32[1024,256]{1,0:T(8,128)S(1)} %shard_map.85.refs_0_, f32[1024,256]{1,0:T(8,128)S(1)} %shard_map.87.refs_10_.refs_1_, bf16[256,256]{1,0:T(8,128)(2,1)S(1)} %get-tuple-element.39.refs_2_, ...), custom_call_target="tpu_custom_call" | custom-call | flops 1024 | bytes 1024 | tf_op jit(solution)/shard_map/pallas_call | solution.py:26
  55.6 1.4 %shard_map.90.refs_0_ = f32[2048,256]{1,0:T(8,128)S(1)} custom-call(bf16[2048,128]{1,0:T(8,128)(2,1)S(1)} %get-tuple-element.27.tag_ref, bf16[2048,256]{1,0:T(8,128)(2,1)S(1)} %copy-done.2, f32[2048,256]{1,0:T(8,128)S(1)} %shard_map.89.refs_0_, bf16[256,256]{1,0:T(8,128)(2,1)S(1)} %collective-permute-done.17.refs_1_, ...), custom_call_target="tpu_custom_call" | custom-call | flops 1024 | bytes 1024 | tf_op jit(solution)/shard_map/pallas_call | solution.py:26
  57.1 1.5 %collective-permute-done.21.refs_1_ = bf16[256,256]{1,0:T(8,128)(2,1)S(1)} collective-permute-done((bf16[256,256]{1,0:T(8,128)(2,1)S(1)}, bf16[256,256]{1,0:T(8,128)(2,1)S(1)}, u32[]{:S(2)}, u32[]{:S(2)}) %collective-permute-start.21) | collective-permute-done | bytes 131104 | tf_op jit(solution)/shard_map/ppermute | solution.py:42
  58.9 1.7 %shard_map.91 = bf16[2048,256]{1,0:T(8,128)(2,1)} custom-call(bf16[2048,128]{1,0:T(8,128)(2,1)S(1)} %get-tuple-element.27.tag_ref, bf16[2048,256]{1,0:T(8,128)(2,1)S(1)} %copy-done.2, f32[2048,256]{1,0:T(8,128)S(1)} %shard_map.90.refs_0_, bf16[256,256]{1,0:T(8,128)(2,1)S(1)} %collective-permute-done.21.refs_1_, ...), custom_call_target="tpu_custom_call" | custom-call | flops 1024 | bytes 1024 | tf_op jit(solution)/shard_map/pallas_call | solution.py:26
  (46 shorter events, 3.0 us)
Async XLA Ops:
  0.0 5.5 %copy-start.4 = (s32[2048,1]{0,1:T(1,128)S(1)}, s32[2048,1]{0,1:T(1,128)}, u32[]{:S(2)}) copy-start(s32[2048,1]{0,1:T(1,128)} %param.9) | copy-start | bytes 24580
  0.0 5.5 %copy-start.1 = (bf16[2048,256]{1,0:T(8,128)(2,1)S(1)}, bf16[2048,256]{1,0:T(8,128)(2,1)}, u32[]{:S(2)}) copy-start(bf16[2048,256]{1,0:T(8,128)(2,1)} %basis_ref.6) | copy-start | bytes 3145732
  0.0 5.5 %copy-start = (bf16[2048,256]{1,0:T(8,128)(2,1)S(1)}, bf16[2048,256]{1,0:T(8,128)(2,1)}, u32[]{:S(2)}) copy-start(bf16[2048,256]{1,0:T(8,128)(2,1)} %fields_ref.3) | copy-start | bytes 3145732
  0.0 6.8 %copy-start.3 = (bf16[1,3,64,512]{3,2,1,0:T(8,128)(2,1)S(1)}, bf16[1,3,64,512]{3,2,1,0:T(8,128)(2,1)}, u32[]{:S(2)}) copy-start(bf16[1,3,64,512]{3,2,1,0:T(8,128)(2,1)} %param.12) | copy-start | bytes 589828
  2.5 10.6 %collective-permute-start = (bf16[2,256,256]{2,1,0:T(8,128)(2,1)S(1)}, bf16[2,256,256]{2,1,0:T(8,128)(2,1)S(1)}, u32[]{:S(2)}, u32[]{:S(2)}) collective-permute-start(bf16[2,256,256]{2,1,0:T(8,128)(2,1)S(1)} %shard_map.82), channel_id=1, source_target_pairs={{0,4},{4,0},{8,12},{12,8},{16,20},{20,16},{24,28},{28,24},{1,5},{5... | collective-permute-start | bytes 786440 | tf_op jit(solution)/shard_map/ppermute | solution.py:42
  6.8 10.9 %collective-permute-start.3 = (bf16[64,512]{1,0:T(8,128)(2,1)S(1)}, bf16[64,512]{1,0:T(8,128)(2,1)S(1)}, u32[]{:S(2)}, u32[]{:S(2)}) collective-permute-start(bf16[64,512]{1,0:T(8,128)(2,1)S(1)} %get-tuple-element.44), channel_id=1, source_target_pairs={{0,8},{4,12},{8,0},{12,4},{16,24},{20,28},{24,16},{28,20},{1,9},{5... | collective-permute-start | bytes 196616 | tf_op jit(solution)/shard_map/ppermute | solution.py:42
  8.4 9.3 %collective-permute-start.4 = (bf16[64,512]{1,0:T(8,128)(2,1)S(1)}, bf16[64,512]{1,0:T(8,128)(2,1)S(1)}, u32[]{:S(2)}, u32[]{:S(2)}) collective-permute-start(bf16[64,512]{1,0:T(8,128)(2,1)S(1)} %get-tuple-element.43), channel_id=1, source_target_pairs={{0,16},{4,20},{8,24},{12,28},{16,0},{20,4},{24,8},{28,12},{1,17},{... | collective-permute-start | bytes 196616 | tf_op jit(solution)/shard_map/ppermute | solution.py:42
  11.0 6.7 %collective-permute-start.2 = (bf16[3,64,512]{2,1,0:T(8,128)(2,1)S(1)}, bf16[3,64,512]{2,1,0:T(8,128)(2,1)S(1)}, u32[]{:S(2)}, u32[]{:S(2)}) collective-permute-start(bf16[3,64,512]{2,1,0:T(8,128)(2,1)S(1)} %bitcast.18), channel_id=1, source_target_pairs={{0,2},{1,3},{2,0},{3,1},{4,6},{5,7},{6,4},{7,5},{8,10},{9,11},{10,... | collective-permute-start | bytes 589832 | tf_op jit(solution)/shard_map/ppermute | solution.py:42
  12.6 6.9 %collective-permute-start.1 = (bf16[2,256,256]{2,1,0:T(8,128)(2,1)S(1)}, bf16[2,256,256]{2,1,0:T(8,128)(2,1)S(1)}, u32[]{:S(2)}, u32[]{:S(2)}) collective-permute-start(bf16[2,256,256]{2,1,0:T(8,128)(2,1)S(1)} %get-tuple-element.29), channel_id=1, source_target_pairs={{0,4},{4,0},{8,12},{12,8},{16,20},{20,16},{24,28},{28,24},{1,5},{5... | collective-permute-start | bytes 786440 | tf_op jit(solution)/shard_map/ppermute | solution.py:42
  13.2 10.4 %copy-start.5 = (s32[8,7]{1,0:T(8,128)S(1)}, s32[8,7]{1,0:T(8,128)}, u32[]{:S(2)}) copy-start(s32[8,7]{1,0:T(8,128)} %index_ref.3) | copy-start | bytes 676
  13.2 10.4 %copy-start.6 = (s32[8]{0:T(128)S(1)}, s32[8]{0:T(128)}, u32[]{:S(2)}) copy-start(s32[8]{0:T(128)} %count_ref.3) | copy-start | bytes 100
  14.0 14.9 %collective-permute-start.11 = (bf16[256,256]{1,0:T(8,128)(2,1)S(1)}, bf16[256,256]{1,0:T(8,128)(2,1)S(1)}, u32[]{:S(2)}, u32[]{:S(2)}) collective-permute-start(bf16[256,256]{1,0:T(8,128)(2,1)S(1)} %get-tuple-element.42.rest_0_), channel_id=1, source_target_pairs={{0,24},{4,28},{8,16},{12,20},{16,8},{20,12},{24,0},{28,4},{1,25},{... | collective-permute-start | bytes 393224 | tf_op jit(solution)/shard_map/ppermute | solution.py:42
  19.5 8.4 %collective-permute-start.5 = (bf16[2,64,512]{2,1,0:T(8,128)(2,1)S(1)}, bf16[2,64,512]{2,1,0:T(8,128)(2,1)S(1)}, u32[]{:S(2)}, u32[]{:S(2)}) collective-permute-start(bf16[2,64,512]{2,1,0:T(8,128)(2,1)S(1)} %pad_maximum_fusion.refs_4_), channel_id=1, source_target_pairs={{0,2},{1,3},{2,0},{3,1},{4,6},{5,7},{6,4},{7,5},{8,10},{9,11},{10,... | collective-permute-start | bytes 393224 | tf_op jit(solution)/shard_map/ppermute | solution.py:42
  20.1 12.4 %collective-permute-start.8 = (bf16[2,64,512]{2,1,0:T(8,128)(2,1)S(1)}, bf16[2,64,512]{2,1,0:T(8,128)(2,1)S(1)}, u32[]{:S(2)}, u32[]{:S(2)}) collective-permute-start(bf16[2,64,512]{2,1,0:T(8,128)(2,1)S(1)} %pad_maximum_fusion.refs_4_), channel_id=1, source_target_pairs={{0,1},{1,0},{2,3},{3,2},{4,5},{5,4},{6,7},{7,6},{8,9},{9,8},{10,11... | collective-permute-start | bytes 393224 | tf_op jit(solution)/shard_map/ppermute | solution.py:42
  20.2 8.7 %collective-permute-start.10 = (bf16[256,256]{1,0:T(8,128)(2,1)S(1)}, bf16[256,256]{1,0:T(8,128)(2,1)S(1)}, u32[]{:S(2)}, u32[]{:S(2)}) collective-permute-start(bf16[256,256]{1,0:T(8,128)(2,1)S(1)} %fusion), channel_id=1, source_target_pairs={{0,8},{4,12},{8,0},{12,4},{16,24},{20,28},{24,16},{28,20},{1,9},{5... | collective-permute-start | bytes 393224 | tf_op jit(solution)/shard_map/ppermute | solution.py:42
  21.0 9.4 %collective-permute-start.12 = (bf16[256,256]{1,0:T(8,128)(2,1)S(1)}, bf16[256,256]{1,0:T(8,128)(2,1)S(1)}, u32[]{:S(2)}, u32[]{:S(2)}) collective-permute-start(bf16[256,256]{1,0:T(8,128)(2,1)S(1)} %get-tuple-element.41), channel_id=1, source_target_pairs={{0,16},{4,20},{8,24},{12,28},{16,0},{20,4},{24,8},{28,12},{1,17},{... | collective-permute-start | bytes 393224 | tf_op jit(solution)/shard_map/ppermute | solution.py:42
  27.9 6.1 %collective-permute-start.6 = (bf16[3,64,512]{2,1,0:T(8,128)(2,1)S(1)}, bf16[3,64,512]{2,1,0:T(8,128)(2,1)S(1)}, u32[]{:S(2)}, u32[]{:S(2)}) collective-permute-start(bf16[3,64,512]{2,1,0:T(8,128)(2,1)S(1)} %bitcast.19), channel_id=1, source_target_pairs={{0,1},{1,0},{2,3},{3,2},{4,5},{5,4},{6,7},{7,6},{8,9},{9,8},{10,11... | collective-permute-start | bytes 589832 | tf_op jit(solution)/shard_map/ppermute | solution.py:42
  28.8 5.2 %collective-permute-start.7 = (bf16[3,64,512]{2,1,0:T(8,128)(2,1)S(1)}, bf16[3,64,512]{2,1,0:T(8,128)(2,1)S(1)}, u32[]{:S(2)}, u32[]{:S(2)}) collective-permute-start(bf16[3,64,512]{2,1,0:T(8,128)(2,1)S(1)} %collective-permute-done.2.refs_2_), channel_id=1, source_target_pairs={{0,1},{1,0},{2,3},{3,2},{4,5},{5,4},{6,7},{7,6},{8,9},{9,8},{10,11... | collective-permute-start | bytes 589832 | tf_op jit(solution)/shard_map/ppermute | solution.py:42
  30.4 5.8 %collective-permute-start.13 = (bf16[256,256]{1,0:T(8,128)(2,1)S(1)}, bf16[256,256]{1,0:T(8,128)(2,1)S(1)}, u32[]{:S(2)}, u32[]{:S(2)}) collective-permute-start(bf16[256,256]{1,0:T(8,128)(2,1)S(1)} %add_convert_fusion.1.refs_8_), channel_id=1, source_target_pairs={{0,4},{4,0},{8,12},{12,8},{16,20},{20,16},{24,28},{28,24},{1,5},{5... | collective-permute-start | bytes 393224 | tf_op jit(solution)/shard_map/ppermute | solution.py:42
  32.0 5.0 %collective-permute-start.14 = (bf16[256,256]{1,0:T(8,128)(2,1)S(1)}, bf16[256,256]{1,0:T(8,128)(2,1)S(1)}, u32[]{:S(2)}, u32[]{:S(2)}) collective-permute-start(bf16[256,256]{1,0:T(8,128)(2,1)S(1)} %add_convert_fusion.1.refs_8_), channel_id=1, source_target_pairs={{0,8},{4,12},{8,0},{12,4},{16,24},{20,28},{24,16},{28,20},{1,9},{5... | collective-permute-start | bytes 393224 | tf_op jit(solution)/shard_map/ppermute | solution.py:42
  32.4 6.8 %collective-permute-start.15 = (bf16[256,256]{1,0:T(8,128)(2,1)S(1)}, bf16[256,256]{1,0:T(8,128)(2,1)S(1)}, u32[]{:S(2)}, u32[]{:S(2)}) collective-permute-start(bf16[256,256]{1,0:T(8,128)(2,1)S(1)} %add_convert_fusion.1.refs_8_), channel_id=1, source_target_pairs={{0,12},{4,8},{8,4},{12,0},{16,28},{20,24},{24,20},{28,16},{1,13},{... | collective-permute-start | bytes 393224 | tf_op jit(solution)/shard_map/ppermute | solution.py:42
  34.0 5.3 %collective-permute-start.9 = (bf16[2,64,512]{2,1,0:T(8,128)(2,1)S(1)}, bf16[2,64,512]{2,1,0:T(8,128)(2,1)S(1)}, u32[]{:S(2)}, u32[]{:S(2)}) collective-permute-start(bf16[2,64,512]{2,1,0:T(8,128)(2,1)S(1)} %collective-permute-done.5.refs_6_), channel_id=1, source_target_pairs={{0,1},{1,0},{2,3},{3,2},{4,5},{5,4},{6,7},{7,6},{8,9},{9,8},{10,11... | collective-permute-start | bytes 393224 | tf_op jit(solution)/shard_map/ppermute | solution.py:42
  39.9 7.4 %collective-permute-start.16 = (bf16[256,256]{1,0:T(8,128)(2,1)S(1)}, bf16[256,256]{1,0:T(8,128)(2,1)S(1)}, u32[]{:S(2)}, u32[]{:S(2)}) collective-permute-start(bf16[256,256]{1,0:T(8,128)(2,1)S(1)} %shard_map.86.rest_0_.refs_8_), channel_id=1, source_target_pairs={{0,16},{4,20},{8,24},{12,28},{16,0},{20,4},{24,8},{28,12},{1,17},{... | collective-permute-start | bytes 393224 | tf_op jit(solution)/shard_map/ppermute | solution.py:42
  45.9 8.8 %copy-start.2 = (bf16[2048,256]{1,0:T(8,128)(2,1)S(1)}, bf16[2048,256]{1,0:T(8,128)(2,1)}, u32[]{:S(2)}) copy-start(bf16[2048,256]{1,0:T(8,128)(2,1)} %basis_ref.9) | copy-start | bytes 3145732
  47.6 6.0 %collective-permute-start.18 = (bf16[256,256]{1,0:T(8,128)(2,1)S(1)}, bf16[256,256]{1,0:T(8,128)(2,1)S(1)}, u32[]{:S(2)}, u32[]{:S(2)}) collective-permute-start(bf16[256,256]{1,0:T(8,128)(2,1)S(1)} %get-tuple-element.39.refs_2_), channel_id=1, source_target_pairs={{0,8},{4,12},{8,0},{12,4},{16,24},{20,28},{24,16},{28,20},{1,9},{5... | collective-permute-start | bytes 393224 | tf_op jit(solution)/shard_map/ppermute | solution.py:42
  47.8 6.1 %collective-permute-start.19 = (bf16[256,256]{1,0:T(8,128)(2,1)S(1)}, bf16[256,256]{1,0:T(8,128)(2,1)S(1)}, u32[]{:S(2)}, u32[]{:S(2)}) collective-permute-start(bf16[256,256]{1,0:T(8,128)(2,1)S(1)} %get-tuple-element.40.refs_3_), channel_id=1, source_target_pairs={{0,4},{4,0},{8,12},{12,8},{16,20},{20,16},{24,28},{28,24},{1,5},{5... | collective-permute-start | bytes 393224 | tf_op jit(solution)/shard_map/ppermute | solution.py:42
  49.3 6.3 %collective-permute-start.17 = (bf16[256,256]{1,0:T(8,128)(2,1)S(1)}, bf16[256,256]{1,0:T(8,128)(2,1)S(1)}, u32[]{:S(2)}, u32[]{:S(2)}) collective-permute-start(bf16[256,256]{1,0:T(8,128)(2,1)S(1)} %get-tuple-element.39.refs_2_), channel_id=1, source_target_pairs={{0,4},{4,0},{8,12},{12,8},{16,20},{20,16},{24,28},{28,24},{1,5},{5... | collective-permute-start | bytes 393224 | tf_op jit(solution)/shard_map/ppermute | solution.py:42
  49.8 5.8 %collective-permute-start.20 = (bf16[256,256]{1,0:T(8,128)(2,1)S(1)}, bf16[256,256]{1,0:T(8,128)(2,1)S(1)}, u32[]{:S(2)}, u32[]{:S(2)}) collective-permute-start(bf16[256,256]{1,0:T(8,128)(2,1)S(1)} %get-tuple-element.40.refs_3_), channel_id=1, source_target_pairs={{0,8},{4,12},{8,0},{12,4},{16,24},{20,28},{24,16},{28,20},{1,9},{5... | collective-permute-start | bytes 393224 | tf_op jit(solution)/shard_map/ppermute | solution.py:42
  53.6 5.0 %collective-permute-start.21 = (bf16[256,256]{1,0:T(8,128)(2,1)S(1)}, bf16[256,256]{1,0:T(8,128)(2,1)S(1)}, u32[]{:S(2)}, u32[]{:S(2)}) collective-permute-start(bf16[256,256]{1,0:T(8,128)(2,1)S(1)} %collective-permute-done.18.refs_2_), channel_id=1, source_target_pairs={{0,4},{4,0},{8,12},{12,8},{16,20},{20,16},{24,28},{28,24},{1,5},{5... | collective-permute-start | bytes 393224 | tf_op jit(solution)/shard_map/ppermute | solution.py:42
  53.9 5.0 %collective-permute-start.22 = (bf16[256,256]{1,0:T(8,128)(2,1)S(1)}, bf16[256,256]{1,0:T(8,128)(2,1)S(1)}, u32[]{:S(2)}, u32[]{:S(2)}) collective-permute-start(bf16[256,256]{1,0:T(8,128)(2,1)S(1)} %collective-permute-done.19.refs_3_), channel_id=1, source_target_pairs={{0,8},{4,12},{8,0},{12,4},{16,24},{20,28},{24,16},{28,20},{1,9},{5... | collective-permute-start | bytes 393224 | tf_op jit(solution)/shard_map/ppermute | solution.py:42

commit v6 on v5

--- a/solution.py
+++ b/solution.py
@@ -345,7 +345,8 @@
         top ^ low ^ high: swapped(from_low[top ^ low], "leaf", high),
     }
     total = [add_far(total, from_low | from_high)]
-    return add_far(total, rest, True)
+    total = [add_far(total, {low ^ high: rest[low ^ high]})]
+    return add_far(total, {top ^ low ^ high: rest[top ^ low ^ high]}, True)
 
 
 def solution(mesh):

time: 60.7 us -> 60.6 us (level)
    pallas_call x10 -> x11, Pallas kernels: 17.9 us -> 18.1 us  [call(): pl.pallas_call(kernel, out_shape=[space(s.shape, s.dtype) for s, space in...]
  transfers between devices with their start and end apart: 23 -> 23, of which waited for: 10 -> 9; matrix products, arithmetic and copies ran while one was open for 0% -> 0% of each run, Pallas kernels for 21% -> 22%
where the time goes in v6:
time: 60.6 us; the launch traced here: 60.5 us
  starting transfers between devices  27.7 us (46%)
  Pallas kernels  18.1 us (30%)
  waiting for transfers between devices  14.2 us (23%)
    ppermute x23, starting transfers between devices, swapped(): lax.ppermute(value, axis, [(i, i ^ mask) for i in range(lax.axis_size(axi...  27.7 us
    pallas_call x11, Pallas kernels, call(): pl.pallas_call(kernel, out_shape=[space(s.shape, s.dtype) for s, space in...  18.1 us
    ppermute x23, waiting for transfers between devices, swapped(): lax.ppermute(value, axis, [(i, i ^ mask) for i in range(lax.axis_size(axi...  14.2 us
  transfers between devices with their start and end apart: 23, of which 9 were waited for; matrix products, arithmetic and copies ran while one was open for 0% of the time, Pallas kernels for 22%

profile of v6, /device:TPU:0, one launch (start us, length us, event | category | flops | bytes accessed | tf_op | source)
XLA Modules:
  0.0 60.5 jit_solution(8342810639843314361)
XLA Ops:
  0.0 2.4 %shard_map.82 = bf16[2,256,256]{2,1,0:T(8,128)(2,1)S(1)} custom-call(s32[1]{0:T(128)} %bitcast.me_ref, s32[1,2048]{1,0:T(1,128)} %bitcast.22, bf16[2048,256]{1,0:T(8,128)(2,1)} %basis_ref.7, bf16[2048,256]{1,0:T(8,128)(2,1)} %fields_ref.3, s32[1]{0:T(128)} %bitcast.2.rest_0_.me_ref), custom_call_target="tpu_custom_call" | custom-call | flops 1024 | bytes 1024 | tf_op jit(solution)/shard_map/pallas_call | solution.py:26
  2.5 3.0 %collective-permute-start = (bf16[2,256,256]{2,1,0:T(8,128)(2,1)S(1)}, bf16[2,256,256]{2,1,0:T(8,128)(2,1)S(1)}, u32[]{:S(2)}, u32[]{:S(2)}) collective-permute-start(bf16[2,256,256]{2,1,0:T(8,128)(2,1)S(1)} %shard_map.82), channel_id=1, source_target_pairs={{0,4},{4,0},{8,12},{12,8},{16,20},{20,16},{24,28},{28,24},{1,5},{5... | collective-permute-start | bytes 786440 | tf_op jit(solution)/shard_map/ppermute | solution.py:42
  5.5 1.3 %shard_map.83 = (f32[2,256,256]{2,1,0:T(8,128)S(1)}, bf16[2,256,256]{2,1,0:T(8,128)(2,1)S(1)}) custom-call(s32[1]{0:T(128)} %bitcast.me_ref, s32[1,2048]{1,0:T(1,128)S(1)} %bitcast.23, bf16[2048,256]{1,0:T(8,128)(2,1)S(1)} %copy-done.2, bf16[2048,256]{1,0:T(8,128)(2,1)S(1)} %copy-done), custom_call_target="tpu_custom_call" | custom-call | flops 1024 | bytes 1024 | tf_op jit(solution)/shard_map/pallas_call | solution.py:26
  6.8 1.6 %collective-permute-start.3 = (bf16[64,512]{1,0:T(8,128)(2,1)S(1)}, bf16[64,512]{1,0:T(8,128)(2,1)S(1)}, u32[]{:S(2)}, u32[]{:S(2)}) collective-permute-start(bf16[64,512]{1,0:T(8,128)(2,1)S(1)} %get-tuple-element.44), channel_id=1, source_target_pairs={{0,8},{4,12},{8,0},{12,4},{16,24},{20,28},{24,16},{28,20},{1,9},{5... | collective-permute-start | bytes 196616 | tf_op jit(solution)/shard_map/ppermute | solution.py:42
  8.4 2.6 %collective-permute-start.4 = (bf16[64,512]{1,0:T(8,128)(2,1)S(1)}, bf16[64,512]{1,0:T(8,128)(2,1)S(1)}, u32[]{:S(2)}, u32[]{:S(2)}) collective-permute-start(bf16[64,512]{1,0:T(8,128)(2,1)S(1)} %get-tuple-element.43), channel_id=1, source_target_pairs={{0,16},{4,20},{8,24},{12,28},{16,0},{20,4},{24,8},{28,12},{1,17},{... | collective-permute-start | bytes 196616 | tf_op jit(solution)/shard_map/ppermute | solution.py:42
  11.0 1.5 %collective-permute-start.2 = (bf16[3,64,512]{2,1,0:T(8,128)(2,1)S(1)}, bf16[3,64,512]{2,1,0:T(8,128)(2,1)S(1)}, u32[]{:S(2)}, u32[]{:S(2)}) collective-permute-start(bf16[3,64,512]{2,1,0:T(8,128)(2,1)S(1)} %bitcast.18), channel_id=1, source_target_pairs={{0,2},{1,3},{2,0},{3,1},{4,6},{5,7},{6,4},{7,5},{8,10},{9,11},{10,... | collective-permute-start | bytes 589832 | tf_op jit(solution)/shard_map/ppermute | solution.py:42
  13.2 0.7 %shard_map.84 = (f32[2,256,256]{2,1,0:T(8,128)S(1)}, bf16[2048,128]{1,0:T(8,128)(2,1)S(1)}) custom-call(s32[1]{0:T(128)} %bitcast.me_ref, s32[1,2048]{1,0:T(1,128)S(1)} %bitcast.24, bf16[2048,256]{1,0:T(8,128)(2,1)S(1)} %copy-done.2, bf16[2048,256]{1,0:T(8,128)(2,1)S(1)} %copy-done, bf16[256,256]{1,0:T(8,128)(2,1)S(1)} %get-tuple-element.42.rest_0_), custom_call_target="tpu_custom_call" | custom-call | flops 1024 | bytes 1024 | tf_op jit(solution)/shard_map/pallas_call | solution.py:26
  14.0 3.8 %collective-permute-start.11 = (bf16[256,256]{1,0:T(8,128)(2,1)S(1)}, bf16[256,256]{1,0:T(8,128)(2,1)S(1)}, u32[]{:S(2)}, u32[]{:S(2)}) collective-permute-start(bf16[256,256]{1,0:T(8,128)(2,1)S(1)} %get-tuple-element.42.rest_0_), channel_id=1, source_target_pairs={{0,24},{4,28},{8,16},{12,20},{16,8},{20,12},{24,0},{28,4},{1,25},{... | collective-permute-start | bytes 393224 | tf_op jit(solution)/shard_map/ppermute | solution.py:42
  17.7 1.7 %collective-permute-done.1 = bf16[2,256,256]{2,1,0:T(8,128)(2,1)S(1)} collective-permute-done((bf16[2,256,256]{2,1,0:T(8,128)(2,1)S(1)}, bf16[2,256,256]{2,1,0:T(8,128)(2,1)S(1)}, u32[]{:S(2)}, u32[]{:S(2)}) %collective-permute-start.1) | collective-permute-done | bytes 262176 | tf_op jit(solution)/shard_map/ppermute | solution.py:42
  19.5 0.6 collective-permute-start.5
  20.2 0.8 %collective-permute-start.10 = (bf16[256,256]{1,0:T(8,128)(2,1)S(1)}, bf16[256,256]{1,0:T(8,128)(2,1)S(1)}, u32[]{:S(2)}, u32[]{:S(2)}) collective-permute-start(bf16[256,256]{1,0:T(8,128)(2,1)S(1)} %fusion), channel_id=1, source_target_pairs={{0,8},{4,12},{8,0},{12,4},{16,24},{20,28},{24,16},{28,20},{1,9},{5... | collective-permute-start | bytes 393224 | tf_op jit(solution)/shard_map/ppermute | solution.py:42
  21.0 2.6 %collective-permute-start.12 = (bf16[256,256]{1,0:T(8,128)(2,1)S(1)}, bf16[256,256]{1,0:T(8,128)(2,1)S(1)}, u32[]{:S(2)}, u32[]{:S(2)}) collective-permute-start(bf16[256,256]{1,0:T(8,128)(2,1)S(1)} %get-tuple-element.41), channel_id=1, source_target_pairs={{0,16},{4,20},{8,24},{12,28},{16,0},{20,4},{24,8},{28,12},{1,17},{... | collective-permute-start | bytes 393224 | tf_op jit(solution)/shard_map/ppermute | solution.py:42
  23.6 4.3 %shard_map.85.refs_0_ = f32[1024,256]{1,0:T(8,128)S(1)} custom-call(s32[8,7]{1,0:T(8,128)S(1)} %copy-done.5, s32[8]{0:T(128)S(1)} %copy-done.6, bf16[8,7,256,256]{3,2,1,0:T(8,128)(2,1)} %blocks_hbm.3, bf16[2048,256]{1,0:T(8,128)(2,1)S(1)} %copy-done, bf16[256,256]{1,0:T(8,128)(2,1)S(1)} %get-tuple-element.42.rest_0_), custom_call_target="tpu_custom_call" | custom-call | flops 1024 | bytes 1024 | tf_op jit(solution)/shard_map/pallas_call | solution.py:26
  28.0 0.8 %collective-permute-done.10 = bf16[256,256]{1,0:T(8,128)(2,1)S(1)} collective-permute-done((bf16[256,256]{1,0:T(8,128)(2,1)S(1)}, bf16[256,256]{1,0:T(8,128)(2,1)S(1)}, u32[]{:S(2)}, u32[]{:S(2)}) %collective-permute-start.10) | collective-permute-done | bytes 131104 | tf_op jit(solution)/shard_map/ppermute | solution.py:42
  28.8 1.5 %collective-permute-done.12 = bf16[256,256]{1,0:T(8,128)(2,1)S(1)} collective-permute-done((bf16[256,256]{1,0:T(8,128)(2,1)S(1)}, bf16[256,256]{1,0:T(8,128)(2,1)S(1)}, u32[]{:S(2)}, u32[]{:S(2)}) %collective-permute-start.12) | collective-permute-done | bytes 131104 | tf_op jit(solution)/shard_map/ppermute | solution.py:42
  30.4 1.6 %collective-permute-start.13 = (bf16[256,256]{1,0:T(8,128)(2,1)S(1)}, bf16[256,256]{1,0:T(8,128)(2,1)S(1)}, u32[]{:S(2)}, u32[]{:S(2)}) collective-permute-start(bf16[256,256]{1,0:T(8,128)(2,1)S(1)} %add_convert_fusion.1.refs_8_), channel_id=1, source_target_pairs={{0,4},{4,0},{8,12},{12,8},{16,20},{20,16},{24,28},{28,24},{1,5},{5... | collective-permute-start | bytes 393224 | tf_op jit(solution)/shard_map/ppermute | solution.py:42
  32.4 1.5 %collective-permute-start.15 = (bf16[256,256]{1,0:T(8,128)(2,1)S(1)}, bf16[256,256]{1,0:T(8,128)(2,1)S(1)}, u32[]{:S(2)}, u32[]{:S(2)}) collective-permute-start(bf16[256,256]{1,0:T(8,128)(2,1)S(1)} %add_convert_fusion.1.refs_8_), channel_id=1, source_target_pairs={{0,12},{4,8},{8,4},{12,0},{16,28},{20,24},{24,20},{28,16},{1,13},{... | collective-permute-start | bytes 393224 | tf_op jit(solution)/shard_map/ppermute | solution.py:42
  34.0 2.3 %collective-permute-done.13.refs_9_ = bf16[256,256]{1,0:T(8,128)(2,1)S(1)} collective-permute-done((bf16[256,256]{1,0:T(8,128)(2,1)S(1)}, bf16[256,256]{1,0:T(8,128)(2,1)S(1)}, u32[]{:S(2)}, u32[]{:S(2)}) %collective-permute-start.13) | collective-permute-done | bytes 131104 | tf_op jit(solution)/shard_map/ppermute | solution.py:42
  36.3 0.7 %collective-permute-done.14.refs_10_ = bf16[256,256]{1,0:T(8,128)(2,1)S(1)} collective-permute-done((bf16[256,256]{1,0:T(8,128)(2,1)S(1)}, bf16[256,256]{1,0:T(8,128)(2,1)S(1)}, u32[]{:S(2)}, u32[]{:S(2)}) %collective-permute-start.14) | collective-permute-done | bytes 131104 | tf_op jit(solution)/shard_map/ppermute | solution.py:42
  37.0 2.3 %collective-permute-done.15.refs_11_ = bf16[256,256]{1,0:T(8,128)(2,1)S(1)} collective-permute-done((bf16[256,256]{1,0:T(8,128)(2,1)S(1)}, bf16[256,256]{1,0:T(8,128)(2,1)S(1)}, u32[]{:S(2)}, u32[]{:S(2)}) %collective-permute-start.15) | collective-permute-done | bytes 131104 | tf_op jit(solution)/shard_map/ppermute | solution.py:42
  39.3 0.7 %shard_map.86.rest_0_.refs_8_ = bf16[256,256]{1,0:T(8,128)(2,1)S(1)} custom-call(s32[1]{0:T(128)} %bitcast.2.rest_0_.me_ref, bf16[3,64,512]{2,1,0:T(8,128)(2,1)S(1)} %bitcast.20, bf16[3,64,512]{2,1,0:T(8,128)(2,1)S(1)} %collective-permute-done.6.refs_1_, bf16[3,64,512]{2,1,0:T(8,128)(2,1)S(1)} %collective-permute-done.2.refs_2_, ...), custom_call_target="tpu_custom_call" | custom-call | flops 1024 | bytes 1024 | tf_op jit(solution)/shard_map/pallas_call | solution.py:26
  39.9 1.7 %collective-permute-start.16 = (bf16[256,256]{1,0:T(8,128)(2,1)S(1)}, bf16[256,256]{1,0:T(8,128)(2,1)S(1)}, u32[]{:S(2)}, u32[]{:S(2)}) collective-permute-start(bf16[256,256]{1,0:T(8,128)(2,1)S(1)} %shard_map.86.rest_0_.refs_8_), channel_id=1, source_target_pairs={{0,16},{4,20},{8,24},{12,28},{16,0},{20,4},{24,8},{28,12},{1,17},{... | collective-permute-start | bytes 393224 | tf_op jit(solution)/shard_map/ppermute | solution.py:42
  41.6 4.3 %shard_map.87.refs_10_.refs_1_ = f32[1024,256]{1,0:T(8,128)S(1)} custom-call(s32[8,7]{1,0:T(8,128)S(1)} %copy-done.5, s32[8]{0:T(128)S(1)} %copy-done.6, bf16[8,7,256,256]{3,2,1,0:T(8,128)(2,1)} %blocks_hbm.3, bf16[2048,256]{1,0:T(8,128)(2,1)S(1)} %copy-done, bf16[256,256]{1,0:T(8,128)(2,1)S(1)} %shard_map.86.rest_0_.refs_8_), custom_call_target="tpu_custom_call" | custom-call | flops 1024 | bytes 1024 | tf_op jit(solution)/shard_map/pallas_call | solution.py:26
  45.9 1.3 %collective-permute-done.16.refs_9_ = bf16[256,256]{1,0:T(8,128)(2,1)S(1)} collective-permute-done((bf16[256,256]{1,0:T(8,128)(2,1)S(1)}, bf16[256,256]{1,0:T(8,128)(2,1)S(1)}, u32[]{:S(2)}, u32[]{:S(2)}) %collective-permute-start.16) | collective-permute-done | bytes 131104 | tf_op jit(solution)/shard_map/ppermute | solution.py:42
  47.8 1.5 %collective-permute-start.19 = (bf16[256,256]{1,0:T(8,128)(2,1)S(1)}, bf16[256,256]{1,0:T(8,128)(2,1)S(1)}, u32[]{:S(2)}, u32[]{:S(2)}) collective-permute-start(bf16[256,256]{1,0:T(8,128)(2,1)S(1)} %get-tuple-element.40.refs_3_), channel_id=1, source_target_pairs={{0,4},{4,0},{8,12},{12,8},{16,20},{20,16},{24,28},{28,24},{1,5},{5... | collective-permute-start | bytes 393224 | tf_op jit(solution)/shard_map/ppermute | solution.py:42
  49.8 1.9 %collective-permute-start.20 = (bf16[256,256]{1,0:T(8,128)(2,1)S(1)}, bf16[256,256]{1,0:T(8,128)(2,1)S(1)}, u32[]{:S(2)}, u32[]{:S(2)}) collective-permute-start(bf16[256,256]{1,0:T(8,128)(2,1)S(1)} %get-tuple-element.40.refs_3_), channel_id=1, source_target_pairs={{0,8},{4,12},{8,0},{12,4},{16,24},{20,28},{24,16},{28,20},{1,9},{5... | collective-permute-start | bytes 393224 | tf_op jit(solution)/shard_map/ppermute | solution.py:42
  51.7 1.9 %collective-permute-done.18.refs_2_ = bf16[256,256]{1,0:T(8,128)(2,1)S(1)} collective-permute-done((bf16[256,256]{1,0:T(8,128)(2,1)S(1)}, bf16[256,256]{1,0:T(8,128)(2,1)S(1)}, u32[]{:S(2)}, u32[]{:S(2)}) %collective-permute-start.18) | collective-permute-done | bytes 131104 | tf_op jit(solution)/shard_map/ppermute | solution.py:42
  53.9 0.8 %collective-permute-start.22 = (bf16[256,256]{1,0:T(8,128)(2,1)S(1)}, bf16[256,256]{1,0:T(8,128)(2,1)S(1)}, u32[]{:S(2)}, u32[]{:S(2)}) collective-permute-start(bf16[256,256]{1,0:T(8,128)(2,1)S(1)} %collective-permute-done.19.refs_3_), channel_id=1, source_target_pairs={{0,8},{4,12},{8,0},{12,4},{16,24},{20,28},{24,16},{28,20},{1,9},{5... | collective-permute-start | bytes 393224 | tf_op jit(solution)/shard_map/ppermute | solution.py:42
  54.8 0.8 %shard_map.89.refs_0_ = f32[2048,256]{1,0:T(8,128)S(1)} custom-call(bf16[2048,128]{1,0:T(8,128)(2,1)S(1)} %get-tuple-element.27.tag_ref, bf16[2048,256]{1,0:T(8,128)(2,1)S(1)} %copy-done.1, f32[1024,256]{1,0:T(8,128)S(1)} %shard_map.85.refs_0_, f32[1024,256]{1,0:T(8,128)S(1)} %shard_map.87.refs_10_.refs_1_, bf16[256,256]{1,0:T(8,128)(2,1)S(1)} %get-tuple-element.39.refs_2_, ...), custom_call_target="tpu_custom_call" | custom-call | flops 1024 | bytes 1024 | tf_op jit(solution)/shard_map/pallas_call | solution.py:26
  55.6 1.4 %shard_map.90.refs_0_ = f32[2048,256]{1,0:T(8,128)S(1)} custom-call(bf16[2048,128]{1,0:T(8,128)(2,1)S(1)} %get-tuple-element.27.tag_ref, bf16[2048,256]{1,0:T(8,128)(2,1)S(1)} %copy-done.1, f32[2048,256]{1,0:T(8,128)S(1)} %shard_map.89.refs_0_, bf16[256,256]{1,0:T(8,128)(2,1)S(1)} %collective-permute-done.17.refs_1_, ...), custom_call_target="tpu_custom_call" | custom-call | flops 1024 | bytes 1024 | tf_op jit(solution)/shard_map/pallas_call | solution.py:26
  57.0 1.5 %collective-permute-done.21.refs_1_ = bf16[256,256]{1,0:T(8,128)(2,1)S(1)} collective-permute-done((bf16[256,256]{1,0:T(8,128)(2,1)S(1)}, bf16[256,256]{1,0:T(8,128)(2,1)S(1)}, u32[]{:S(2)}, u32[]{:S(2)}) %collective-permute-start.21) | collective-permute-done | bytes 131104 | tf_op jit(solution)/shard_map/ppermute | solution.py:42
  59.1 1.4 %shard_map.92 = bf16[2048,256]{1,0:T(8,128)(2,1)} custom-call(bf16[2048,128]{1,0:T(8,128)(2,1)S(1)} %get-tuple-element.27.tag_ref, bf16[2048,256]{1,0:T(8,128)(2,1)S(1)} %copy-done.1, f32[2048,256]{1,0:T(8,128)S(1)} %shard_map.91.refs_0_, bf16[256,256]{1,0:T(8,128)(2,1)S(1)} %collective-permute-done.22.refs_1_), custom_call_target="tpu_custom_call" | custom-call | flops 1024 | bytes 1024 | tf_op jit(solution)/shard_map/pallas_call | solution.py:26
  (47 shorter events, 3.2 us)
Async XLA Ops:
  0.0 5.5 %copy-start.4 = (s32[2048,1]{0,1:T(1,128)S(1)}, s32[2048,1]{0,1:T(1,128)}, u32[]{:S(2)}) copy-start(s32[2048,1]{0,1:T(1,128)} %param.9) | copy-start | bytes 24580
  0.0 5.5 %copy-start.2 = (bf16[2048,256]{1,0:T(8,128)(2,1)S(1)}, bf16[2048,256]{1,0:T(8,128)(2,1)}, u32[]{:S(2)}) copy-start(bf16[2048,256]{1,0:T(8,128)(2,1)} %basis_ref.7) | copy-start | bytes 3145732
  0.0 5.5 %copy-start = (bf16[2048,256]{1,0:T(8,128)(2,1)S(1)}, bf16[2048,256]{1,0:T(8,128)(2,1)}, u32[]{:S(2)}) copy-start(bf16[2048,256]{1,0:T(8,128)(2,1)} %fields_ref.3) | copy-start | bytes 3145732
  0.0 6.8 %copy-start.3 = (bf16[1,3,64,512]{3,2,1,0:T(8,128)(2,1)S(1)}, bf16[1,3,64,512]{3,2,1,0:T(8,128)(2,1)}, u32[]{:S(2)}) copy-start(bf16[1,3,64,512]{3,2,1,0:T(8,128)(2,1)} %param.12) | copy-start | bytes 589828
  2.5 10.6 %collective-permute-start = (bf16[2,256,256]{2,1,0:T(8,128)(2,1)S(1)}, bf16[2,256,256]{2,1,0:T(8,128)(2,1)S(1)}, u32[]{:S(2)}, u32[]{:S(2)}) collective-permute-start(bf16[2,256,256]{2,1,0:T(8,128)(2,1)S(1)} %shard_map.82), channel_id=1, source_target_pairs={{0,4},{4,0},{8,12},{12,8},{16,20},{20,16},{24,28},{28,24},{1,5},{5... | collective-permute-start | bytes 786440 | tf_op jit(solution)/shard_map/ppermute | solution.py:42
  6.8 10.9 %collective-permute-start.3 = (bf16[64,512]{1,0:T(8,128)(2,1)S(1)}, bf16[64,512]{1,0:T(8,128)(2,1)S(1)}, u32[]{:S(2)}, u32[]{:S(2)}) collective-permute-start(bf16[64,512]{1,0:T(8,128)(2,1)S(1)} %get-tuple-element.44), channel_id=1, source_target_pairs={{0,8},{4,12},{8,0},{12,4},{16,24},{20,28},{24,16},{28,20},{1,9},{5... | collective-permute-start | bytes 196616 | tf_op jit(solution)/shard_map/ppermute | solution.py:42
  8.4 9.3 %collective-permute-start.4 = (bf16[64,512]{1,0:T(8,128)(2,1)S(1)}, bf16[64,512]{1,0:T(8,128)(2,1)S(1)}, u32[]{:S(2)}, u32[]{:S(2)}) collective-permute-start(bf16[64,512]{1,0:T(8,128)(2,1)S(1)} %get-tuple-element.43), channel_id=1, source_target_pairs={{0,16},{4,20},{8,24},{12,28},{16,0},{20,4},{24,8},{28,12},{1,17},{... | collective-permute-start | bytes 196616 | tf_op jit(solution)/shard_map/ppermute | solution.py:42
  11.0 6.7 %collective-permute-start.2 = (bf16[3,64,512]{2,1,0:T(8,128)(2,1)S(1)}, bf16[3,64,512]{2,1,0:T(8,128)(2,1)S(1)}, u32[]{:S(2)}, u32[]{:S(2)}) collective-permute-start(bf16[3,64,512]{2,1,0:T(8,128)(2,1)S(1)} %bitcast.18), channel_id=1, source_target_pairs={{0,2},{1,3},{2,0},{3,1},{4,6},{5,7},{6,4},{7,5},{8,10},{9,11},{10,... | collective-permute-start | bytes 589832 | tf_op jit(solution)/shard_map/ppermute | solution.py:42
  12.6 6.9 %collective-permute-start.1 = (bf16[2,256,256]{2,1,0:T(8,128)(2,1)S(1)}, bf16[2,256,256]{2,1,0:T(8,128)(2,1)S(1)}, u32[]{:S(2)}, u32[]{:S(2)}) collective-permute-start(bf16[2,256,256]{2,1,0:T(8,128)(2,1)S(1)} %get-tuple-element.29), channel_id=1, source_target_pairs={{0,4},{4,0},{8,12},{12,8},{16,20},{20,16},{24,28},{28,24},{1,5},{5... | collective-permute-start | bytes 786440 | tf_op jit(solution)/shard_map/ppermute | solution.py:42
  13.2 10.4 %copy-start.5 = (s32[8,7]{1,0:T(8,128)S(1)}, s32[8,7]{1,0:T(8,128)}, u32[]{:S(2)}) copy-start(s32[8,7]{1,0:T(8,128)} %index_ref.3) | copy-start | bytes 676
  13.2 10.4 %copy-start.6 = (s32[8]{0:T(128)S(1)}, s32[8]{0:T(128)}, u32[]{:S(2)}) copy-start(s32[8]{0:T(128)} %count_ref.3) | copy-start | bytes 100
  14.0 14.9 %collective-permute-start.11 = (bf16[256,256]{1,0:T(8,128)(2,1)S(1)}, bf16[256,256]{1,0:T(8,128)(2,1)S(1)}, u32[]{:S(2)}, u32[]{:S(2)}) collective-permute-start(bf16[256,256]{1,0:T(8,128)(2,1)S(1)} %get-tuple-element.42.rest_0_), channel_id=1, source_target_pairs={{0,24},{4,28},{8,16},{12,20},{16,8},{20,12},{24,0},{28,4},{1,25},{... | collective-permute-start | bytes 393224 | tf_op jit(solution)/shard_map/ppermute | solution.py:42
  19.5 8.4 %collective-permute-start.5 = (bf16[2,64,512]{2,1,0:T(8,128)(2,1)S(1)}, bf16[2,64,512]{2,1,0:T(8,128)(2,1)S(1)}, u32[]{:S(2)}, u32[]{:S(2)}) collective-permute-start(bf16[2,64,512]{2,1,0:T(8,128)(2,1)S(1)} %pad_maximum_fusion.refs_4_), channel_id=1, source_target_pairs={{0,2},{1,3},{2,0},{3,1},{4,6},{5,7},{6,4},{7,5},{8,10},{9,11},{10,... | collective-permute-start | bytes 393224 | tf_op jit(solution)/shard_map/ppermute | solution.py:42
  20.1 12.4 %collective-permute-start.8 = (bf16[2,64,512]{2,1,0:T(8,128)(2,1)S(1)}, bf16[2,64,512]{2,1,0:T(8,128)(2,1)S(1)}, u32[]{:S(2)}, u32[]{:S(2)}) collective-permute-start(bf16[2,64,512]{2,1,0:T(8,128)(2,1)S(1)} %pad_maximum_fusion.refs_4_), channel_id=1, source_target_pairs={{0,1},{1,0},{2,3},{3,2},{4,5},{5,4},{6,7},{7,6},{8,9},{9,8},{10,11... | collective-permute-start | bytes 393224 | tf_op jit(solution)/shard_map/ppermute | solution.py:42
  20.2 8.7 %collective-permute-start.10 = (bf16[256,256]{1,0:T(8,128)(2,1)S(1)}, bf16[256,256]{1,0:T(8,128)(2,1)S(1)}, u32[]{:S(2)}, u32[]{:S(2)}) collective-permute-start(bf16[256,256]{1,0:T(8,128)(2,1)S(1)} %fusion), channel_id=1, source_target_pairs={{0,8},{4,12},{8,0},{12,4},{16,24},{20,28},{24,16},{28,20},{1,9},{5... | collective-permute-start | bytes 393224 | tf_op jit(solution)/shard_map/ppermute | solution.py:42
  21.0 9.4 %collective-permute-start.12 = (bf16[256,256]{1,0:T(8,128)(2,1)S(1)}, bf16[256,256]{1,0:T(8,128)(2,1)S(1)}, u32[]{:S(2)}, u32[]{:S(2)}) collective-permute-start(bf16[256,256]{1,0:T(8,128)(2,1)S(1)} %get-tuple-element.41), channel_id=1, source_target_pairs={{0,16},{4,20},{8,24},{12,28},{16,0},{20,4},{24,8},{28,12},{1,17},{... | collective-permute-start | bytes 393224 | tf_op jit(solution)/shard_map/ppermute | solution.py:42
  27.9 6.1 %collective-permute-start.6 = (bf16[3,64,512]{2,1,0:T(8,128)(2,1)S(1)}, bf16[3,64,512]{2,1,0:T(8,128)(2,1)S(1)}, u32[]{:S(2)}, u32[]{:S(2)}) collective-permute-start(bf16[3,64,512]{2,1,0:T(8,128)(2,1)S(1)} %bitcast.19), channel_id=1, source_target_pairs={{0,1},{1,0},{2,3},{3,2},{4,5},{5,4},{6,7},{7,6},{8,9},{9,8},{10,11... | collective-permute-start | bytes 589832 | tf_op jit(solution)/shard_map/ppermute | solution.py:42
  28.8 5.2 %collective-permute-start.7 = (bf16[3,64,512]{2,1,0:T(8,128)(2,1)S(1)}, bf16[3,64,512]{2,1,0:T(8,128)(2,1)S(1)}, u32[]{:S(2)}, u32[]{:S(2)}) collective-permute-start(bf16[3,64,512]{2,1,0:T(8,128)(2,1)S(1)} %collective-permute-done.2.refs_2_), channel_id=1, source_target_pairs={{0,1},{1,0},{2,3},{3,2},{4,5},{5,4},{6,7},{7,6},{8,9},{9,8},{10,11... | collective-permute-start | bytes 589832 | tf_op jit(solution)/shard_map/ppermute | solution.py:42
  30.4 5.8 %collective-permute-start.13 = (bf16[256,256]{1,0:T(8,128)(2,1)S(1)}, bf16[256,256]{1,0:T(8,128)(2,1)S(1)}, u32[]{:S(2)}, u32[]{:S(2)}) collective-permute-start(bf16[256,256]{1,0:T(8,128)(2,1)S(1)} %add_convert_fusion.1.refs_8_), channel_id=1, source_target_pairs={{0,4},{4,0},{8,12},{12,8},{16,20},{20,16},{24,28},{28,24},{1,5},{5... | collective-permute-start | bytes 393224 | tf_op jit(solution)/shard_map/ppermute | solution.py:42
  32.0 5.0 %collective-permute-start.14 = (bf16[256,256]{1,0:T(8,128)(2,1)S(1)}, bf16[256,256]{1,0:T(8,128)(2,1)S(1)}, u32[]{:S(2)}, u32[]{:S(2)}) collective-permute-start(bf16[256,256]{1,0:T(8,128)(2,1)S(1)} %add_convert_fusion.1.refs_8_), channel_id=1, source_target_pairs={{0,8},{4,12},{8,0},{12,4},{16,24},{20,28},{24,16},{28,20},{1,9},{5... | collective-permute-start | bytes 393224 | tf_op jit(solution)/shard_map/ppermute | solution.py:42
  32.4 6.8 %collective-permute-start.15 = (bf16[256,256]{1,0:T(8,128)(2,1)S(1)}, bf16[256,256]{1,0:T(8,128)(2,1)S(1)}, u32[]{:S(2)}, u32[]{:S(2)}) collective-permute-start(bf16[256,256]{1,0:T(8,128)(2,1)S(1)} %add_convert_fusion.1.refs_8_), channel_id=1, source_target_pairs={{0,12},{4,8},{8,4},{12,0},{16,28},{20,24},{24,20},{28,16},{1,13},{... | collective-permute-start | bytes 393224 | tf_op jit(solution)/shard_map/ppermute | solution.py:42
  34.0 5.3 %collective-permute-start.9 = (bf16[2,64,512]{2,1,0:T(8,128)(2,1)S(1)}, bf16[2,64,512]{2,1,0:T(8,128)(2,1)S(1)}, u32[]{:S(2)}, u32[]{:S(2)}) collective-permute-start(bf16[2,64,512]{2,1,0:T(8,128)(2,1)S(1)} %collective-permute-done.5.refs_6_), channel_id=1, source_target_pairs={{0,1},{1,0},{2,3},{3,2},{4,5},{5,4},{6,7},{7,6},{8,9},{9,8},{10,11... | collective-permute-start | bytes 393224 | tf_op jit(solution)/shard_map/ppermute | solution.py:42
  39.9 7.4 %collective-permute-start.16 = (bf16[256,256]{1,0:T(8,128)(2,1)S(1)}, bf16[256,256]{1,0:T(8,128)(2,1)S(1)}, u32[]{:S(2)}, u32[]{:S(2)}) collective-permute-start(bf16[256,256]{1,0:T(8,128)(2,1)S(1)} %shard_map.86.rest_0_.refs_8_), channel_id=1, source_target_pairs={{0,16},{4,20},{8,24},{12,28},{16,0},{20,4},{24,8},{28,12},{1,17},{... | collective-permute-start | bytes 393224 | tf_op jit(solution)/shard_map/ppermute | solution.py:42
  45.9 8.8 %copy-start.1 = (bf16[2048,256]{1,0:T(8,128)(2,1)S(1)}, bf16[2048,256]{1,0:T(8,128)(2,1)}, u32[]{:S(2)}) copy-start(bf16[2048,256]{1,0:T(8,128)(2,1)} %basis_ref.11) | copy-start | bytes 3145732
  47.6 6.0 %collective-permute-start.18 = (bf16[256,256]{1,0:T(8,128)(2,1)S(1)}, bf16[256,256]{1,0:T(8,128)(2,1)S(1)}, u32[]{:S(2)}, u32[]{:S(2)}) collective-permute-start(bf16[256,256]{1,0:T(8,128)(2,1)S(1)} %get-tuple-element.39.refs_2_), channel_id=1, source_target_pairs={{0,8},{4,12},{8,0},{12,4},{16,24},{20,28},{24,16},{28,20},{1,9},{5... | collective-permute-start | bytes 393224 | tf_op jit(solution)/shard_map/ppermute | solution.py:42
  47.8 6.1 %collective-permute-start.19 = (bf16[256,256]{1,0:T(8,128)(2,1)S(1)}, bf16[256,256]{1,0:T(8,128)(2,1)S(1)}, u32[]{:S(2)}, u32[]{:S(2)}) collective-permute-start(bf16[256,256]{1,0:T(8,128)(2,1)S(1)} %get-tuple-element.40.refs_3_), channel_id=1, source_target_pairs={{0,4},{4,0},{8,12},{12,8},{16,20},{20,16},{24,28},{28,24},{1,5},{5... | collective-permute-start | bytes 393224 | tf_op jit(solution)/shard_map/ppermute | solution.py:42
  49.3 6.3 %collective-permute-start.17 = (bf16[256,256]{1,0:T(8,128)(2,1)S(1)}, bf16[256,256]{1,0:T(8,128)(2,1)S(1)}, u32[]{:S(2)}, u32[]{:S(2)}) collective-permute-start(bf16[256,256]{1,0:T(8,128)(2,1)S(1)} %get-tuple-element.39.refs_2_), channel_id=1, source_target_pairs={{0,4},{4,0},{8,12},{12,8},{16,20},{20,16},{24,28},{28,24},{1,5},{5... | collective-permute-start | bytes 393224 | tf_op jit(solution)/shard_map/ppermute | solution.py:42
  49.8 5.8 %collective-permute-start.20 = (bf16[256,256]{1,0:T(8,128)(2,1)S(1)}, bf16[256,256]{1,0:T(8,128)(2,1)S(1)}, u32[]{:S(2)}, u32[]{:S(2)}) collective-permute-start(bf16[256,256]{1,0:T(8,128)(2,1)S(1)} %get-tuple-element.40.refs_3_), channel_id=1, source_target_pairs={{0,8},{4,12},{8,0},{12,4},{16,24},{20,28},{24,16},{28,20},{1,9},{5... | collective-permute-start | bytes 393224 | tf_op jit(solution)/shard_map/ppermute | solution.py:42
  53.6 5.0 %collective-permute-start.21 = (bf16[256,256]{1,0:T(8,128)(2,1)S(1)}, bf16[256,256]{1,0:T(8,128)(2,1)S(1)}, u32[]{:S(2)}, u32[]{:S(2)}) collective-permute-start(bf16[256,256]{1,0:T(8,128)(2,1)S(1)} %collective-permute-done.18.refs_2_), channel_id=1, source_target_pairs={{0,4},{4,0},{8,12},{12,8},{16,20},{20,16},{24,28},{28,24},{1,5},{5... | collective-permute-start | bytes 393224 | tf_op jit(solution)/shard_map/ppermute | solution.py:42
  53.9 5.2 %collective-permute-start.22 = (bf16[256,256]{1,0:T(8,128)(2,1)S(1)}, bf16[256,256]{1,0:T(8,128)(2,1)S(1)}, u32[]{:S(2)}, u32[]{:S(2)}) collective-permute-start(bf16[256,256]{1,0:T(8,128)(2,1)S(1)} %collective-permute-done.19.refs_3_), channel_id=1, source_target_pairs={{0,8},{4,12},{8,0},{12,4},{16,24},{20,28},{24,16},{28,20},{1,9},{5... | collective-permute-start | bytes 393224 | tf_op jit(solution)/shard_map/ppermute | solution.py:42

commit v7 on v5

--- a/solution.py
+++ b/solution.py
@@ -337,8 +337,8 @@
     known = {0: own[0], top: own[1]}
     total = near
     high = mid
-    from_low = {j ^ low: swapped(v, "leaf", low) for j, v in known.items()}
     from_high = {j ^ high: swapped(v, "leaf", high) for j, v in known.items()}
+    from_low = {j ^ low: swapped(v, "leaf", low) for j, v in reversed(known.items())}
     total = [add_far(total, known)]
     rest = {
         low ^ high: swapped(from_high[high], "leaf", low),

time: 60.7 us -> 60.7 us (level)
  no operation moved by 1% of the time
where the time goes in v7:
time: 60.7 us; the launch traced here: 60.6 us
  starting transfers between devices  27.7 us (46%)
  Pallas kernels  17.9 us (29%)
  waiting for transfers between devices  14.5 us (24%)
    ppermute x23, starting transfers between devices, swapped(): lax.ppermute(value, axis, [(i, i ^ mask) for i in range(lax.axis_size(axi...  27.7 us
    pallas_call x10, Pallas kernels, call(): pl.pallas_call(kernel, out_shape=[space(s.shape, s.dtype) for s, space in...  17.9 us
    ppermute x23, waiting for transfers between devices, swapped(): lax.ppermute(value, axis, [(i, i ^ mask) for i in range(lax.axis_size(axi...  14.5 us
  transfers between devices with their start and end apart: 23, of which 10 were waited for; matrix products, arithmetic and copies ran while one was open for 0% of the time, Pallas kernels for 21%

profile of v7, /device:TPU:0, one launch (start us, length us, event | category | flops | bytes accessed | tf_op | source)
XLA Modules:
  0.0 60.6 jit_solution(13375826448709201)
XLA Ops:
  0.0 2.4 %shard_map.82 = bf16[2,256,256]{2,1,0:T(8,128)(2,1)S(1)} custom-call(s32[1]{0:T(128)} %bitcast.me_ref, s32[1,2048]{1,0:T(1,128)} %bitcast.22, bf16[2048,256]{1,0:T(8,128)(2,1)} %basis_ref.6, bf16[2048,256]{1,0:T(8,128)(2,1)} %fields_ref.3, s32[1]{0:T(128)} %bitcast.2.rest_0_.me_ref), custom_call_target="tpu_custom_call" | custom-call | flops 1024 | bytes 1024 | tf_op jit(solution)/shard_map/pallas_call | solution.py:26
  2.5 3.0 %collective-permute-start = (bf16[2,256,256]{2,1,0:T(8,128)(2,1)S(1)}, bf16[2,256,256]{2,1,0:T(8,128)(2,1)S(1)}, u32[]{:S(2)}, u32[]{:S(2)}) collective-permute-start(bf16[2,256,256]{2,1,0:T(8,128)(2,1)S(1)} %shard_map.82), channel_id=1, source_target_pairs={{0,4},{4,0},{8,12},{12,8},{16,20},{20,16},{24,28},{28,24},{1,5},{5... | collective-permute-start | bytes 786440 | tf_op jit(solution)/shard_map/ppermute | solution.py:42
  5.5 1.3 %shard_map.83 = (f32[2,256,256]{2,1,0:T(8,128)S(1)}, bf16[2,256,256]{2,1,0:T(8,128)(2,1)S(1)}) custom-call(s32[1]{0:T(128)} %bitcast.me_ref, s32[1,2048]{1,0:T(1,128)S(1)} %bitcast.23, bf16[2048,256]{1,0:T(8,128)(2,1)S(1)} %copy-done.1, bf16[2048,256]{1,0:T(8,128)(2,1)S(1)} %copy-done), custom_call_target="tpu_custom_call" | custom-call | flops 1024 | bytes 1024 | tf_op jit(solution)/shard_map/pallas_call | solution.py:26
  6.8 1.6 %collective-permute-start.3 = (bf16[64,512]{1,0:T(8,128)(2,1)S(1)}, bf16[64,512]{1,0:T(8,128)(2,1)S(1)}, u32[]{:S(2)}, u32[]{:S(2)}) collective-permute-start(bf16[64,512]{1,0:T(8,128)(2,1)S(1)} %get-tuple-element.44), channel_id=1, source_target_pairs={{0,8},{4,12},{8,0},{12,4},{16,24},{20,28},{24,16},{28,20},{1,9},{5... | collective-permute-start | bytes 196616 | tf_op jit(solution)/shard_map/ppermute | solution.py:42
  8.4 2.6 %collective-permute-start.4 = (bf16[64,512]{1,0:T(8,128)(2,1)S(1)}, bf16[64,512]{1,0:T(8,128)(2,1)S(1)}, u32[]{:S(2)}, u32[]{:S(2)}) collective-permute-start(bf16[64,512]{1,0:T(8,128)(2,1)S(1)} %get-tuple-element.43), channel_id=1, source_target_pairs={{0,16},{4,20},{8,24},{12,28},{16,0},{20,4},{24,8},{28,12},{1,17},{... | collective-permute-start | bytes 196616 | tf_op jit(solution)/shard_map/ppermute | solution.py:42
  11.0 1.5 %collective-permute-start.2 = (bf16[3,64,512]{2,1,0:T(8,128)(2,1)S(1)}, bf16[3,64,512]{2,1,0:T(8,128)(2,1)S(1)}, u32[]{:S(2)}, u32[]{:S(2)}) collective-permute-start(bf16[3,64,512]{2,1,0:T(8,128)(2,1)S(1)} %bitcast.18), channel_id=1, source_target_pairs={{0,2},{1,3},{2,0},{3,1},{4,6},{5,7},{6,4},{7,5},{8,10},{9,11},{10,... | collective-permute-start | bytes 589832 | tf_op jit(solution)/shard_map/ppermute | solution.py:42
  13.2 0.7 %shard_map.84 = (f32[2,256,256]{2,1,0:T(8,128)S(1)}, bf16[2048,128]{1,0:T(8,128)(2,1)S(1)}) custom-call(s32[1]{0:T(128)} %bitcast.me_ref, s32[1,2048]{1,0:T(1,128)S(1)} %bitcast.24, bf16[2048,256]{1,0:T(8,128)(2,1)S(1)} %copy-done.1, bf16[2048,256]{1,0:T(8,128)(2,1)S(1)} %copy-done, bf16[256,256]{1,0:T(8,128)(2,1)S(1)} %get-tuple-element.42.rest_0_), custom_call_target="tpu_custom_call" | custom-call | flops 1024 | bytes 1024 | tf_op jit(solution)/shard_map/pallas_call | solution.py:26
  14.0 3.8 %collective-permute-start.11 = (bf16[256,256]{1,0:T(8,128)(2,1)S(1)}, bf16[256,256]{1,0:T(8,128)(2,1)S(1)}, u32[]{:S(2)}, u32[]{:S(2)}) collective-permute-start(bf16[256,256]{1,0:T(8,128)(2,1)S(1)} %get-tuple-element.42.rest_0_), channel_id=1, source_target_pairs={{0,24},{4,28},{8,16},{12,20},{16,8},{20,12},{24,0},{28,4},{1,25},{... | collective-permute-start | bytes 393224 | tf_op jit(solution)/shard_map/ppermute | solution.py:42
  17.7 1.7 %collective-permute-done.1 = bf16[2,256,256]{2,1,0:T(8,128)(2,1)S(1)} collective-permute-done((bf16[2,256,256]{2,1,0:T(8,128)(2,1)S(1)}, bf16[2,256,256]{2,1,0:T(8,128)(2,1)S(1)}, u32[]{:S(2)}, u32[]{:S(2)}) %collective-permute-start.1) | collective-permute-done | bytes 262176 | tf_op jit(solution)/shard_map/ppermute | solution.py:42
  19.5 0.6 collective-permute-start.5
  20.2 0.8 %collective-permute-start.10 = (bf16[256,256]{1,0:T(8,128)(2,1)S(1)}, bf16[256,256]{1,0:T(8,128)(2,1)S(1)}, u32[]{:S(2)}, u32[]{:S(2)}) collective-permute-start(bf16[256,256]{1,0:T(8,128)(2,1)S(1)} %fusion), channel_id=1, source_target_pairs={{0,8},{4,12},{8,0},{12,4},{16,24},{20,28},{24,16},{28,20},{1,9},{5... | collective-permute-start | bytes 393224 | tf_op jit(solution)/shard_map/ppermute | solution.py:42
  21.0 2.6 %collective-permute-start.12 = (bf16[256,256]{1,0:T(8,128)(2,1)S(1)}, bf16[256,256]{1,0:T(8,128)(2,1)S(1)}, u32[]{:S(2)}, u32[]{:S(2)}) collective-permute-start(bf16[256,256]{1,0:T(8,128)(2,1)S(1)} %get-tuple-element.41), channel_id=1, source_target_pairs={{0,16},{4,20},{8,24},{12,28},{16,0},{20,4},{24,8},{28,12},{1,17},{... | collective-permute-start | bytes 393224 | tf_op jit(solution)/shard_map/ppermute | solution.py:42
  23.6 4.3 %shard_map.85.refs_0_ = f32[1024,256]{1,0:T(8,128)S(1)} custom-call(s32[8,7]{1,0:T(8,128)S(1)} %copy-done.5, s32[8]{0:T(128)S(1)} %copy-done.6, bf16[8,7,256,256]{3,2,1,0:T(8,128)(2,1)} %blocks_hbm.3, bf16[2048,256]{1,0:T(8,128)(2,1)S(1)} %copy-done, bf16[256,256]{1,0:T(8,128)(2,1)S(1)} %get-tuple-element.42.rest_0_), custom_call_target="tpu_custom_call" | custom-call | flops 1024 | bytes 1024 | tf_op jit(solution)/shard_map/pallas_call | solution.py:26
  28.0 0.8 %collective-permute-done.10 = bf16[256,256]{1,0:T(8,128)(2,1)S(1)} collective-permute-done((bf16[256,256]{1,0:T(8,128)(2,1)S(1)}, bf16[256,256]{1,0:T(8,128)(2,1)S(1)}, u32[]{:S(2)}, u32[]{:S(2)}) %collective-permute-start.10) | collective-permute-done | bytes 131104 | tf_op jit(solution)/shard_map/ppermute | solution.py:42
  28.8 1.5 %collective-permute-done.12 = bf16[256,256]{1,0:T(8,128)(2,1)S(1)} collective-permute-done((bf16[256,256]{1,0:T(8,128)(2,1)S(1)}, bf16[256,256]{1,0:T(8,128)(2,1)S(1)}, u32[]{:S(2)}, u32[]{:S(2)}) %collective-permute-start.12) | collective-permute-done | bytes 131104 | tf_op jit(solution)/shard_map/ppermute | solution.py:42
  30.4 1.6 %collective-permute-start.13 = (bf16[256,256]{1,0:T(8,128)(2,1)S(1)}, bf16[256,256]{1,0:T(8,128)(2,1)S(1)}, u32[]{:S(2)}, u32[]{:S(2)}) collective-permute-start(bf16[256,256]{1,0:T(8,128)(2,1)S(1)} %add_convert_fusion.1.refs_8_), channel_id=1, source_target_pairs={{0,4},{4,0},{8,12},{12,8},{16,20},{20,16},{24,28},{28,24},{1,5},{5... | collective-permute-start | bytes 393224 | tf_op jit(solution)/shard_map/ppermute | solution.py:42
  32.4 1.5 %collective-permute-start.15 = (bf16[256,256]{1,0:T(8,128)(2,1)S(1)}, bf16[256,256]{1,0:T(8,128)(2,1)S(1)}, u32[]{:S(2)}, u32[]{:S(2)}) collective-permute-start(bf16[256,256]{1,0:T(8,128)(2,1)S(1)} %add_convert_fusion.1.refs_8_), channel_id=1, source_target_pairs={{0,12},{4,8},{8,4},{12,0},{16,28},{20,24},{24,20},{28,16},{1,13},{... | collective-permute-start | bytes 393224 | tf_op jit(solution)/shard_map/ppermute | solution.py:42
  34.0 2.3 %collective-permute-done.13.refs_9_ = bf16[256,256]{1,0:T(8,128)(2,1)S(1)} collective-permute-done((bf16[256,256]{1,0:T(8,128)(2,1)S(1)}, bf16[256,256]{1,0:T(8,128)(2,1)S(1)}, u32[]{:S(2)}, u32[]{:S(2)}) %collective-permute-start.13) | collective-permute-done | bytes 131104 | tf_op jit(solution)/shard_map/ppermute | solution.py:42
  36.3 0.7 %collective-permute-done.14.refs_10_ = bf16[256,256]{1,0:T(8,128)(2,1)S(1)} collective-permute-done((bf16[256,256]{1,0:T(8,128)(2,1)S(1)}, bf16[256,256]{1,0:T(8,128)(2,1)S(1)}, u32[]{:S(2)}, u32[]{:S(2)}) %collective-permute-start.14) | collective-permute-done | bytes 131104 | tf_op jit(solution)/shard_map/ppermute | solution.py:42
  37.0 2.3 %collective-permute-done.15.refs_11_ = bf16[256,256]{1,0:T(8,128)(2,1)S(1)} collective-permute-done((bf16[256,256]{1,0:T(8,128)(2,1)S(1)}, bf16[256,256]{1,0:T(8,128)(2,1)S(1)}, u32[]{:S(2)}, u32[]{:S(2)}) %collective-permute-start.15) | collective-permute-done | bytes 131104 | tf_op jit(solution)/shard_map/ppermute | solution.py:42
  39.3 0.7 %shard_map.86.rest_0_.refs_8_ = bf16[256,256]{1,0:T(8,128)(2,1)S(1)} custom-call(s32[1]{0:T(128)} %bitcast.2.rest_0_.me_ref, bf16[3,64,512]{2,1,0:T(8,128)(2,1)S(1)} %bitcast.20, bf16[3,64,512]{2,1,0:T(8,128)(2,1)S(1)} %collective-permute-done.6.refs_1_, bf16[3,64,512]{2,1,0:T(8,128)(2,1)S(1)} %collective-permute-done.2.refs_2_, ...), custom_call_target="tpu_custom_call" | custom-call | flops 1024 | bytes 1024 | tf_op jit(solution)/shard_map/pallas_call | solution.py:26
  39.9 1.7 %collective-permute-start.16 = (bf16[256,256]{1,0:T(8,128)(2,1)S(1)}, bf16[256,256]{1,0:T(8,128)(2,1)S(1)}, u32[]{:S(2)}, u32[]{:S(2)}) collective-permute-start(bf16[256,256]{1,0:T(8,128)(2,1)S(1)} %shard_map.86.rest_0_.refs_8_), channel_id=1, source_target_pairs={{0,16},{4,20},{8,24},{12,28},{16,0},{20,4},{24,8},{28,12},{1,17},{... | collective-permute-start | bytes 393224 | tf_op jit(solution)/shard_map/ppermute | solution.py:42
  41.6 4.3 %shard_map.87.refs_10_.refs_1_ = f32[1024,256]{1,0:T(8,128)S(1)} custom-call(s32[8,7]{1,0:T(8,128)S(1)} %copy-done.5, s32[8]{0:T(128)S(1)} %copy-done.6, bf16[8,7,256,256]{3,2,1,0:T(8,128)(2,1)} %blocks_hbm.3, bf16[2048,256]{1,0:T(8,128)(2,1)S(1)} %copy-done, bf16[256,256]{1,0:T(8,128)(2,1)S(1)} %shard_map.86.rest_0_.refs_8_), custom_call_target="tpu_custom_call" | custom-call | flops 1024 | bytes 1024 | tf_op jit(solution)/shard_map/pallas_call | solution.py:26
  45.9 1.3 %collective-permute-done.16.refs_9_ = bf16[256,256]{1,0:T(8,128)(2,1)S(1)} collective-permute-done((bf16[256,256]{1,0:T(8,128)(2,1)S(1)}, bf16[256,256]{1,0:T(8,128)(2,1)S(1)}, u32[]{:S(2)}, u32[]{:S(2)}) %collective-permute-start.16) | collective-permute-done | bytes 131104 | tf_op jit(solution)/shard_map/ppermute | solution.py:42
  47.8 1.5 %collective-permute-start.19 = (bf16[256,256]{1,0:T(8,128)(2,1)S(1)}, bf16[256,256]{1,0:T(8,128)(2,1)S(1)}, u32[]{:S(2)}, u32[]{:S(2)}) collective-permute-start(bf16[256,256]{1,0:T(8,128)(2,1)S(1)} %get-tuple-element.40.refs_3_), channel_id=1, source_target_pairs={{0,4},{4,0},{8,12},{12,8},{16,20},{20,16},{24,28},{28,24},{1,5},{5... | collective-permute-start | bytes 393224 | tf_op jit(solution)/shard_map/ppermute | solution.py:42
  49.8 1.9 %collective-permute-start.20 = (bf16[256,256]{1,0:T(8,128)(2,1)S(1)}, bf16[256,256]{1,0:T(8,128)(2,1)S(1)}, u32[]{:S(2)}, u32[]{:S(2)}) collective-permute-start(bf16[256,256]{1,0:T(8,128)(2,1)S(1)} %get-tuple-element.40.refs_3_), channel_id=1, source_target_pairs={{0,8},{4,12},{8,0},{12,4},{16,24},{20,28},{24,16},{28,20},{1,9},{5... | collective-permute-start | bytes 393224 | tf_op jit(solution)/shard_map/ppermute | solution.py:42
  51.7 1.9 %collective-permute-done.18.refs_2_ = bf16[256,256]{1,0:T(8,128)(2,1)S(1)} collective-permute-done((bf16[256,256]{1,0:T(8,128)(2,1)S(1)}, bf16[256,256]{1,0:T(8,128)(2,1)S(1)}, u32[]{:S(2)}, u32[]{:S(2)}) %collective-permute-start.18) | collective-permute-done | bytes 131104 | tf_op jit(solution)/shard_map/ppermute | solution.py:42
  53.9 0.8 %collective-permute-start.22 = (bf16[256,256]{1,0:T(8,128)(2,1)S(1)}, bf16[256,256]{1,0:T(8,128)(2,1)S(1)}, u32[]{:S(2)}, u32[]{:S(2)}) collective-permute-start(bf16[256,256]{1,0:T(8,128)(2,1)S(1)} %collective-permute-done.19.refs_3_), channel_id=1, source_target_pairs={{0,8},{4,12},{8,0},{12,4},{16,24},{20,28},{24,16},{28,20},{1,9},{5... | collective-permute-start | bytes 393224 | tf_op jit(solution)/shard_map/ppermute | solution.py:42
  54.8 0.8 %shard_map.89.refs_0_ = f32[2048,256]{1,0:T(8,128)S(1)} custom-call(bf16[2048,128]{1,0:T(8,128)(2,1)S(1)} %get-tuple-element.27.tag_ref, bf16[2048,256]{1,0:T(8,128)(2,1)S(1)} %copy-done.2, f32[1024,256]{1,0:T(8,128)S(1)} %shard_map.85.refs_0_, f32[1024,256]{1,0:T(8,128)S(1)} %shard_map.87.refs_10_.refs_1_, bf16[256,256]{1,0:T(8,128)(2,1)S(1)} %get-tuple-element.39.refs_2_, ...), custom_call_target="tpu_custom_call" | custom-call | flops 1024 | bytes 1024 | tf_op jit(solution)/shard_map/pallas_call | solution.py:26
  55.6 1.4 %shard_map.90.refs_0_ = f32[2048,256]{1,0:T(8,128)S(1)} custom-call(bf16[2048,128]{1,0:T(8,128)(2,1)S(1)} %get-tuple-element.27.tag_ref, bf16[2048,256]{1,0:T(8,128)(2,1)S(1)} %copy-done.2, f32[2048,256]{1,0:T(8,128)S(1)} %shard_map.89.refs_0_, bf16[256,256]{1,0:T(8,128)(2,1)S(1)} %collective-permute-done.17.refs_1_, ...), custom_call_target="tpu_custom_call" | custom-call | flops 1024 | bytes 1024 | tf_op jit(solution)/shard_map/pallas_call | solution.py:26
  57.1 1.5 %collective-permute-done.21.refs_1_ = bf16[256,256]{1,0:T(8,128)(2,1)S(1)} collective-permute-done((bf16[256,256]{1,0:T(8,128)(2,1)S(1)}, bf16[256,256]{1,0:T(8,128)(2,1)S(1)}, u32[]{:S(2)}, u32[]{:S(2)}) %collective-permute-start.21) | collective-permute-done | bytes 131104 | tf_op jit(solution)/shard_map/ppermute | solution.py:42
  58.9 1.7 %shard_map.91 = bf16[2048,256]{1,0:T(8,128)(2,1)} custom-call(bf16[2048,128]{1,0:T(8,128)(2,1)S(1)} %get-tuple-element.27.tag_ref, bf16[2048,256]{1,0:T(8,128)(2,1)S(1)} %copy-done.2, f32[2048,256]{1,0:T(8,128)S(1)} %shard_map.90.refs_0_, bf16[256,256]{1,0:T(8,128)(2,1)S(1)} %collective-permute-done.21.refs_1_, ...), custom_call_target="tpu_custom_call" | custom-call | flops 1024 | bytes 1024 | tf_op jit(solution)/shard_map/pallas_call | solution.py:26
  (46 shorter events, 3.0 us)
Async XLA Ops:
  0.0 5.5 %copy-start.4 = (s32[2048,1]{0,1:T(1,128)S(1)}, s32[2048,1]{0,1:T(1,128)}, u32[]{:S(2)}) copy-start(s32[2048,1]{0,1:T(1,128)} %param.9) | copy-start | bytes 24580
  0.0 5.5 %copy-start.1 = (bf16[2048,256]{1,0:T(8,128)(2,1)S(1)}, bf16[2048,256]{1,0:T(8,128)(2,1)}, u32[]{:S(2)}) copy-start(bf16[2048,256]{1,0:T(8,128)(2,1)} %basis_ref.6) | copy-start | bytes 3145732
  0.0 5.5 %copy-start = (bf16[2048,256]{1,0:T(8,128)(2,1)S(1)}, bf16[2048,256]{1,0:T(8,128)(2,1)}, u32[]{:S(2)}) copy-start(bf16[2048,256]{1,0:T(8,128)(2,1)} %fields_ref.3) | copy-start | bytes 3145732
  0.0 6.8 %copy-start.3 = (bf16[1,3,64,512]{3,2,1,0:T(8,128)(2,1)S(1)}, bf16[1,3,64,512]{3,2,1,0:T(8,128)(2,1)}, u32[]{:S(2)}) copy-start(bf16[1,3,64,512]{3,2,1,0:T(8,128)(2,1)} %param.12) | copy-start | bytes 589828
  2.5 10.6 %collective-permute-start = (bf16[2,256,256]{2,1,0:T(8,128)(2,1)S(1)}, bf16[2,256,256]{2,1,0:T(8,128)(2,1)S(1)}, u32[]{:S(2)}, u32[]{:S(2)}) collective-permute-start(bf16[2,256,256]{2,1,0:T(8,128)(2,1)S(1)} %shard_map.82), channel_id=1, source_target_pairs={{0,4},{4,0},{8,12},{12,8},{16,20},{20,16},{24,28},{28,24},{1,5},{5... | collective-permute-start | bytes 786440 | tf_op jit(solution)/shard_map/ppermute | solution.py:42
  6.8 10.9 %collective-permute-start.3 = (bf16[64,512]{1,0:T(8,128)(2,1)S(1)}, bf16[64,512]{1,0:T(8,128)(2,1)S(1)}, u32[]{:S(2)}, u32[]{:S(2)}) collective-permute-start(bf16[64,512]{1,0:T(8,128)(2,1)S(1)} %get-tuple-element.44), channel_id=1, source_target_pairs={{0,8},{4,12},{8,0},{12,4},{16,24},{20,28},{24,16},{28,20},{1,9},{5... | collective-permute-start | bytes 196616 | tf_op jit(solution)/shard_map/ppermute | solution.py:42
  8.4 9.3 %collective-permute-start.4 = (bf16[64,512]{1,0:T(8,128)(2,1)S(1)}, bf16[64,512]{1,0:T(8,128)(2,1)S(1)}, u32[]{:S(2)}, u32[]{:S(2)}) collective-permute-start(bf16[64,512]{1,0:T(8,128)(2,1)S(1)} %get-tuple-element.43), channel_id=1, source_target_pairs={{0,16},{4,20},{8,24},{12,28},{16,0},{20,4},{24,8},{28,12},{1,17},{... | collective-permute-start | bytes 196616 | tf_op jit(solution)/shard_map/ppermute | solution.py:42
  11.0 6.7 %collective-permute-start.2 = (bf16[3,64,512]{2,1,0:T(8,128)(2,1)S(1)}, bf16[3,64,512]{2,1,0:T(8,128)(2,1)S(1)}, u32[]{:S(2)}, u32[]{:S(2)}) collective-permute-start(bf16[3,64,512]{2,1,0:T(8,128)(2,1)S(1)} %bitcast.18), channel_id=1, source_target_pairs={{0,2},{1,3},{2,0},{3,1},{4,6},{5,7},{6,4},{7,5},{8,10},{9,11},{10,... | collective-permute-start | bytes 589832 | tf_op jit(solution)/shard_map/ppermute | solution.py:42
  12.6 6.9 %collective-permute-start.1 = (bf16[2,256,256]{2,1,0:T(8,128)(2,1)S(1)}, bf16[2,256,256]{2,1,0:T(8,128)(2,1)S(1)}, u32[]{:S(2)}, u32[]{:S(2)}) collective-permute-start(bf16[2,256,256]{2,1,0:T(8,128)(2,1)S(1)} %get-tuple-element.29), channel_id=1, source_target_pairs={{0,4},{4,0},{8,12},{12,8},{16,20},{20,16},{24,28},{28,24},{1,5},{5... | collective-permute-start | bytes 786440 | tf_op jit(solution)/shard_map/ppermute | solution.py:42
  13.2 10.4 %copy-start.5 = (s32[8,7]{1,0:T(8,128)S(1)}, s32[8,7]{1,0:T(8,128)}, u32[]{:S(2)}) copy-start(s32[8,7]{1,0:T(8,128)} %index_ref.3) | copy-start | bytes 676
  13.2 10.4 %copy-start.6 = (s32[8]{0:T(128)S(1)}, s32[8]{0:T(128)}, u32[]{:S(2)}) copy-start(s32[8]{0:T(128)} %count_ref.3) | copy-start | bytes 100
  14.0 14.9 %collective-permute-start.11 = (bf16[256,256]{1,0:T(8,128)(2,1)S(1)}, bf16[256,256]{1,0:T(8,128)(2,1)S(1)}, u32[]{:S(2)}, u32[]{:S(2)}) collective-permute-start(bf16[256,256]{1,0:T(8,128)(2,1)S(1)} %get-tuple-element.42.rest_0_), channel_id=1, source_target_pairs={{0,24},{4,28},{8,16},{12,20},{16,8},{20,12},{24,0},{28,4},{1,25},{... | collective-permute-start | bytes 393224 | tf_op jit(solution)/shard_map/ppermute | solution.py:42
  19.5 8.4 %collective-permute-start.5 = (bf16[2,64,512]{2,1,0:T(8,128)(2,1)S(1)}, bf16[2,64,512]{2,1,0:T(8,128)(2,1)S(1)}, u32[]{:S(2)}, u32[]{:S(2)}) collective-permute-start(bf16[2,64,512]{2,1,0:T(8,128)(2,1)S(1)} %pad_maximum_fusion.refs_4_), channel_id=1, source_target_pairs={{0,2},{1,3},{2,0},{3,1},{4,6},{5,7},{6,4},{7,5},{8,10},{9,11},{10,... | collective-permute-start | bytes 393224 | tf_op jit(solution)/shard_map/ppermute | solution.py:42
  20.1 12.4 %collective-permute-start.8 = (bf16[2,64,512]{2,1,0:T(8,128)(2,1)S(1)}, bf16[2,64,512]{2,1,0:T(8,128)(2,1)S(1)}, u32[]{:S(2)}, u32[]{:S(2)}) collective-permute-start(bf16[2,64,512]{2,1,0:T(8,128)(2,1)S(1)} %pad_maximum_fusion.refs_4_), channel_id=1, source_target_pairs={{0,1},{1,0},{2,3},{3,2},{4,5},{5,4},{6,7},{7,6},{8,9},{9,8},{10,11... | collective-permute-start | bytes 393224 | tf_op jit(solution)/shard_map/ppermute | solution.py:42
  20.2 8.7 %collective-permute-start.10 = (bf16[256,256]{1,0:T(8,128)(2,1)S(1)}, bf16[256,256]{1,0:T(8,128)(2,1)S(1)}, u32[]{:S(2)}, u32[]{:S(2)}) collective-permute-start(bf16[256,256]{1,0:T(8,128)(2,1)S(1)} %fusion), channel_id=1, source_target_pairs={{0,8},{4,12},{8,0},{12,4},{16,24},{20,28},{24,16},{28,20},{1,9},{5... | collective-permute-start | bytes 393224 | tf_op jit(solution)/shard_map/ppermute | solution.py:42
  21.0 9.4 %collective-permute-start.12 = (bf16[256,256]{1,0:T(8,128)(2,1)S(1)}, bf16[256,256]{1,0:T(8,128)(2,1)S(1)}, u32[]{:S(2)}, u32[]{:S(2)}) collective-permute-start(bf16[256,256]{1,0:T(8,128)(2,1)S(1)} %get-tuple-element.41), channel_id=1, source_target_pairs={{0,16},{4,20},{8,24},{12,28},{16,0},{20,4},{24,8},{28,12},{1,17},{... | collective-permute-start | bytes 393224 | tf_op jit(solution)/shard_map/ppermute | solution.py:42
  27.9 6.1 %collective-permute-start.6 = (bf16[3,64,512]{2,1,0:T(8,128)(2,1)S(1)}, bf16[3,64,512]{2,1,0:T(8,128)(2,1)S(1)}, u32[]{:S(2)}, u32[]{:S(2)}) collective-permute-start(bf16[3,64,512]{2,1,0:T(8,128)(2,1)S(1)} %bitcast.19), channel_id=1, source_target_pairs={{0,1},{1,0},{2,3},{3,2},{4,5},{5,4},{6,7},{7,6},{8,9},{9,8},{10,11... | collective-permute-start | bytes 589832 | tf_op jit(solution)/shard_map/ppermute | solution.py:42
  28.8 5.2 %collective-permute-start.7 = (bf16[3,64,512]{2,1,0:T(8,128)(2,1)S(1)}, bf16[3,64,512]{2,1,0:T(8,128)(2,1)S(1)}, u32[]{:S(2)}, u32[]{:S(2)}) collective-permute-start(bf16[3,64,512]{2,1,0:T(8,128)(2,1)S(1)} %collective-permute-done.2.refs_2_), channel_id=1, source_target_pairs={{0,1},{1,0},{2,3},{3,2},{4,5},{5,4},{6,7},{7,6},{8,9},{9,8},{10,11... | collective-permute-start | bytes 589832 | tf_op jit(solution)/shard_map/ppermute | solution.py:42
  30.4 5.8 %collective-permute-start.13 = (bf16[256,256]{1,0:T(8,128)(2,1)S(1)}, bf16[256,256]{1,0:T(8,128)(2,1)S(1)}, u32[]{:S(2)}, u32[]{:S(2)}) collective-permute-start(bf16[256,256]{1,0:T(8,128)(2,1)S(1)} %add_convert_fusion.1.refs_8_), channel_id=1, source_target_pairs={{0,4},{4,0},{8,12},{12,8},{16,20},{20,16},{24,28},{28,24},{1,5},{5... | collective-permute-start | bytes 393224 | tf_op jit(solution)/shard_map/ppermute | solution.py:42
  32.0 5.0 %collective-permute-start.14 = (bf16[256,256]{1,0:T(8,128)(2,1)S(1)}, bf16[256,256]{1,0:T(8,128)(2,1)S(1)}, u32[]{:S(2)}, u32[]{:S(2)}) collective-permute-start(bf16[256,256]{1,0:T(8,128)(2,1)S(1)} %add_convert_fusion.1.refs_8_), channel_id=1, source_target_pairs={{0,8},{4,12},{8,0},{12,4},{16,24},{20,28},{24,16},{28,20},{1,9},{5... | collective-permute-start | bytes 393224 | tf_op jit(solution)/shard_map/ppermute | solution.py:42
  32.4 6.8 %collective-permute-start.15 = (bf16[256,256]{1,0:T(8,128)(2,1)S(1)}, bf16[256,256]{1,0:T(8,128)(2,1)S(1)}, u32[]{:S(2)}, u32[]{:S(2)}) collective-permute-start(bf16[256,256]{1,0:T(8,128)(2,1)S(1)} %add_convert_fusion.1.refs_8_), channel_id=1, source_target_pairs={{0,12},{4,8},{8,4},{12,0},{16,28},{20,24},{24,20},{28,16},{1,13},{... | collective-permute-start | bytes 393224 | tf_op jit(solution)/shard_map/ppermute | solution.py:42
  34.0 5.3 %collective-permute-start.9 = (bf16[2,64,512]{2,1,0:T(8,128)(2,1)S(1)}, bf16[2,64,512]{2,1,0:T(8,128)(2,1)S(1)}, u32[]{:S(2)}, u32[]{:S(2)}) collective-permute-start(bf16[2,64,512]{2,1,0:T(8,128)(2,1)S(1)} %collective-permute-done.5.refs_6_), channel_id=1, source_target_pairs={{0,1},{1,0},{2,3},{3,2},{4,5},{5,4},{6,7},{7,6},{8,9},{9,8},{10,11... | collective-permute-start | bytes 393224 | tf_op jit(solution)/shard_map/ppermute | solution.py:42
  39.9 7.4 %collective-permute-start.16 = (bf16[256,256]{1,0:T(8,128)(2,1)S(1)}, bf16[256,256]{1,0:T(8,128)(2,1)S(1)}, u32[]{:S(2)}, u32[]{:S(2)}) collective-permute-start(bf16[256,256]{1,0:T(8,128)(2,1)S(1)} %shard_map.86.rest_0_.refs_8_), channel_id=1, source_target_pairs={{0,16},{4,20},{8,24},{12,28},{16,0},{20,4},{24,8},{28,12},{1,17},{... | collective-permute-start | bytes 393224 | tf_op jit(solution)/shard_map/ppermute | solution.py:42
  45.9 8.8 %copy-start.2 = (bf16[2048,256]{1,0:T(8,128)(2,1)S(1)}, bf16[2048,256]{1,0:T(8,128)(2,1)}, u32[]{:S(2)}) copy-start(bf16[2048,256]{1,0:T(8,128)(2,1)} %basis_ref.9) | copy-start | bytes 3145732
  47.6 6.0 %collective-permute-start.18 = (bf16[256,256]{1,0:T(8,128)(2,1)S(1)}, bf16[256,256]{1,0:T(8,128)(2,1)S(1)}, u32[]{:S(2)}, u32[]{:S(2)}) collective-permute-start(bf16[256,256]{1,0:T(8,128)(2,1)S(1)} %get-tuple-element.39.refs_2_), channel_id=1, source_target_pairs={{0,8},{4,12},{8,0},{12,4},{16,24},{20,28},{24,16},{28,20},{1,9},{5... | collective-permute-start | bytes 393224 | tf_op jit(solution)/shard_map/ppermute | solution.py:42
  47.8 6.1 %collective-permute-start.19 = (bf16[256,256]{1,0:T(8,128)(2,1)S(1)}, bf16[256,256]{1,0:T(8,128)(2,1)S(1)}, u32[]{:S(2)}, u32[]{:S(2)}) collective-permute-start(bf16[256,256]{1,0:T(8,128)(2,1)S(1)} %get-tuple-element.40.refs_3_), channel_id=1, source_target_pairs={{0,4},{4,0},{8,12},{12,8},{16,20},{20,16},{24,28},{28,24},{1,5},{5... | collective-permute-start | bytes 393224 | tf_op jit(solution)/shard_map/ppermute | solution.py:42
  49.3 6.3 %collective-permute-start.17 = (bf16[256,256]{1,0:T(8,128)(2,1)S(1)}, bf16[256,256]{1,0:T(8,128)(2,1)S(1)}, u32[]{:S(2)}, u32[]{:S(2)}) collective-permute-start(bf16[256,256]{1,0:T(8,128)(2,1)S(1)} %get-tuple-element.39.refs_2_), channel_id=1, source_target_pairs={{0,4},{4,0},{8,12},{12,8},{16,20},{20,16},{24,28},{28,24},{1,5},{5... | collective-permute-start | bytes 393224 | tf_op jit(solution)/shard_map/ppermute | solution.py:42
  49.8 5.8 %collective-permute-start.20 = (bf16[256,256]{1,0:T(8,128)(2,1)S(1)}, bf16[256,256]{1,0:T(8,128)(2,1)S(1)}, u32[]{:S(2)}, u32[]{:S(2)}) collective-permute-start(bf16[256,256]{1,0:T(8,128)(2,1)S(1)} %get-tuple-element.40.refs_3_), channel_id=1, source_target_pairs={{0,8},{4,12},{8,0},{12,4},{16,24},{20,28},{24,16},{28,20},{1,9},{5... | collective-permute-start | bytes 393224 | tf_op jit(solution)/shard_map/ppermute | solution.py:42
  53.6 5.0 %collective-permute-start.21 = (bf16[256,256]{1,0:T(8,128)(2,1)S(1)}, bf16[256,256]{1,0:T(8,128)(2,1)S(1)}, u32[]{:S(2)}, u32[]{:S(2)}) collective-permute-start(bf16[256,256]{1,0:T(8,128)(2,1)S(1)} %collective-permute-done.18.refs_2_), channel_id=1, source_target_pairs={{0,4},{4,0},{8,12},{12,8},{16,20},{20,16},{24,28},{28,24},{1,5},{5... | collective-permute-start | bytes 393224 | tf_op jit(solution)/shard_map/ppermute | solution.py:42
  53.9 5.0 %collective-permute-start.22 = (bf16[256,256]{1,0:T(8,128)(2,1)S(1)}, bf16[256,256]{1,0:T(8,128)(2,1)S(1)}, u32[]{:S(2)}, u32[]{:S(2)}) collective-permute-start(bf16[256,256]{1,0:T(8,128)(2,1)S(1)} %collective-permute-done.19.refs_3_), channel_id=1, source_target_pairs={{0,8},{4,12},{8,0},{12,4},{16,24},{20,28},{24,16},{28,20},{1,9},{5... | collective-permute-start | bytes 393224 | tf_op jit(solution)/shard_map/ppermute | solution.py:42
